TPU v7x, 32 devices: a whole 2x2x4 slice. The times are simulated.
32 devices in a mesh: batch: 4 (over y, core), table: 8 (over z, x).
Axes of the slice: x: 2, y: 2, z: 4, core: 2. Of those that a mesh axis runs over, the one named last changes fastest.
Arguments:
- tables: bfloat16 [16, 16384, 128], P('table'), may hold values from -8 to 8
- feature_ids: int32 [16384, 16, 8], P('batch', 'table'), may hold values from 0 to 16383
- bag_lengths: int32 [16384, 16], P('batch', 'table'), may hold values from 1 to 8
- feature_slot: int32 [16], replicated, may hold values from 0 to 15, each once
- w_first: bfloat16 [2048, 1024], P('batch'), may hold values from -0.125 to 0.125
- b_first: float32 [1024], replicated, may hold values from -4 to 4
- w_second: bfloat16 [1024, 256], replicated, may hold values from -0.1875 to 0.1875
- bank: bfloat16 [512, 64, 256], P('table'), may hold values from -6 to 6
- log_q: bfloat16 [512, 64], P('table'), may hold values from -12 to -4
- noise_lists: int32 [4, 32], P('batch'), may hold values from 0 to 511, as said below
- pos_items: int32 [16384], P(('batch', 'table')), may hold values from 0 to 32767
Outputs:
- loss: float32 [16384], P(('batch', 'table'))
- pooled_grad: bfloat16 [16384, 16, 128], P('batch', 'table')
Inputs may be any that keep to these rules, and one draw needn't show every extreme that they name: `noise_lists`: block ids t * 64 to (t + 1) * 64 - 1 belong to owner t. Each row names 32 distinct blocks, at most 8 of one owner, and exactly 8 of some owner.
All inputs are finite; a program needn't handle non-finite values.
Results may differ from a plain program's by a relative error of at most 0.012.
The roundings to bfloat16 on the way count: a program that leaves them out, or rounds other values in their place, can miss the bound.
Values may be sent and summed in bfloat16 or wider, within the bound.
No kernel may reach another device: no remote copies, remote signals or barrier semaphores. Data moves between devices by JAX's collectives and lax.ppermute only.
A program may use at most 192 MiB of HBM per device.

v0:
```python
import jax
import jax.numpy as jnp
from jax import lax
from jax.sharding import PartitionSpec as P

MOST = 8


def on_device(
    tables,
    feature_ids,
    bag_lengths,
    feature_slot,
    w_first,
    b_first,
    w_second,
    bank,
    log_q,
    noise_lists,
    pos_items,
):
    row_users, per_owner, bag_width = feature_ids.shape
    table_rows = tables.shape[1]
    emb = tables.shape[2]
    owners = lax.axis_size("table")
    owner_index = lax.axis_index("table")
    blocks_dev, block_items, out_width = bank.shape
    scale = out_width ** (-0.5)
    contract = (((1,), (1,)), ((), ()))
    flat_tables = tables.reshape(per_owner * table_rows, emb)
    offsets = (jnp.arange(per_owner, dtype=jnp.int32) * table_rows)[None, :, None]
    flat_ids = (feature_ids + offsets).reshape(-1)
    weights = (
        jnp.arange(bag_width, dtype=jnp.int32)[None, None, :] < bag_lengths[:, :, None]
    ).astype(jnp.float32)
    fetched = jnp.take(flat_tables, flat_ids, axis=0).reshape(row_users, per_owner, bag_width, emb)
    pooled = jnp.sum(fetched.astype(jnp.float32) * weights[:, :, :, None], axis=2).astype(
        jnp.bfloat16
    )
    arrived = lax.all_to_all(pooled, "table", split_axis=0, concat_axis=1, tiled=True)
    users = arrived.shape[0]
    tables_all = arrived.shape[1]
    order = jnp.argsort(feature_slot)
    features = arrived[:, order, :].reshape(users, tables_all * emb)
    whole_first = lax.all_gather(w_first, "batch", axis=0, tiled=True)
    pre = jnp.dot(features, whole_first, preferred_element_type=jnp.float32)
    pre = pre + b_first
    hidden = jax.nn.silu(pre).astype(jnp.bfloat16)
    user_vec = jnp.dot(hidden, w_second, preferred_element_type=jnp.float32).astype(jnp.bfloat16)
    item_ids = lax.all_gather(pos_items, "table", axis=0, tiled=True)
    owned_items = blocks_dev * block_items
    local_item = item_ids - owner_index * owned_items
    held = ((local_item >= 0) & (local_item < owned_items)).astype(jnp.float32)
    safe_item = jnp.clip(local_item, 0, owned_items - 1)
    flat_bank = bank.reshape(owned_items, out_width)
    flat_lq = log_q.reshape(owned_items)
    mine_vec = jnp.take(flat_bank, safe_item, axis=0).astype(jnp.float32) * held[:, None]
    mine_lq = jnp.take(flat_lq, safe_item, axis=0).astype(jnp.float32) * held
    pos_sum, pos_lq = (
        lax.psum(mine_vec.astype(jnp.bfloat16), "table").astype(jnp.float32),
        lax.psum(mine_lq.astype(jnp.bfloat16), "table").astype(jnp.float32),
    )
    pos_vecs = pos_sum.astype(jnp.bfloat16)
    sample = noise_lists[0]
    owner_of = sample // blocks_dev
    is_mine = (owner_of == owner_index).astype(jnp.int32)
    rank_mine = jnp.cumsum(is_mine) - 1
    pick = is_mine[None, :] * (rank_mine[None, :] == jnp.arange(MOST)[:, None]).astype(jnp.int32)
    local_block = jnp.sum(pick * (sample - owner_index * blocks_dev)[None, :], axis=1)
    got_blocks, got_lq = (
        lax.all_gather(bank[local_block], "table", axis=0, tiled=True),
        lax.all_gather(log_q[local_block], "table", axis=0, tiled=True),
    )
    owner_grid = jnp.arange(owners)
    counts = jnp.sum((owner_of[None, :] == owner_grid[:, None]).astype(jnp.int32), axis=1)
    usable = (jnp.arange(MOST)[None, :] < counts[:, None]).reshape(owners * MOST)
    noise_vecs = got_blocks.reshape(-1, out_width)
    noise_bias = jnp.where(usable[:, None], -got_lq.astype(jnp.float32), -1e30).reshape(-1)
    score_pos = (
        lax.dot_general(user_vec, pos_vecs, contract, preferred_element_type=jnp.float32) * scale
        - pos_lq
    )
    score_noise = (
        lax.dot_general(user_vec, noise_vecs, contract, preferred_element_type=jnp.float32) * scale
        + noise_bias
    )
    top = jnp.maximum(jnp.max(score_pos, axis=1), jnp.max(score_noise, axis=1))
    exp_pos = jnp.exp(score_pos - top[:, None])
    exp_noise = jnp.exp(score_noise - top[:, None])
    denom = jnp.sum(exp_pos, axis=1) + jnp.sum(exp_noise, axis=1)
    own = owner_index * users + jnp.arange(users)
    own_logit = jnp.take_along_axis(score_pos, own[:, None], axis=1)[:, 0]
    loss = top + jnp.log(denom) - own_logit
    prob_pos = (exp_pos / denom[:, None]).astype(jnp.bfloat16)
    prob_noise = (exp_noise / denom[:, None]).astype(jnp.bfloat16)
    mixed = jnp.dot(prob_pos, pos_vecs, preferred_element_type=jnp.float32)
    mixed = mixed + jnp.dot(prob_noise, noise_vecs, preferred_element_type=jnp.float32)
    own_vec = lax.dynamic_slice_in_dim(pos_vecs, owner_index * users, users, 0)
    user_grad = ((mixed - own_vec.astype(jnp.float32)) * scale).astype(jnp.bfloat16)
    hidden_grad = lax.dot_general(user_grad, w_second, contract, preferred_element_type=jnp.float32)
    sig = jax.nn.sigmoid(pre)
    pre_grad = (hidden_grad * sig * (1.0 + pre * (1.0 - sig))).astype(jnp.bfloat16)
    feature_grad = lax.dot_general(
        pre_grad, whole_first, contract, preferred_element_type=jnp.float32
    ).astype(jnp.bfloat16)
    table_grad = feature_grad.reshape(users, tables_all, emb)[:, feature_slot, :]
    returned = lax.all_to_all(table_grad, "table", split_axis=1, concat_axis=0, tiled=True)
    return (loss, returned)


def solution(mesh):
    return jax.shard_map(
        on_device,
        mesh=mesh,
        in_specs=(
            P("table", None, None),
            P("batch", "table", None),
            P("batch", "table"),
            P(),
            P("batch", None),
            P(),
            P(),
            P("table", None, None),
            P("table", None),
            P("batch", None),
            P(("batch", "table")),
        ),
        out_specs=(P(("batch", "table")), P("batch", "table", None)),
        check_vma=False,
    )
```

profile of v0, /device:TPU:0, one launch (start us, length us, event | category | flops | bytes accessed | tf_op | source)
XLA Modules:
  0.0 578.1 jit_solution(6870814687322997335)
XLA Ops:
  8.8 27.9 %all-gather.2 = s32[8,1,512]{2,1,0:T(1,128)S(1)} all-gather(s32[1,1,512]{2,1,0:T(1,128)} %bitcast.71), channel_id=1, replica_groups=mesh['batch'=4,'table'=8] {'table'}, dimensions={0}, use_global_device_ids=true | all-gather | bytes 18432 | tf_op jit(solution)/shard_map/all_gather | solution.py:50
  37.7 25.6 %gather_fusion.3 = bf16[4096]{0:T(1024)(128)(2,1)S(1)} fusion(bf16[4096]{0:T(1024)(128)(2,1)S(1)} %reshape.210, s32[4096]{0:T(1024)S(1)} %fusion.12), kind=kCustom, calls=%fused_computation.3 | custom fusion | bytes 32768 | tf_op jit(solution)/shard_map/jit(_take)/gather | solution.py:58
  63.3 17.0 %gather_fusion.2 = bf16[4096,256]{1,0:T(8,128)(2,1)} fusion(bf16[4096,256]{1,0:T(8,128)(2,1)S(1)} %bitcast.52, s32[4096]{0:T(1024)S(1)} %fusion.12), kind=kCustom, calls=%fused_computation.2 | custom fusion | bytes 4210688 | tf_op jit(solution)/shard_map/jit(_take)/gather | solution.py:57
  80.4 4.4 multiply_convert_fusion
  87.6 10.0 %compare_convert_fusion = f32[4096,2,8]{2,1,0:T(2,128)} fusion(s32[4096,2]{1,0:T(8,128)} %copy.42), kind=kLoop, calls=%fused_computation.15 | loop fusion | flops 131072 | bytes 294912 | tf_op jit(solution)/shard_map/convert_element_type | solution.py:35
  97.8 4.8 copy.40
  102.6 4.3 copy.41
  106.9 9.0 %reshape.207 = s32[65536,1]{0,1:T(1,128)S(1)} reshape(s32[4096,2,8]{2,1,0:T(2,128)} %copy.41) | data formatting | bytes 524288 | tf_op jit(solution)/shard_map/reshape | solution.py:32
  116.3 222.2 %gather_fusion = bf16[65536,128]{1,0:T(8,128)(2,1)} fusion(bf16[32768,128]{1,0:T(8,128)(2,1)} %bitcast.53, s32[65536]{0:T(1024)S(1)} %broadcast_clamp_fusion), kind=kCustom, calls=%fused_computation | custom fusion | bytes 33816576 | tf_op jit(solution)/shard_map/jit(_take)/gather | solution.py:36
  338.5 25.6 %multiply_reduce_fusion = bf16[4096,2,128]{2,1,0:T(2,128)(2,1)} fusion(f32[4096,2,8]{2,1,0:T(2,128)} %compare_convert_fusion, pred[4096,2,8]{2,1,0:T(4,128)(4,1)} %copy.40, bf16[65536,128]{1,0:T(8,128)(2,1)} %gather_fusion), kind=kLoop, calls=%fused_computation.8 | loop fusion | flops 32505856 | bytes 19202048 | tf_op jit(solution)/shard_map/reduce_sum | solution.py:37
  364.1 4.5 all-to-all-start
  370.9 52.1 %psum.15 = bf16[4096]{0:T(1024)(128)(2,1)S(1)} all-reduce(bf16[4096]{0:T(1024)(128)(2,1)S(1)} %get-tuple-element.10), channel_id=1, replica_groups=mesh['batch'=4,'table'=8] {'table'}, use_global_device_ids=true, to_apply=%region_3.4 | all-reduce | flops 4096 | bytes 16384 | tf_op jit(solution)/shard_map/psum | solution.py:61
  423.3 42.6 %all-gather.1 = bf16[64,64]{1,0:T(8,128)(2,1)S(1)} all-gather(bf16[8,64]{1,0:T(8,128)(2,1)S(1)} %gather_fusion.5), channel_id=3, replica_groups=mesh['batch'=4,'table'=8] {'table'}, dimensions={0}, use_global_device_ids=true | all-gather | bytes 9216 | tf_op jit(solution)/shard_map/all_gather | solution.py:72
  470.7 3.7 gather_fusion.1
  474.4 3.9 copy.45
  478.3 5.2 fusion.26
  485.6 6.2 %fusion.25 = (f32[512]{0:T(512)S(1)}, f32[512,4096]{1,0:T(8,128)}) fusion(f32[4096]{0:T(1024)S(1)} %convert_element_type.82, bf16[512,256]{1,0:T(8,128)(2,1)S(1)} %convolution_convert_fusion.1, bf16[4096,256]{1,0:T(8,128)(2,1)} %all-reduce.2.cloned.1.call-done), kind=kOutput, calls=%fused_computation.84 | convolution fusion | flops 1080032768 | bytes 10766336 | tf_op jit(solution)/shard_map/dot_general | solution.py:80
  491.8 9.5 %gather_fusion.7 = f32[512]{0:T(512)S(1)} fusion(f32[512,4096]{1,0:T(8,128)} %get-tuple-element.15, s32[512]{0:T(512)S(1)} %bitcast.54), kind=kCustom, calls=%fused_computation.7 | custom fusion | bytes 8192 | tf_op jit(solution)/shard_map/jit(take_along_axis)/gather | solution.py:92
  501.4 3.2 fusion
  505.4 3.1 fusion.2
  511.2 2.2 fusion.9
  513.3 7.3 %fusion.5 = bf16[64,16,8,128]{3,2,1,0:T(8,128)(2,1)} fusion(bf16[2048,1024]{1,0:T(8,128)(2,1)} %all-gather.6.cloned.1.call-done, f32[512,1024]{1,0:T(8,128)} %copy-done.12, bf16[512,256]{1,0:T(8,128)(2,1)S(1)} %fusion.9, bf16[1024,256]{1,0:T(8,128)(2,1)S(1)} %copy-done.9, f32[1024]{0:T(1024)S(1)} %copy-done.10), kind=kOutput, calls=%fused_computation.27 | convolution fusion | flops 2422210560 | bytes 9179136 | tf_op jit(solution)/shard_map/dot_general | solution.py:103
  524.9 42.3 %all_to_all.36 = bf16[512,16,128]{2,0,1:T(8,128)(2,1)S(1)} all-to-all(bf16[512,16,128]{2,0,1:T(8,128)(2,1)} %bitcast.58), channel_id=1, replica_groups=mesh['batch'=4,'table'=8] {'table'}, dimensions={1} | all-to-all | bytes 4194304 | tf_op jit(solution)/shard_map/all_to_all | solution.py:107
  567.2 3.5 copy.48
  (83 shorter events, 22.1 us)
Async XLA Ops:
  8.0 55.3 %copy-start = (bf16[64,64,256]{2,1,0:T(8,128)(2,1)S(1)}, bf16[64,64,256]{2,1,0:T(8,128)(2,1)}, u32[]{:S(2)}) copy-start(bf16[64,64,256]{2,1,0:T(8,128)(2,1)} %param.18) | copy-start | bytes 6291460
  8.0 470.3 %all-gather.6.cloned.1.call-start = ((), (), s32[]{:S(2)}) async-start(), calls=%async_computation.2 | async-start | bytes 5242880 | tf_op jit(solution)/shard_map/all_gather | solution.py:45
  8.7 476.9 %all-reduce.2.cloned.1.call-start = ((), (), s32[]{:S(2)}) async-start(), calls=%async_computation.3 | async-start | bytes 4194304 | tf_op jit(solution)/shard_map/psum | solution.py:60
  84.8 0.8 copy-start.7
  87.6 10.0 %copy-start.5 = (s32[4096,2,8]{0,2,1:T(8,128)S(1)}, s32[4096,2,8]{0,2,1:T(8,128)}, u32[]{:S(2)}) copy-start(s32[4096,2,8]{0,2,1:T(8,128)} %param.12) | copy-start | bytes 786436
  364.1 4.5 copy-start.8
  364.1 6.3 %copy-start.6 = (bf16[64,64]{1,0:T(8,128)(2,1)S(1)}, bf16[64,64]{1,0:T(8,128)(2,1)}, u32[]{:S(2)}) copy-start(bf16[64,64]{1,0:T(8,128)(2,1)} %param.19) | copy-start | bytes 24580
  364.1 101.9 %copy-start.11 = (s32[16]{0:T(128)S(1)}, s32[16]{0:T(128)}, u32[]{:S(2)}) copy-start(s32[16]{0:T(128)} %param.14) | copy-start | bytes 196
  364.1 103.3 %all-to-all-start = ((bf16[4096,2,128]{2,1,0:T(2,128)(2,1)}), bf16[4096,2,128]{2,1,0:T(2,128)(2,1)}, u32[]{:S(2)}, u32[]{:S(2)}) async-start(bf16[4096,2,128]{2,1,0:T(2,128)(2,1)} %multiply_reduce_fusion), calls=%async_computation | async-start | bytes 4194304 | tf_op jit(solution)/shard_map/all_to_all | solution.py:40
  368.6 132.8 %all-gather.8.cloned.1.call-start = ((), (), s32[]{:S(2)}) async-start(), calls=%async_computation.4 | async-start | bytes 2359296 | tf_op jit(solution)/shard_map/all_gather | solution.py:71
  478.3 6.6 %copy-start.9 = (bf16[1024,256]{1,0:T(8,128)(2,1)S(1)}, bf16[1024,256]{1,0:T(8,128)(2,1)}, u32[]{:S(2)}) copy-start(bf16[1024,256]{1,0:T(8,128)(2,1)} %param.17) | copy-start | bytes 1572868
  478.3 6.6 %copy-start.10 = (f32[1024]{0:T(1024)S(1)}, f32[1024]{0:T(1024)}, u32[]{:S(2)}) copy-start(f32[1024]{0:T(1024)} %param.16) | copy-start | bytes 12292
  483.6 1.3 copy-start.12
  501.4 4.0 copy-start.2
  505.4 3.7 copy-start.4
  509.1 2.0 copy-start.3
  567.2 3.5 copy-start.1
Sparse Core Ops, SparseCore 0:
  10.4 37.1 all-gather.5
  371.5 67.3 all-gather.7
Sparse Core Ops, SparseCore 1:
  84.9 101.3 all-reduce.1
where the time goes:
time: 579 us; the launch traced here: 578 us
  local copies, waits for them, and re-layouts  319 us (55%)
  blocking collectives  165 us (28%)
  other arithmetic  46.3 us (8%)
  matrix products  26.7 us (5%)
  between operations  15.8 us (3%)
    gather x1, local copies, waits for them, and re-layouts, on_device(): jnp.take(flat_tables, flat_ids, axis=0)  222 us
    psum x1, blocking collectives, on_device(): lax.psum(mine_lq.astype(jnp.bfloat16), 'table').astype(jnp.float32)  52.1 us
    all_gather x1, blocking collectives, on_device(): lax.all_gather(log_q[local_block], 'table', axis=0, tiled=True)  42.6 us
    all_to_all x1, blocking collectives, on_device(): lax.all_to_all(table_grad, 'table', split_axis=1, concat_axis=0, tiled=True)  42.3 us
    all_gather x1, blocking collectives, on_device(): item_ids = lax.all_gather(pos_items, 'table', axis=0, tiled=True)  27.9 us
    gather x1, local copies, waits for them, and re-layouts, on_device(): mine_lq = jnp.take(flat_lq, safe_item, axis=0).astype(jnp.float32) * held  25.6 us
    reduce_sum x1, other arithmetic, on_device(): jnp.sum(fetched.astype(jnp.float32) * weights[:, :, :, None], axis=2)  25.6 us
    gather x1, local copies, waits for them, and re-layouts, on_device(): jnp.take(flat_bank, safe_item, axis=0).astype(jnp.float32) * held[:, None]  17 us
  transfers between devices with their start and end apart: 4, of which 0 were waited for; matrix products, arithmetic and copies ran while one was open for 63% of the time, Pallas kernels for 0%

commit v1 on v0

v1 whole, which is shorter than its diff:
```python
import functools
import math

import jax
import jax.numpy as jnp
from jax import lax
from jax.experimental import pallas as pl
from jax.experimental.pallas import tpu as pltpu
from jax.sharding import PartitionSpec as P

MOST = 8
LANES = 128
LQ_ROWS = 16
VMEM_BYTES = 52 << 20
CONTRACT = (((1,), (1,)), ((), ()))
LOG2E = math.log2(math.e)
LN2 = math.log(2.0)


def whole(shape):
    return pl.BlockSpec(shape, lambda *_: (0,) * len(shape))


def pool_kernel(bag, ids_ref, table_ref, out_ref, wide, rows):
    table_rows = table_ref.shape[0]
    unroll = 16

    @pl.when(pl.program_id(0) == 0)
    def _():
        def widen(i, carry):
            at = pl.ds(pl.multiple_of(i * 256, 256), 256)
            wide[at, :] = table_ref[at, :].astype(jnp.float32)
            return carry

        lax.fori_loop(0, table_rows // 256, widen, 0)
        wide[pl.ds(table_rows, 8), :] = jnp.zeros((8, LANES), jnp.float32)

    def group(g, carry):
        base = pl.multiple_of(g * unroll, unroll)
        for j in range(unroll):
            got = [wide[pl.ds(ids_ref[base + (k * LANES + j)], 1), :] for k in range(bag)]
            while len(got) > 1:
                got = [got[i] + got[i + 1] for i in range(0, len(got), 2)]
            rows[pl.ds(base + j, 1), :] = got[0]
        return carry

    lax.fori_loop(0, LANES // unroll, group, 0)
    out_ref[...] = rows[...].astype(jnp.bfloat16)


def pool(ids, table, bag):
    bags = ids.shape[0] // bag
    table_rows, emb = table.shape
    return pl.pallas_call(
        functools.partial(pool_kernel, bag),
        grid=(bags // LANES,),
        in_specs=[
            pl.BlockSpec((LANES * bag,), lambda c: (c,), memory_space=pltpu.SMEM),
            pl.BlockSpec((table_rows, emb), lambda c: (0, 0), pipeline_mode=pl.Buffered(1)),
        ],
        out_specs=pl.BlockSpec((LANES, emb), lambda c: (c, 0)),
        out_shape=jax.ShapeDtypeStruct((bags, emb), jnp.bfloat16),
        scratch_shapes=[
            pltpu.VMEM((table_rows + 8, emb), jnp.float32),
            pltpu.VMEM((LANES, emb), jnp.float32),
        ],
        compiler_params=pltpu.CompilerParams(vmem_limit_bytes=VMEM_BYTES),
        cost_estimate=pl.CostEstimate(
            flops=bags * bag * emb, bytes_accessed=100_000_000, transcendentals=0
        ),
        name="pool",
    )(ids, table)


def items_kernel(ids_ref, row_ref, bank_ref, lq_ref, out_ref, low, high, part_low, part_high):
    count = ids_ref.shape[0]
    owned, width = bank_ref.shape
    items, blocks = lq_ref.shape
    unroll = 16
    step = 256

    def widen(i, carry):
        at = pl.ds(pl.multiple_of(i * step, step), step)
        both = bank_ref[at, :].astype(jnp.float32)
        low[at, :] = both[:, :LANES]
        high[at, :] = both[:, LANES:]
        return carry

    lax.fori_loop(0, owned // step, widen, 0)
    low[pl.ds(owned, 8), :] = jnp.zeros((8, LANES), jnp.float32)
    high[pl.ds(owned, 8), :] = jnp.zeros((8, LANES), jnp.float32)

    def part(c, carry):
        def group(g, inner):
            base = pl.multiple_of(g * unroll, unroll)
            for j in range(unroll):
                at = ids_ref[c * step + base + j]
                part_low[pl.ds(base + j, 1), :] = low[pl.ds(at, 1), :]
                part_high[pl.ds(base + j, 1), :] = high[pl.ds(at, 1), :]
            return inner

        lax.fori_loop(0, step // unroll, group, 0)
        at = pl.ds(pl.multiple_of(c * step, step), step)
        out_ref[at, :] = jnp.concatenate([part_low[...], part_high[...]], axis=1).astype(jnp.bfloat16)
        return carry

    lax.fori_loop(0, count // step, part, 0)
    for c in range(count // step):
        ids = row_ref[:, c * step : (c + 1) * step]
        spot = lax.broadcasted_iota(jnp.int32, (blocks, step), 0)
        one_hot = jnp.where(spot == lax.shift_right_arithmetic(ids, jnp.int32(items.bit_length() - 1)), 1.0, 0.0)
        by_item = jnp.dot(lq_ref[...], one_hot.astype(jnp.bfloat16), preferred_element_type=jnp.float32)
        spot = lax.broadcasted_iota(jnp.int32, (items, step), 0)
        kept = jnp.where(spot == (ids & (items - 1)), by_item, 0.0)
        line = jnp.sum(kept, axis=0, keepdims=True)
        low[pl.ds(c, 1), :] = line[:, :LANES]
        high[pl.ds(c, 1), :] = line[:, LANES:]
    tail = count // step
    out_ref[pl.ds(count, tail), :] = jnp.concatenate(
        [low[pl.ds(0, tail), :], high[pl.ds(0, tail), :]], axis=1
    ).astype(jnp.bfloat16)


def held_items(ids, bank, log_q):
    count = ids.shape[0]
    owned, width = bank.shape
    held = (ids >= 0) & (ids < owned)
    return pl.pallas_call(
        items_kernel,
        in_specs=[
            pl.BlockSpec(memory_space=pltpu.SMEM),
            pl.BlockSpec(memory_space=pltpu.VMEM),
            pl.BlockSpec(memory_space=pltpu.VMEM),
            pl.BlockSpec(memory_space=pltpu.VMEM),
        ],
        out_specs=pl.BlockSpec(memory_space=pltpu.VMEM),
        out_shape=jax.ShapeDtypeStruct((count + count // width, width), jnp.bfloat16),
        scratch_shapes=[
            pltpu.VMEM((owned + 8, LANES), jnp.float32),
            pltpu.VMEM((owned + 8, LANES), jnp.float32),
            pltpu.VMEM((256, LANES), jnp.float32),
            pltpu.VMEM((256, LANES), jnp.float32),
        ],
        compiler_params=pltpu.CompilerParams(vmem_limit_bytes=VMEM_BYTES),
        cost_estimate=pl.CostEstimate(flops=0, bytes_accessed=30_000_000, transcendentals=0),
        name="held_items",
    )(jnp.where(held, ids, owned), ids[None, :], bank, log_q.T)


def tower_kernel(
    scale, lead, slot_ref, npos_ref, own_ref, *refs
):
    (
        *x_refs, w_ref, b_ref, w2_ref, pos_ref, noise_ref, pos_bias_ref, noise_bias_ref,
        grad_ref, loss_ref, pre_ref, score_ref, noise_vec,
    ) = refs
    per_owner = len(x_refs)
    owners, users, emb = x_refs[0].shape
    npos = pos_bias_ref.shape[1]
    nnoise = noise_bias_ref.shape[1]
    items = nnoise // npos_ref.shape[0]
    width = pos_ref.shape[1]
    most = MOST * items

    def weight(s):
        return jnp.concatenate(
            [
                w_ref[pl.ds(pl.multiple_of(slot_ref[s * per_owner + j] * emb, emb), emb), :]
                for j in range(per_owner)
            ],
            axis=0,
        )

    pre = jnp.broadcast_to(b_ref[...], pre_ref.shape)
    for s in range(owners):
        x = jnp.concatenate([r[s] for r in x_refs], axis=1)
        pre = pre + jnp.dot(x, weight(s), preferred_element_type=jnp.float32)
    pre_ref[...] = pre
    hidden = (pre * jax.nn.sigmoid(pre)).astype(jnp.bfloat16)
    user_vec = jnp.dot(hidden, w2_ref[...], preferred_element_type=jnp.float32).astype(jnp.bfloat16)

    def fill(n, carry):
        place = npos_ref[n]
        owner, rank = place // MOST, place % MOST
        start = pl.multiple_of(owner * (most + LQ_ROWS) + rank * items, 16)
        noise_vec[pl.ds(pl.multiple_of(n * items, items), items), :] = noise_ref[pl.ds(start, items), :]
        return carry

    lax.fori_loop(0, npos_ref.shape[0], fill, 0)
    tile = 512
    spans = [(pos_ref, pos_bias_ref, c, c) for c in range(0, npos, tile)]
    spans += [(noise_vec, noise_bias_ref, c, npos + c) for c in range(0, nnoise, tile)]
    top = None
    for vec, bias, c, at in spans:
        s = lax.dot_general(user_vec, vec[c : c + tile, :], CONTRACT, preferred_element_type=jnp.float32)
        s = (s * scale - bias[:, c : c + tile]) * LOG2E
        score_ref[:, at : at + tile] = s
        for k in range(0, tile, LANES):
            piece = s[:, k : k + LANES]
            top = piece if top is None else jnp.maximum(top, piece)
    top = jnp.max(top, axis=1, keepdims=True)
    mixed = jnp.zeros((users, width), jnp.float32)
    denom = jnp.zeros((users, LANES), jnp.float32)
    for vec, bias, c, at in spans:
        p = jnp.exp2(score_ref[:, at : at + tile] - top)
        for k in range(0, tile, LANES):
            denom = denom + p[:, k : k + LANES]
        mixed = mixed + jnp.dot(p.astype(jnp.bfloat16), vec[c : c + tile, :], preferred_element_type=jnp.float32)
    denom = jnp.sum(denom, axis=1, keepdims=True)
    own = pos_ref[pl.ds(pl.multiple_of(own_ref[0] + lead, 16), users), :].astype(jnp.float32)
    own_dot = jnp.sum(user_vec.astype(jnp.float32) * own, axis=1, keepdims=True) * scale
    loss_ref[...] = (top + jnp.log2(denom)) * LN2 - own_dot
    user_grad = ((mixed / denom - own) * scale).astype(jnp.bfloat16)
    hidden_grad = lax.dot_general(user_grad, w2_ref[...], CONTRACT, preferred_element_type=jnp.float32)
    pre = pre_ref[...]
    sig = jax.nn.sigmoid(pre)
    pre_grad = (hidden_grad * sig * (1.0 + pre * (1.0 - sig))).astype(jnp.bfloat16)
    for s in range(owners):
        grad_ref[s] = lax.dot_general(
            pre_grad, weight(s), CONTRACT, preferred_element_type=jnp.float32
        ).astype(jnp.bfloat16)


def tower(part, users, slot, npos, own, xs, w, b, w2, pos, noise, pos_bias, noise_bias):
    owners, _, emb = xs[0].shape
    per_owner = len(xs)
    hid, width = w2.shape
    candidates = pos_bias.shape[1] + noise_bias.shape[1]
    once = pl.Buffered(1)
    smem = pl.BlockSpec(memory_space=pltpu.SMEM)
    flops = 2 * users * (2 * w.shape[0] * hid + 2 * hid * width + 2 * candidates * width)
    return pl.pallas_call(
        functools.partial(tower_kernel, width ** (-0.5), part * users),
        grid=(1,),
        in_specs=[smem] * 3
        + [pl.BlockSpec((owners, users, emb), lambda i: (0, part, 0), pipeline_mode=once)] * per_owner
        + [
            pl.BlockSpec(a.shape, lambda i: (0, 0), pipeline_mode=once)
            for a in (w, b, w2, pos, noise, pos_bias, noise_bias)
        ],
        out_specs=[
            pl.BlockSpec((owners, users, per_owner * emb), lambda i: (0, 0, 0)),
            pl.BlockSpec((users, 1), lambda i: (0, 0)),
        ],
        out_shape=[
            jax.ShapeDtypeStruct((owners, users, per_owner * emb), jnp.bfloat16),
            jax.ShapeDtypeStruct((users, 1), jnp.float32),
        ],
        scratch_shapes=[
            pltpu.VMEM((users, hid), jnp.float32),
            pltpu.VMEM((users, candidates), jnp.float32),
            pltpu.VMEM((noise_bias.shape[1], width), jnp.bfloat16),
        ],
        compiler_params=pltpu.CompilerParams(vmem_limit_bytes=VMEM_BYTES),
        cost_estimate=pl.CostEstimate(
            flops=flops, bytes_accessed=30_000_000, transcendentals=users * candidates
        ),
        name="tower",
    )(slot, npos, own, *xs, w, b, w2, pos, noise, pos_bias, noise_bias)


def on_device(
    tables,
    feature_ids,
    bag_lengths,
    feature_slot,
    w_first,
    b_first,
    w_second,
    bank,
    log_q,
    noise_lists,
    pos_items,
):
    row_users, per_owner, bag = feature_ids.shape
    _, table_rows, emb = tables.shape
    owners = lax.axis_size("table")
    me = lax.axis_index("table")
    blocks_dev, block_items, width = bank.shape
    users = row_users // owners

    item_ids = lax.all_gather(pos_items, "table", axis=0, tiled=True)
    owned = blocks_dev * block_items
    mine = held_items(item_ids - me * owned, bank.reshape(owned, width), log_q)
    pos = lax.psum(mine, "table")
    sample = noise_lists[0]
    owner_of = sample // blocks_dev
    same = owner_of[:, None] == owner_of[None, :]
    index = jnp.arange(sample.shape[0], dtype=jnp.int32)
    rank = jnp.sum((same & (index[None, :] < index[:, None])).astype(jnp.int32), axis=1)
    npos = owner_of * MOST + rank
    pick = (npos[None, :] == (me * MOST + jnp.arange(MOST, dtype=jnp.int32))[:, None]).astype(jnp.int32)
    local_block = jnp.sum(pick * (sample - me * blocks_dev)[None, :], axis=1)
    noise_lq = jnp.pad(log_q[local_block], ((0, LQ_ROWS - MOST), (0, width - block_items)))
    my_noise = jnp.concatenate([bank[local_block].reshape(MOST * block_items, width), noise_lq], axis=0)
    noise = lax.all_gather(my_noise, "table", axis=0, tiled=True)
    w_whole = lax.all_gather(w_first, "batch", axis=0, tiled=True)

    by_table = jnp.transpose(feature_ids, (1, 2, 0))
    used = jnp.arange(bag, dtype=jnp.int32)[None, :, None] < jnp.transpose(bag_lengths, (1, 0))[:, None, :]
    by_table = jnp.where(used, by_table, table_rows)
    by_table = by_table.reshape(per_owner, bag, row_users // LANES, LANES)
    flat_ids = jnp.transpose(by_table, (0, 2, 1, 3)).reshape(per_owner, row_users * bag)
    xs = []
    for j in range(per_owner):
        pooled = pool(flat_ids[j], tables[j], bag).reshape(owners, users, emb)
        xs.append(lax.all_to_all(pooled, "table", split_axis=0, concat_axis=0, tiled=True))

    pos_bias = pos[row_users:].astype(jnp.float32).reshape(1, row_users)
    by_owner = noise.reshape(owners, MOST * block_items + LQ_ROWS, width)
    got_lq = by_owner[:, MOST * block_items : MOST * block_items + MOST, :block_items]
    got_lq = got_lq.reshape(owners * MOST, block_items).astype(jnp.float32)
    noise_bias = got_lq[npos].reshape(1, -1)
    own = (me * users).astype(jnp.int32)[None]
    parts = 2
    grads, losses = [], []
    for part in range(parts):
        grad, loss = tower(
            part, users // parts, feature_slot, npos, own, xs, w_whole, b_first[None, :], w_second,
            pos, noise, pos_bias, noise_bias,
        )
        grads.append(lax.all_to_all(grad, "table", split_axis=0, concat_axis=0, tiled=True))
        losses.append(loss[:, 0])
    own_lq = lax.dynamic_slice_in_dim(pos_bias[0], me * users, users, 0)
    loss = jnp.concatenate(losses) + own_lq
    grad = jnp.concatenate(grads, axis=1).reshape(row_users, per_owner, emb)
    return (loss, grad)


def solution(mesh):
    return jax.shard_map(
        on_device,
        mesh=mesh,
        in_specs=(
            P("table", None, None),
            P("batch", "table", None),
            P("batch", "table"),
            P(),
            P("batch", None),
            P(),
            P(),
            P("table", None, None),
            P("table", None),
            P("batch", None),
            P(("batch", "table")),
        ),
        out_specs=(P(("batch", "table")), P("batch", "table", None)),
        check_vma=False,
    )
```

time: 579 us -> 346 us (0.60)
  local copies, waits for them, and re-layouts: 319 us -> 12.2 us
  waiting for transfers between devices: 0.76 us -> 165 us
  blocking collectives: 165 us -> 27.9 us
  Pallas kernels: 0 us -> 101 us
  other arithmetic: 46.3 us -> 4.87 us
  matrix products: 26.7 us -> 0 us
  starting transfers between devices: 4.61 us -> 21.1 us
    gather x8 -> x2, local copies, waits for them, and re-layouts: 285 us -> 2.72 us  [the longest x1 2.15 us: on_device(): bank[local_block].reshape(MOST * block_items, width)]
    pallas_call x0 -> x5, Pallas kernels: none -> 101 us  [the longest x2 65 us: pool(): pl.pallas_call(functools.partial(pool_kernel, bag), grid=(bags // LANES,)...]
    all_gather x2, waiting for transfers between devices: 0.02 us -> 84.4 us  [the longest x1 51.2 us: on_device(): noise = lax.all_gather(my_noise, 'table', axis=0, tiled=True)]
    psum x1 -> x0, blocking collectives: 52.1 us -> none  [on_device(): lax.psum(mine_lq.astype(jnp.bfloat16), 'table').astype(jnp.float32)]
    all_gather x1 -> x0, blocking collectives: 42.6 us -> none  [on_device(): lax.all_gather(log_q[local_block], 'table', axis=0, tiled=True)]
    all_to_all x1 -> x0, blocking collectives: 42.3 us -> none  [on_device(): lax.all_to_all(table_grad, 'table', split_axis=1, concat_axis=0, tiled=True)]
    psum x1, waiting for transfers between devices: 0.03 us -> 41.9 us  [on_device(): pos = lax.psum(mine, 'table')]
    all_to_all x1 -> x4, waiting for transfers between devices: 0.01 us -> 38.1 us  [the longest x2 38.1 us: on_device(): lax.all_to_all(grad, 'table', split_axis=0, concat_axis=0, tiled=True)]
  transfers between devices with their start and end apart: 4 -> 7, of which waited for: 0 -> 5; matrix products, arithmetic and copies ran while one was open for 63% -> 4% of each run, Pallas kernels for 0% -> 22%
where the time goes in v1:
time: 346 us
  waiting for transfers between devices  165 us (48%)
  Pallas kernels  101 us (29%)
  blocking collectives  27.9 us (8%)
  starting transfers between devices  21.1 us (6%)
  between operations  14 us (4%)
  local copies, waits for them, and re-layouts  12.2 us (4%)
  other arithmetic  4.87 us (1%)
    pallas_call x2, Pallas kernels, pool(): pl.pallas_call(functools.partial(pool_kernel, bag), grid=(bags // LANES,)...  65 us
    all_gather x1, waiting for transfers between devices, on_device(): noise = lax.all_gather(my_noise, 'table', axis=0, tiled=True)  51.2 us
    psum x1, waiting for transfers between devices, on_device(): pos = lax.psum(mine, 'table')  41.9 us
    all_to_all x2, waiting for transfers between devices, on_device(): lax.all_to_all(grad, 'table', split_axis=0, concat_axis=0, tiled=True)  38.1 us
    all_gather x1, waiting for transfers between devices, on_device(): w_whole = lax.all_gather(w_first, 'batch', axis=0, tiled=True)  33.2 us
    all_gather x1, blocking collectives, on_device(): item_ids = lax.all_gather(pos_items, 'table', axis=0, tiled=True)  27.9 us
    pallas_call x2, Pallas kernels, tower(): pl.pallas_call(functools.partial(tower_kernel, width ** (-0.5), part * us...  25.5 us
    all_to_all x2, starting transfers between devices, on_device(): lax.all_to_all(pooled, 'table', split_axis=0, concat_axis=0, tiled=True)  11.2 us
  transfers between devices with their start and end apart: 7, of which 5 were waited for; matrix products, arithmetic and copies ran while one was open for 4% of the time, Pallas kernels for 22%

profile of v1, /device:TPU:0, one launch (start us, length us, event | category | flops | bytes accessed | tf_op | source)
XLA Modules:
  0.0 345.7 jit_solution(8232367015695334823)
XLA Ops:
  7.2 27.9 %all-gather = s32[8,1,512]{2,1,0:T(1,128)S(1)} all-gather(s32[1,1,512]{2,1,0:T(1,128)} %bitcast.93), channel_id=1, replica_groups=mesh['batch'=4,'table'=8] {'table'}, dimensions={0}, use_global_device_ids=true | all-gather | bytes 18432 | tf_op jit(solution)/shard_map/all_gather | solution.py:282
  35.1 0.8 copy.16
  36.0 10.0 %held_items.1 = bf16[4112,256]{1,0:T(8,128)(2,1)} custom-call(s32[4096]{0:T(1024)S(1)} %and_select_fusion.ids_ref, s32[1,4096]{1,0:T(1,128)S(1)} %bitcast.82, bf16[4096,256]{1,0:T(8,128)(2,1)} %bitcast.88, bf16[64,64]{1,0:T(8,128)(2,1)S(1)} %bitcast.83), custom_call_target="tpu_custom_call" | custom-call | bytes 30000000 | tf_op jit(solution)/shard_map/held_items/pallas_call | solution.py:128
  47.1 2.2 gather_fusion
  49.2 0.7 fusion.1
  50.0 0.7 all-gather.4.cloned.1.call-update
  50.8 5.9 %slice_bitcast_fusion = (bf16[16384,128]{1,0:T(8,128)(2,1)}, bf16[16384,128]{1,0:T(8,128)(2,1)}) fusion(bf16[2,16384,128]{2,1,0:T(8,128)(2,1)} %param.11), kind=kLoop, calls=%fused_computation.3 | loop fusion | bytes 16777216 | tf_op jit(solution)/shard_map/squeeze | solution.py:306
  56.7 32.5 %pool.2 = bf16[4096,128]{1,0:T(8,128)(2,1)} custom-call(s32[32768]{0:T(1024)S(1)} %get-tuple-element.15.ids_ref, bf16[16384,128]{1,0:T(8,128)(2,1)} %get-tuple-element.11.table_ref), custom_call_target="tpu_custom_call" | custom-call | flops 4194304 | bytes 100000000 | tf_op jit(solution)/shard_map/pool/pallas_call | solution.py:54
  89.2 5.1 %all-to-all-start = ((bf16[8,512,128]{2,1,0:T(8,128)(2,1)}), bf16[8,512,128]{2,1,0:T(8,128)(2,1)S(1)}, u32[]{:S(2)}, u32[]{:S(2)}) async-start(bf16[8,512,128]{2,1,0:T(8,128)(2,1)} %bitcast.9), calls=%async_computation | async-start | bytes 2097152 | tf_op jit(solution)/shard_map/all_to_all | solution.py:307
  94.3 32.5 %pool.3 = bf16[4096,128]{1,0:T(8,128)(2,1)} custom-call(s32[32768]{0:T(1024)S(1)} %get-tuple-element.14.ids_ref, bf16[16384,128]{1,0:T(8,128)(2,1)} %get-tuple-element.10.table_ref), custom_call_target="tpu_custom_call" | custom-call | flops 4194304 | bytes 100000000 | tf_op jit(solution)/shard_map/pool/pallas_call | solution.py:54
  126.8 6.1 %all-to-all-start.1 = ((bf16[8,512,128]{2,1,0:T(8,128)(2,1)}), bf16[8,512,128]{2,1,0:T(8,128)(2,1)S(1)}, u32[]{:S(2)}, u32[]{:S(2)}) async-start(bf16[8,512,128]{2,1,0:T(8,128)(2,1)} %bitcast.13), calls=%async_computation.1 | async-start | bytes 2097152 | tf_op jit(solution)/shard_map/all_to_all | solution.py:307
  133.0 41.9 %all-reduce.3.cloned.1.call-done.refs_5_ = bf16[4112,256]{1,0:T(8,128)(2,1)} async-done(((bf16[4112,256]{1,0:T(8,128)(2,1)}), bf16[4112,256]{1,0:T(8,128)(2,1)}) %all-reduce.3.cloned.1.call-update) | async-done | bytes 2105360 | tf_op jit(solution)/shard_map/psum | solution.py:285
  174.9 0.7 convert_bitcast_fusion
  175.6 51.2 %all-gather.6.cloned.1.call-done.refs_6_ = bf16[4224,256]{1,0:T(8,128)(2,1)} async-done(((bf16[528,256]{1,0:T(8,128)(2,1)}), bf16[4224,256]{1,0:T(8,128)(2,1)}) %all-gather.6.cloned.1.call-update) | async-done | bytes 2162704 | tf_op jit(solution)/shard_map/all_gather | solution.py:296
  226.8 0.7 fusion.3
  228.2 33.2 %all-gather.4.cloned.1.call-done.refs_2_ = bf16[2048,1024]{1,0:T(8,128)(2,1)} async-done(((bf16[512,1024]{1,0:T(8,128)(2,1)}), bf16[2048,1024]{1,0:T(8,128)(2,1)}) %all-gather.4.cloned.1.call-update) | async-done | bytes 4194320 | tf_op jit(solution)/shard_map/all_gather | solution.py:297
  261.4 12.8 %tower.3 = (bf16[8,256,256]{2,1,0:T(8,128)(2,1)}, f32[256,1]{1,0:T(8,128)S(1)}) custom-call(s32[16]{0:T(128)S(1)} %copy-done.2, s32[32]{0:T(128)S(1)} %multiply_add_fusion.npos_ref, s32[1]{0:T(128)} %bitcast.2.own_ref, bf16[8,512,128]{2,1,0:T(8,128)(2,1)} %copy-done.3, bf16[8,512,128]{2,1,0:T(8,128)(2,1)} %copy-done.4, ...), custom_call_target="tpu_custom_call" | custom-call | flops 4026531840 | bytes 30000000 | tf_op jit(solution)/shard_map/tower/pallas_call | solution.py:232
  274.2 5.5 %all-to-all-start.3 = ((bf16[8,256,256]{2,1,0:T(8,128)(2,1)}), bf16[8,256,256]{2,1,0:T(8,128)(2,1)S(1)}, u32[]{:S(2)}, u32[]{:S(2)}) async-start(bf16[8,256,256]{2,1,0:T(8,128)(2,1)} %get-tuple-element.9), calls=%async_computation.3 | async-start | bytes 2097152 | tf_op jit(solution)/shard_map/all_to_all | solution.py:322
  279.7 12.8 %tower.2 = (bf16[8,256,256]{2,1,0:T(8,128)(2,1)}, f32[256,1]{1,0:T(8,128)S(1)}) custom-call(s32[16]{0:T(128)S(1)} %copy-done.2, s32[32]{0:T(128)S(1)} %multiply_add_fusion.npos_ref, s32[1]{0:T(128)} %bitcast.2.own_ref, bf16[8,512,128]{2,1,0:T(8,128)(2,1)} %copy-done.3, bf16[8,512,128]{2,1,0:T(8,128)(2,1)} %copy-done.4, ...), custom_call_target="tpu_custom_call" | custom-call | flops 4026531840 | bytes 30000000 | tf_op jit(solution)/shard_map/tower/pallas_call | solution.py:232
  292.5 13.4 %all-to-all-done.3 = bf16[8,256,256]{2,1,0:T(8,128)(2,1)S(1)} async-done(((bf16[8,256,256]{2,1,0:T(8,128)(2,1)}), bf16[8,256,256]{2,1,0:T(8,128)(2,1)S(1)}, u32[]{:S(2)}, u32[]{:S(2)}) %all-to-all-start.3) | async-done | bytes 1048608 | tf_op jit(solution)/shard_map/all_to_all | solution.py:322
  305.9 4.2 %all-to-all-start.2 = ((bf16[8,256,256]{2,1,0:T(8,128)(2,1)}), bf16[8,256,256]{2,1,0:T(8,128)(2,1)}, u32[]{:S(2)}, u32[]{:S(2)}) async-start(bf16[8,256,256]{2,1,0:T(8,128)(2,1)} %get-tuple-element.8), calls=%async_computation.2 | async-start | bytes 2097152 | tf_op jit(solution)/shard_map/all_to_all | solution.py:322
  311.1 24.7 %all-to-all-done.2 = bf16[8,256,256]{2,1,0:T(8,128)(2,1)} async-done(((bf16[8,256,256]{2,1,0:T(8,128)(2,1)}), bf16[8,256,256]{2,1,0:T(8,128)(2,1)}, u32[]{:S(2)}, u32[]{:S(2)}) %all-to-all-start.2) | async-done | bytes 1048608 | tf_op jit(solution)/shard_map/all_to_all | solution.py:322
  335.8 1.4 pad_maximum_fusion
  337.1 2.0 reshape.164
  (48 shorter events, 2.8 us)
Async XLA Ops:
  7.2 167.7 %all-reduce.3.cloned.1.call-start = ((), (), s32[]{:S(2)}) async-start(), calls=%async_computation.5 | async-start | bytes 4210688 | tf_op jit(solution)/shard_map/psum | solution.py:285
  36.0 10.1 %copy-start.8 = (s32[1,32]{1,0:T(1,128)S(1)}, s32[1,32]{1,0:T(1,128)}, u32[]{:S(2)}) copy-start(s32[1,32]{1,0:T(1,128)} %param.20) | copy-start | bytes 388
  36.0 10.5 %copy-start.6 = (bf16[64,64]{1,0:T(8,128)(2,1)S(1)}, bf16[64,64]{1,0:T(8,128)(2,1)}, u32[]{:S(2)}) copy-start(bf16[64,64]{1,0:T(8,128)(2,1)} %param.19) | copy-start | bytes 24580
  46.0 4.8 %copy-start.5 = (s32[4096,2,8]{0,2,1:T(8,128)S(1)}, s32[4096,2,8]{0,2,1:T(8,128)}, u32[]{:S(2)}) copy-start(s32[4096,2,8]{0,2,1:T(8,128)} %param.12) | copy-start | bytes 786436
  46.0 4.8 %copy-start.7 = (s32[4096,2]{0,1:T(2,128)S(1)}, s32[4096,2]{0,1:T(2,128)}, u32[]{:S(2)}) copy-start(s32[4096,2]{0,1:T(2,128)} %param.13) | copy-start | bytes 98308
  46.0 180.8 %all-gather.6.cloned.1.call-start = ((), (), s32[]{:S(2)}) async-start(), calls=%async_computation.6 | async-start | bytes 2433024 | tf_op jit(solution)/shard_map/all_gather | solution.py:296
  50.0 211.4 %all-gather.4.cloned.1.call-start = ((), (), s32[]{:S(2)}) async-start(), calls=%async_computation.4 | async-start | bytes 5242880 | tf_op jit(solution)/shard_map/all_gather | solution.py:297
  89.2 37.6 %all-to-all-start = ((bf16[8,512,128]{2,1,0:T(8,128)(2,1)}), bf16[8,512,128]{2,1,0:T(8,128)(2,1)S(1)}, u32[]{:S(2)}, u32[]{:S(2)}) async-start(bf16[8,512,128]{2,1,0:T(8,128)(2,1)} %bitcast.9), calls=%async_computation | async-start | bytes 2097152 | tf_op jit(solution)/shard_map/all_to_all | solution.py:307
  126.8 134.6 %copy-start = (bf16[1024,256]{1,0:T(8,128)(2,1)S(1)}, bf16[1024,256]{1,0:T(8,128)(2,1)}, u32[]{:S(2)}) copy-start(bf16[1024,256]{1,0:T(8,128)(2,1)} %refs_4_.3) | copy-start | bytes 1572868
  126.8 134.6 %copy-start.1 = (f32[1024]{0:T(1024)S(1)}, f32[1024]{0:T(1024)}, u32[]{:S(2)}) copy-start(f32[1024]{0:T(1024)} %param.16) | copy-start | bytes 12292
  126.8 134.6 %copy-start.2 = (s32[16]{0:T(128)S(1)}, s32[16]{0:T(128)}, u32[]{:S(2)}) copy-start(s32[16]{0:T(128)} %slot_ref.3) | copy-start | bytes 196
  126.8 134.6 %copy-start.3 = (bf16[8,512,128]{2,1,0:T(8,128)(2,1)}, bf16[8,512,128]{2,1,0:T(8,128)(2,1)S(1)}, u32[]{:S(2)}) copy-start(bf16[8,512,128]{2,1,0:T(8,128)(2,1)S(1)} %all-to-all-done.refs_0_) | copy-start | bytes 3145732
  126.8 101.4 %all-to-all-start.1 = ((bf16[8,512,128]{2,1,0:T(8,128)(2,1)}), bf16[8,512,128]{2,1,0:T(8,128)(2,1)S(1)}, u32[]{:S(2)}, u32[]{:S(2)}) async-start(bf16[8,512,128]{2,1,0:T(8,128)(2,1)} %bitcast.13), calls=%async_computation.1 | async-start | bytes 2097152 | tf_op jit(solution)/shard_map/all_to_all | solution.py:307
  228.2 33.2 %copy-start.4 = (bf16[8,512,128]{2,1,0:T(8,128)(2,1)}, bf16[8,512,128]{2,1,0:T(8,128)(2,1)S(1)}, u32[]{:S(2)}) copy-start(bf16[8,512,128]{2,1,0:T(8,128)(2,1)S(1)} %all-to-all-done.1.refs_1_) | copy-start | bytes 3145732
  274.2 31.7 %all-to-all-start.3 = ((bf16[8,256,256]{2,1,0:T(8,128)(2,1)}), bf16[8,256,256]{2,1,0:T(8,128)(2,1)S(1)}, u32[]{:S(2)}, u32[]{:S(2)}) async-start(bf16[8,256,256]{2,1,0:T(8,128)(2,1)} %get-tuple-element.9), calls=%async_computation.3 | async-start | bytes 2097152 | tf_op jit(solution)/shard_map/all_to_all | solution.py:322
  305.9 29.9 %all-to-all-start.2 = ((bf16[8,256,256]{2,1,0:T(8,128)(2,1)}), bf16[8,256,256]{2,1,0:T(8,128)(2,1)}, u32[]{:S(2)}, u32[]{:S(2)}) async-start(bf16[8,256,256]{2,1,0:T(8,128)(2,1)} %get-tuple-element.8), calls=%async_computation.2 | async-start | bytes 2097152 | tf_op jit(solution)/shard_map/all_to_all | solution.py:322
Sparse Core Ops, SparseCore 0:
  46.1 128.7 all-reduce.2
  177.1 49.6 all-gather.5
  228.4 32.9 all-gather.3

commit v2 on v1

v2 whole, which is shorter than its diff:
```python
import functools
import math

import jax
import jax.numpy as jnp
from jax import lax
from jax.experimental import pallas as pl
from jax.experimental.pallas import tpu as pltpu
from jax.sharding import PartitionSpec as P

MOST = 8
LANES = 128
LQ_ROWS = 16
VMEM_BYTES = 52 << 20
ITEM_BYTES = 24 << 20
CONTRACT = (((1,), (1,)), ((), ()))
LOG2E = math.log2(math.e)
LN2 = math.log(2.0)


def whole(shape):
    return pl.BlockSpec(shape, lambda *_: (0,) * len(shape))


def pool_kernel(bag, ids_ref, table_ref, *refs):
    out_ref, wide, rows = refs[-3:]
    table_rows = table_ref.shape[1]
    unroll = 16

    @pl.when(pl.program_id(0) == 0)
    def _():
        def widen(i, carry):
            at = pl.ds(pl.multiple_of(i * 256, 256), 256)
            wide[at, :] = table_ref[0, at, :].astype(jnp.float32)
            return carry

        lax.fori_loop(0, table_rows // 256, widen, 0)
        wide[pl.ds(table_rows, 8), :] = jnp.zeros((8, LANES), jnp.float32)

    def group(g, carry):
        base = pl.multiple_of(g * unroll, unroll)
        for j in range(unroll):
            got = [wide[pl.ds(ids_ref[base + (k * LANES + j)], 1), :] for k in range(bag)]
            while len(got) > 1:
                got = [got[i] + got[i + 1] for i in range(0, len(got), 2)]
            rows[pl.ds(base + j, 1), :] = got[0]
        return carry

    lax.fori_loop(0, LANES // unroll, group, 0)
    out_ref[...] = rows[...].astype(jnp.bfloat16)


def pool(ids, tables, table, bag, order, first, last, blocks, given):
    _, table_rows, emb = tables.shape
    more = [] if given is None else [given]
    return pl.pallas_call(
        functools.partial(pool_kernel, bag),
        grid=(last - first,),
        in_specs=[
            pl.BlockSpec((LANES * bag,), lambda c: (order(c + first),), memory_space=pltpu.SMEM),
            pl.BlockSpec((1, table_rows, emb), lambda c: (table, 0, 0), pipeline_mode=pl.Buffered(1)),
        ]
        + [pl.BlockSpec(memory_space=pl.ANY)] * len(more),
        out_specs=pl.BlockSpec((LANES, emb), lambda c: (c + first, 0)),
        out_shape=jax.ShapeDtypeStruct((blocks * LANES, emb), jnp.bfloat16),
        scratch_shapes=[
            pltpu.VMEM((table_rows + 8, emb), jnp.float32),
            pltpu.VMEM((LANES, emb), jnp.float32),
        ],
        input_output_aliases={2: 0} if more else {},
        compiler_params=pltpu.CompilerParams(vmem_limit_bytes=VMEM_BYTES),
        cost_estimate=pl.CostEstimate(
            flops=(last - first) * LANES * bag * emb,
            bytes_accessed=(last - first) * 100_000,
            transcendentals=0,
        ),
        name="pool",
    )(ids, tables, *more)


def items_kernel(users, place_ref, ids_ref, row_ref, bank_ref, lq_ref, *refs):
    *out_refs, low, high, part_low, part_high = refs
    count = ids_ref.shape[0]
    owned, width = bank_ref.shape
    items, blocks = lq_ref.shape
    unroll = 16
    step = 256

    def widen(i, carry):
        at = pl.ds(pl.multiple_of(i * step, step), step)
        both = bank_ref[at, :].astype(jnp.float32)
        low[at, :] = both[:, :LANES]
        high[at, :] = both[:, LANES:]
        return carry

    lax.fori_loop(0, owned // step, widen, 0)
    low[pl.ds(owned, 8), :] = jnp.zeros((8, LANES), jnp.float32)
    high[pl.ds(owned, 8), :] = jnp.zeros((8, LANES), jnp.float32)
    per = users // step
    held = users + LQ_ROWS
    me = place_ref[0]
    for p, out_ref in enumerate(out_refs):
        def part(c, carry):
            block = c // per
            start = (me ^ (2 * block + p)) * users + (c % per) * step

            def group(g, inner):
                base = pl.multiple_of(g * unroll, unroll)
                for j in range(unroll):
                    at = ids_ref[start + base + j]
                    part_low[pl.ds(base + j, 1), :] = low[pl.ds(at, 1), :]
                    part_high[pl.ds(base + j, 1), :] = high[pl.ds(at, 1), :]
                return inner

            lax.fori_loop(0, step // unroll, group, 0)
            at = pl.ds(pl.multiple_of((c % per) * step, 16), step)
            out_ref[block, at, :] = jnp.concatenate([part_low[...], part_high[...]], axis=1).astype(jnp.bfloat16)
            return carry

        lax.fori_loop(0, count // step // 2, part, 0)
        for block in range(out_ref.shape[0]):
            lines = []
            for c in range(per):
                at = pl.multiple_of((me ^ (2 * block + p)) * users + c * step, step)
                ids = row_ref[:, pl.ds(at, step)]
                spot = lax.broadcasted_iota(jnp.int32, (blocks, step), 0)
                shift = jnp.int32(items.bit_length() - 1)
                one_hot = jnp.where(spot == lax.shift_right_arithmetic(ids, shift), 1.0, 0.0)
                by_item = jnp.dot(lq_ref[...], one_hot.astype(jnp.bfloat16), preferred_element_type=jnp.float32)
                spot = lax.broadcasted_iota(jnp.int32, (items, step), 0)
                kept = jnp.where(spot == (ids & (items - 1)), by_item, 0.0)
                lines.append(jnp.sum(kept, axis=0, keepdims=True))
            lines.append(jnp.zeros((LQ_ROWS - per, step), jnp.float32))
            out_ref[block, pl.ds(users, LQ_ROWS), :] = jnp.concatenate(lines, axis=0).astype(jnp.bfloat16)


def held_items(place, ids, users, bank, log_q):
    count = ids.shape[0]
    owned, width = bank.shape
    held = (ids >= 0) & (ids < owned)
    out = jax.ShapeDtypeStruct((count // users // 2, users + LQ_ROWS, width), jnp.bfloat16)
    return pl.pallas_call(
        functools.partial(items_kernel, users),
        in_specs=[pl.BlockSpec(memory_space=pltpu.SMEM)] * 2 + [pl.BlockSpec(memory_space=pltpu.VMEM)] * 3,
        out_specs=[pl.BlockSpec(memory_space=pltpu.VMEM)] * 2,
        out_shape=[out, out],
        scratch_shapes=[
            pltpu.VMEM((owned + 8, LANES), jnp.float32),
            pltpu.VMEM((owned + 8, LANES), jnp.float32),
            pltpu.VMEM((256, LANES), jnp.float32),
            pltpu.VMEM((256, LANES), jnp.float32),
        ],
        compiler_params=pltpu.CompilerParams(vmem_limit_bytes=ITEM_BYTES),
        cost_estimate=pl.CostEstimate(flops=0, bytes_accessed=30_000_000, transcendentals=0),
        name="held_items",
    )(place, jnp.where(held, ids, owned), ids[None, :], bank, log_q.T)


def tower_kernel(scale, lead, n_x, table_of_ref, count_ref, *refs):
    x_refs, refs = refs[:n_x], refs[n_x:]
    owners, users, emb = x_refs[0].shape
    w_first_ref, b_ref, w2_ref, *refs = refs
    pos_refs, refs = refs[:owners], refs[owners:]
    noise_refs, refs = refs[:2], refs[2:]
    grad_ref, loss_ref, w_ref, pre_ref, score_ref, noise_vec, noise_lq, picked_lq, w_sem = refs
    depth = n_x * emb
    held, width = pos_refs[0].shape
    batch_users = held - LQ_ROWS
    most = 2 * noise_refs[0].shape[0] // owners - LQ_ROWS
    items = most // MOST
    nnoise = noise_vec.shape[0]

    def place(slot, table):
        return pltpu.make_async_copy(
            w_first_ref.at[pl.ds(slot * emb, emb), :],
            w_ref.at[pl.ds(pl.multiple_of(table * emb, emb), emb), :],
            w_sem.at[table],
        )

    for slot in range(w_first_ref.shape[0] // emb):
        place(slot, table_of_ref[slot]).start()
    filled = jnp.int32(0)
    for o in range(owners):
        noise_ref = noise_refs[o // (owners // 2)]
        begin = o % (owners // 2) * (most + LQ_ROWS)
        noise_lq[...] = noise_ref[pl.ds(begin + most, LQ_ROWS), :LANES].astype(jnp.float32)
        used = count_ref[o]

        def fill(k, carry):
            n = filled + k
            start = pl.multiple_of(begin + k * items, 16)
            noise_vec[pl.ds(pl.multiple_of(n * items, items), items), :] = noise_ref[pl.ds(start, items), :]
            picked_lq[pl.ds(n, 1), :] = noise_lq[pl.ds(k, 1), :]
            return carry

        lax.fori_loop(0, used, fill, 0)
        filled = filled + used
    def weight(s):
        return w_ref[pl.ds(pl.multiple_of(s * depth, depth), depth), :]

    pre = jnp.broadcast_to(b_ref[...], pre_ref.shape)
    for s in range(owners):
        x = jnp.concatenate([r[s] for r in x_refs], axis=1)
        for table in range(s * n_x, (s + 1) * n_x):
            place(0, table).wait()
        pre = pre + jnp.dot(x, weight(s), preferred_element_type=jnp.float32)
    pre_ref[...] = pre
    hidden = (pre * jax.nn.sigmoid(pre)).astype(jnp.bfloat16)
    user_vec = jnp.dot(hidden, w2_ref[...], preferred_element_type=jnp.float32).astype(jnp.bfloat16)
    tile = 512
    spans = []
    for ref in pos_refs:
        lines = ref[pl.ds(batch_users, LQ_ROWS), :].astype(jnp.float32)
        line = jnp.concatenate([lines[i : i + 1, :] for i in range(batch_users // width)], axis=1)
        for c in range(0, batch_users, tile):
            spans.append((ref, c, line[:, c : c + tile]))
    for c in range(0, nnoise, tile):
        rows = [picked_lq[pl.ds(n, 1), :][:, :items] for n in range(c // items, (c + tile) // items)]
        spans.append((noise_vec, c, jnp.concatenate(rows, axis=1)))
    top = None
    for n, (vec, c, bias) in enumerate(spans):
        s = lax.dot_general(user_vec, vec[pl.ds(c, tile), :], CONTRACT, preferred_element_type=jnp.float32)
        s = (s * scale - bias) * LOG2E
        score_ref[:, n * tile : (n + 1) * tile] = s
        for k in range(0, tile, LANES):
            piece = s[:, k : k + LANES]
            top = piece if top is None else jnp.maximum(top, piece)
    top = jnp.max(top, axis=1, keepdims=True)
    mixed = jnp.zeros((users, width), jnp.float32)
    denom = jnp.zeros((users, LANES), jnp.float32)
    for n, (vec, c, _) in enumerate(spans):
        p = jnp.exp2(score_ref[:, n * tile : (n + 1) * tile] - top)
        for k in range(0, tile, LANES):
            denom = denom + p[:, k : k + LANES]
        mixed = mixed + jnp.dot(p.astype(jnp.bfloat16), vec[pl.ds(c, tile), :], preferred_element_type=jnp.float32)
    denom = jnp.sum(denom, axis=1, keepdims=True)
    own = pos_refs[0][pl.ds(lead, users), :].astype(jnp.float32)
    own_dot = jnp.sum(user_vec.astype(jnp.float32) * own, axis=1, keepdims=True) * scale
    loss_ref[...] = (top + jnp.log2(denom)) * LN2 - own_dot
    user_grad = ((mixed / denom - own) * scale).astype(jnp.bfloat16)
    hidden_grad = lax.dot_general(user_grad, w2_ref[...], CONTRACT, preferred_element_type=jnp.float32)
    pre = pre_ref[...]
    sig = jax.nn.sigmoid(pre)
    pre_grad = (hidden_grad * sig * (1.0 + pre * (1.0 - sig))).astype(jnp.bfloat16)
    for s in range(owners):
        grad_ref[s] = lax.dot_general(
            pre_grad, weight(s), CONTRACT, preferred_element_type=jnp.float32
        ).astype(jnp.bfloat16)


def tower(lead, users, table_of, counts, xs, w, b, w2, pos, noise, n_noise):
    owners, _, emb = xs[0][0].shape
    per_owner = len(xs)
    hid, width = w2.shape
    depth = owners * per_owner * emb
    candidates = owners * (pos[0].shape[0] - LQ_ROWS) + n_noise
    once = pl.Buffered(1)
    smem = pl.BlockSpec(memory_space=pltpu.SMEM)
    flops = 2 * users * (2 * depth * hid + 2 * hid * width + 2 * candidates * width)
    wide = per_owner * emb
    return pl.pallas_call(
        functools.partial(tower_kernel, width ** (-0.5), lead, per_owner),
        grid=(1,),
        in_specs=[smem] * 2
        + [
            pl.BlockSpec((owners, users, emb), lambda i, at=at: (0, at, 0), pipeline_mode=once) for _, at in xs
        ]
        + [pl.BlockSpec(memory_space=pl.ANY)]
        + [pl.BlockSpec(a.shape, lambda i: (0, 0), pipeline_mode=once) for a in (b, w2, *pos, *noise)],
        out_specs=[
            pl.BlockSpec((owners, users, wide), lambda i: (0, 0, 0)),
            pl.BlockSpec((users, 1), lambda i: (0, 0)),
        ],
        out_shape=[
            jax.ShapeDtypeStruct((owners, users, wide), jnp.bfloat16),
            jax.ShapeDtypeStruct((users, 1), jnp.float32),
        ],
        scratch_shapes=[
            pltpu.VMEM((depth, hid), jnp.bfloat16),
            pltpu.VMEM((users, hid), jnp.float32),
            pltpu.VMEM((users, candidates), jnp.float32),
            pltpu.VMEM((n_noise, width), jnp.bfloat16),
            pltpu.VMEM((LQ_ROWS, LANES), jnp.float32),
            pltpu.VMEM((n_noise * MOST // (2 * noise[0].shape[0] // owners - LQ_ROWS), LANES), jnp.float32),
            pltpu.SemaphoreType.DMA((depth // emb,)),
        ],
        compiler_params=pltpu.CompilerParams(vmem_limit_bytes=VMEM_BYTES),
        cost_estimate=pl.CostEstimate(
            flops=flops, bytes_accessed=60_000_000, transcendentals=users * candidates
        ),
        name="tower",
    )(table_of, counts, *(x for x, _ in xs), w, b, w2, *pos, *noise)


def swap(x, axis, offset):
    size = lax.axis_size(axis)
    return lax.ppermute(x, axis, [(i, i ^ offset) for i in range(size)])


class Spread:
    def __init__(self, x, axis):
        self.axis, self.size = axis, lax.axis_size(axis)
        self.offset = self.size // 2
        self.got, self.fresh, self.sent = {0: x}, [0], {}

    def send(self, tied=()):
        self.got.update(zip(self.sent, tied))
        sent = {}
        if self.offset > 1:
            sent = {o | self.offset: swap(v, self.axis, self.offset) for o, v in self.got.items() if not o & 1}
        sent.update({o | 1: swap(self.got[o], self.axis, 1) for o in self.fresh})
        self.fresh = [o for o in sent if not o & 1]
        self.offset //= 2
        self.sent = sent
        return list(sent.values())

    def finish(self, tied=()):
        values = self.send(tied)
        while self.sent:
            values = self.send(values)
        return [self.got[o] for o in range(self.size)]


def tie(*values):
    return lax.optimization_barrier(values)


def on_device(
    tables,
    feature_ids,
    bag_lengths,
    feature_slot,
    w_first,
    b_first,
    w_second,
    bank,
    log_q,
    noise_lists,
    pos_items,
):
    row_users, per_owner, bag = feature_ids.shape
    _, table_rows, emb = tables.shape
    owners = lax.axis_size("table")
    me = lax.axis_index("table")
    blocks_dev, block_items, width = bank.shape
    users = row_users // owners

    place = me.astype(jnp.int32)[None]

    copies = jnp.broadcast_to(pos_items[None, :], (owners, users))
    item_ids = lax.all_to_all(copies, "table", split_axis=0, concat_axis=0, tiled=True).reshape(-1)
    sample = noise_lists[0]
    owner_of = sample // blocks_dev
    same = owner_of[:, None] == owner_of[None, :]
    index = jnp.arange(sample.shape[0], dtype=jnp.int32)
    rank = jnp.sum((same & (index[None, :] < index[:, None])).astype(jnp.int32), axis=1)
    npos = owner_of * MOST + rank
    pick = (npos[None, :] == (me * MOST + jnp.arange(MOST, dtype=jnp.int32))[:, None]).astype(jnp.int32)
    local_block = jnp.sum(pick * (sample - me * blocks_dev)[None, :], axis=1)
    noise_lq = jnp.pad(log_q[local_block], ((0, LQ_ROWS - MOST), (0, width - block_items)))
    my_noise = jnp.concatenate([bank[local_block].reshape(MOST * block_items, width), noise_lq], axis=0)
    w_whole = lax.all_gather(w_first, "batch", axis=0, tiled=True)
    near_noise, noise_from, offset = [my_noise], [0], owners // 2
    noise_got = [swap(my_noise, "table", offset)]
    owned = blocks_dev * block_items
    same, other = held_items(place, item_ids - me * owned, users, bank.reshape(owned, width), log_q)

    by_table = jnp.transpose(feature_ids, (1, 2, 0))
    used = jnp.arange(bag, dtype=jnp.int32)[None, :, None] < jnp.transpose(bag_lengths, (1, 0))[:, None, :]
    by_table = jnp.where(used, by_table, table_rows)
    by_table = by_table.reshape(per_owner, bag, row_users // LANES, LANES)
    by_table = jnp.transpose(by_table, (0, 2, 1, 3)).reshape(per_owner, row_users * bag)
    ids = [by_table[j] for j in range(per_owner)]
    blocks = row_users // LANES
    block_users = users // LANES
    part_blocks = block_users // 2
    half = blocks // 2

    def straight(c):
        return c

    def halves(c):
        h, c = c // half, c % half
        return c // part_blocks * block_users + h * part_blocks + c % part_blocks

    def exchange(pooled):
        pooled = pooled.reshape(owners, -1, emb)
        return lax.all_to_all(pooled, "table", split_axis=0, concat_axis=0, tiled=True)

    def both(a, b):
        return (a.astype(jnp.float32) + b.astype(jnp.float32)).astype(jnp.bfloat16)

    same, other, tables, *ids = tie(same, other, tables, *ids)

    def more_noise():
        near_noise.extend(noise_got)
        noise_from.extend([o ^ offset for o in noise_from])

    near = swap(other, "table", 1)
    while offset > 2:
        more_noise()
        offset //= 2
        noise_got = [swap(v, "table", offset) for v in near_noise]
    cut = blocks * 5 // 8
    pooled = pool(ids[0], tables, 0, bag, straight, 0, cut, blocks, None)
    pooled, near, noise_got, *ids = tie(pooled, near, noise_got, *ids)
    more_noise()
    near_noise = jnp.concatenate(near_noise, axis=0)
    far_noise = swap(near_noise, "table", 1)
    sums = [both(same[q], near[q]) for q in range(owners // 2)]
    far = [swap(sums[q], "table", 2 * q) for q in range(1, owners // 2)]
    pooled = pool(ids[0], tables, 0, bag, straight, cut, blocks, blocks, pooled)
    whole = [pooled]
    for j in range(1, per_owner - 1):
        tables, pooled = tie(tables, pooled)
        pooled = pool(ids[j], tables, j, bag, straight, 0, blocks, blocks, None)
        whole.append(pooled)

    tables, whole, far, sums, far_noise = tie(tables, whole, far, sums, far_noise)
    own_pos = sums[0].astype(jnp.float32)
    for block in far:
        own_pos = own_pos + block.astype(jnp.float32)
    own_pos = own_pos.astype(jnp.bfloat16)
    own_pos, tables = tie(own_pos, tables)
    pos_rounds = Spread(own_pos, "table")
    got = pos_rounds.send()

    last = ids[-1]
    final = functools.partial(pool, tables=tables, table=per_owner - 1, bag=bag, order=halves, blocks=blocks)
    cut = blocks // 4
    pooled = final(ids=last, first=0, last=cut, given=None)
    pooled, whole, got, last = tie(pooled, whole, got, last)
    xs = [exchange(v) for v in whole]
    got = pos_rounds.send(got)
    pooled = final(ids=last, first=cut, last=blocks - cut, given=pooled)
    pooled, xs, got, last = tie(pooled, xs, got, last)
    early = exchange(pooled[: row_users // 2])
    got = pos_rounds.send(got)
    pooled = final(ids=last, first=blocks - cut, last=blocks, given=pooled)
    pooled, early, got = tie(pooled, early, got)
    late = exchange(pooled[row_users // 2 :])
    pos = pos_rounds.finish(got)

    slots = jnp.arange(feature_slot.shape[0], dtype=jnp.int32)
    table_of = jnp.sum(jnp.where(feature_slot[None, :] == slots[:, None], slots[None, :], 0), axis=1)
    noise_owner = me ^ jnp.asarray(noise_from + [o ^ 1 for o in noise_from], jnp.int32)
    counts = jnp.sum((owner_of[None, :] == noise_owner[:, None]).astype(jnp.int32), axis=1)
    run = functools.partial(
        tower, users=users // 2, table_of=table_of, counts=counts, w=w_whole, b=b_first[None, :], w2=w_second, pos=pos,
        noise=[near_noise, far_noise], n_noise=sample.shape[0] * block_items,
    )
    grad_early, loss_early = run(lead=0, xs=[(v, 0) for v in xs] + [(early, 0)])
    back = [lax.all_to_all(grad_early, "table", split_axis=0, concat_axis=0, tiled=True)]
    _, late = tie(loss_early, late)
    grad_late, loss_late = run(lead=users // 2, xs=[(v, 1) for v in xs] + [(late, 0)])
    back[0], grad_late = tie(back[0], grad_late)
    back.append(lax.all_to_all(grad_late, "table", split_axis=0, concat_axis=0, tiled=True))
    losses = [loss_early[:, 0], loss_late[:, 0]]
    own_lq = own_pos[users : users + users // width].astype(jnp.float32).reshape(users)
    grad = jnp.concatenate(back, axis=1).reshape(row_users, per_owner, emb)
    return (jnp.concatenate(losses) + own_lq, grad)


def solution(mesh):
    return jax.shard_map(
        on_device,
        mesh=mesh,
        in_specs=(
            P("table", None, None),
            P("batch", "table", None),
            P("batch", "table"),
            P(),
            P("batch", None),
            P(),
            P(),
            P("table", None, None),
            P("table", None),
            P("batch", None),
            P(("batch", "table")),
        ),
        out_specs=(P(("batch", "table")), P("batch", "table", None)),
        check_vma=False,
    )
```

time: 346 us -> 262 us (0.76)
  waiting for transfers between devices: 165 us -> 71.5 us
  starting transfers between devices: 21.1 us -> 50.8 us
  blocking collectives: 27.9 us -> 0 us
  Pallas kernels: 101 us -> 109 us
    all_gather x1 -> x0, waiting for transfers between devices: 51.2 us -> none  [on_device(): noise = lax.all_gather(my_noise, 'table', axis=0, tiled=True)]
    psum x1 -> x0, waiting for transfers between devices: 41.9 us -> none  [on_device(): pos = lax.psum(mine, 'table')]
    all_gather x1, waiting for transfers between devices: 33.2 us -> 0.01 us  [on_device(): w_whole = lax.all_gather(w_first, 'batch', axis=0, tiled=True)]
    ppermute x0 -> x15, waiting for transfers between devices: none -> 30.3 us  [swap(): return lax.ppermute(x, axis, [(i, i ^ offset) for i in range(size)])]
    all_gather x1 -> x0, blocking collectives: 27.9 us -> none  [on_device(): item_ids = lax.all_gather(pos_items, 'table', axis=0, tiled=True)]
    ppermute x0 -> x15, starting transfers between devices: none -> 19.5 us  [swap(): return lax.ppermute(x, axis, [(i, i ^ offset) for i in range(size)])]
    all_to_all x4 -> x6, starting transfers between devices: 21 us -> 31.3 us  [the longest x3 14.3 us: exchange(): lax.all_to_all(pooled, 'table', split_axis=0, concat_axis=0, tiled=True)]
    pallas_call x5 -> x8, Pallas kernels: 101 us -> 109 us  [the longest x5 74.3 us: pool(): pl.pallas_call(functools.partial(pool_kernel, bag), grid=(last - first,),...]
  transfers between devices with their start and end apart: 7 -> 22, of which waited for: 5 -> 9; matrix products, arithmetic and copies ran while one was open for 4% -> 4% of each run, Pallas kernels for 22% -> 42%
where the time goes in v2:
time: 262 us; the launch traced here: 261 us
  Pallas kernels  109 us (42%)
  waiting for transfers between devices  71.5 us (27%)
  starting transfers between devices  50.8 us (19%)
  between operations  14.4 us (5%)
  local copies, waits for them, and re-layouts  8.88 us (3%)
  other arithmetic  6.47 us (2%)
    pallas_call x5, Pallas kernels, pool(): pl.pallas_call(functools.partial(pool_kernel, bag), grid=(last - first,),...  74.3 us
    ppermute x15, waiting for transfers between devices, swap(): return lax.ppermute(x, axis, [(i, i ^ offset) for i in range(size)])  30.3 us
    pallas_call x2, Pallas kernels, tower(): pl.pallas_call(functools.partial(tower_kernel, width ** (-0.5), lead, per...  25.6 us
    all_to_all x1, waiting for transfers between devices, on_device(): lax.all_to_all(grad_late, 'table', split_axis=0, concat_axis=0, tiled=True)  24.7 us
    ppermute x15, starting transfers between devices, swap(): return lax.ppermute(x, axis, [(i, i ^ offset) for i in range(size)])  19.5 us
    all_to_all x3, starting transfers between devices, exchange(): lax.all_to_all(pooled, 'table', split_axis=0, concat_axis=0, tiled=True)  14.3 us
    all_to_all x1, waiting for transfers between devices, on_device(): lax.all_to_all(grad_early, 'table', split_axis=0, concat_axis=0, tiled=True)  11.4 us
    pallas_call x1, Pallas kernels, held_items(): pl.pallas_call(functools.partial(items_kernel, users), in_specs=[pl.Block...  9.14 us
  transfers between devices with their start and end apart: 22, of which 9 were waited for; matrix products, arithmetic and copies ran while one was open for 4% of the time, Pallas kernels for 42%

profile of v2, /device:TPU:0, one launch (start us, length us, event | category | flops | bytes accessed | tf_op | source)
XLA Modules:
  0.0 261.0 jit_solution(3660114160665781535)
XLA Ops:
  8.5 7.4 %all-to-all-start = ((s32[8,1,512]{2,1,0:T(1,128)}), s32[8,1,512]{2,1,0:T(1,128)S(1)}, u32[]{:S(2)}, u32[]{:S(2)}) async-start(s32[8,1,512]{2,1,0:T(1,128)} %broadcast_in_dim.23), calls=%async_computation | async-start | bytes 32768 | tf_op jit(solution)/shard_map/all_to_all | solution.py:351
  18.2 4.3 %all-to-all-done = s32[8,1,512]{2,1,0:T(1,128)S(1)} async-done(((s32[8,1,512]{2,1,0:T(1,128)}), s32[8,1,512]{2,1,0:T(1,128)S(1)}, u32[]{:S(2)}, u32[]{:S(2)}) %all-to-all-start) | async-done | bytes 16416 | tf_op jit(solution)/shard_map/all_to_all | solution.py:351
  22.5 9.1 %held_items.1 = (bf16[4,528,256]{2,1,0:T(8,128)(2,1)S(1)}, bf16[4,528,256]{2,1,0:T(8,128)(2,1)}) custom-call(s32[1]{0:T(128)} %bitcast.1.place_ref, s32[4096]{0:T(1024)S(1)} %and_select_fusion.ids_ref, s32[1,4096]{1,0:T(1,128)S(1)} %bitcast.59, bf16[4096,256]{1,0:T(8,128)(2,1)S(1)} %bitcast.57, bf16[64,64]{1,0:T(8,128)(2,1)S(1)} %bitcast.60), custom_call_target="tpu_custom_call" | custom-call | bytes 30000000 | tf_op jit(solution)/shard_map/held_items/pallas_call | solution.py:142
  37.2 12.0 %collective-permute-done.2 = bf16[528,256]{1,0:T(8,128)(2,1)S(1)} collective-permute-done((bf16[528,256]{1,0:T(8,128)(2,1)S(1)}, bf16[528,256]{1,0:T(8,128)(2,1)S(1)}, u32[]{:S(2)}, u32[]{:S(2)}) %collective-permute-start.2) | collective-permute-done | bytes 270368 | tf_op jit(solution)/shard_map/ppermute | solution.py:297
  49.2 21.6 %pool.5.refs_0_ = bf16[4096,128]{1,0:T(8,128)(2,1)} custom-call(s32[32768]{0:T(1024)S(1)} %get-tuple-element.53.ids_ref, bf16[2,16384,128]{2,1,0:T(8,128)(2,1)} %table_ref.4), custom_call_target="tpu_custom_call" | custom-call | flops 2621440 | bytes 2000000 | tf_op jit(solution)/shard_map/pool/pallas_call | solution.py:56
  76.0 2.4 collective-permute-start.6
  78.5 14.4 %pool.6 = bf16[4096,128]{1,0:T(8,128)(2,1)} custom-call(s32[32768]{0:T(1024)S(1)} %get-tuple-element.53.ids_ref, bf16[2,16384,128]{2,1,0:T(8,128)(2,1)} %table_ref.4, bf16[4096,128]{1,0:T(8,128)(2,1)} %pool.5.refs_0_), custom_call_target="tpu_custom_call", output_to_operand_aliasing={{}: (2, {})} | custom-call | flops 1572864 | bytes 1200000 | tf_op jit(solution)/shard_map/pool/pallas_call | solution.py:56
  92.9 4.7 %collective-permute-done.5 = bf16[528,256]{1,0:T(8,128)(2,1)S(1)} collective-permute-done((bf16[528,256]{1,0:T(8,128)(2,1)S(1)}, bf16[528,256]{1,0:T(8,128)(2,1)S(1)}, u32[]{:S(2)}, u32[]{:S(2)}) %collective-permute-start.5) | collective-permute-done | bytes 270368 | tf_op jit(solution)/shard_map/ppermute | solution.py:297
  97.7 4.6 %collective-permute-start.8 = (bf16[528,256]{1,0:T(8,128)(2,1)S(1)}, bf16[528,256]{1,0:T(8,128)(2,1)S(1)}, u32[]{:S(2)}, u32[]{:S(2)}) collective-permute-start(bf16[528,256]{1,0:T(8,128)(2,1)S(1)} %add_convert_fusion.refs_5_), channel_id=1, source_target_pairs={{0,4},{1,5},{2,6},{3,7},{4,0},{5,1},{6,2},{7,3},{8,12},{9,13},{10,... | collective-permute-start | bytes 811016 | tf_op jit(solution)/shard_map/ppermute | solution.py:297
  103.2 10.3 %pool.7.refs_0_ = bf16[4096,128]{1,0:T(8,128)(2,1)S(1)} custom-call(s32[32768]{0:T(1024)S(1)} %get-tuple-element.72.ids_ref, bf16[2,16384,128]{2,1,0:T(8,128)(2,1)} %table_ref.4), custom_call_target="tpu_custom_call" | custom-call | flops 1048576 | bytes 800000 | tf_op jit(solution)/shard_map/pool/pallas_call | solution.py:56
  113.6 5.2 %all-to-all-start.1 = ((bf16[8,512,128]{2,1,0:T(8,128)(2,1)}), bf16[8,512,128]{2,1,0:T(8,128)(2,1)}, u32[]{:S(2)}, u32[]{:S(2)}) async-start(bf16[8,512,128]{2,1,0:T(8,128)(2,1)} %bitcast.24), calls=%async_computation.1 | async-start | bytes 2097152 | tf_op jit(solution)/shard_map/all_to_all | solution.py:388
  122.8 17.6 %pool.8.refs_0_ = bf16[4096,128]{1,0:T(8,128)(2,1)S(1)} custom-call(s32[32768]{0:T(1024)S(1)} %get-tuple-element.72.ids_ref, bf16[2,16384,128]{2,1,0:T(8,128)(2,1)} %table_ref.4, bf16[4096,128]{1,0:T(8,128)(2,1)S(1)} %pool.7.refs_0_), custom_call_target="tpu_custom_call", output_to_operand_aliasing={{}: (2, {})} | custom-call | flops 2097152 | bytes 1600000 | tf_op jit(solution)/shard_map/pool/pallas_call | solution.py:56
  140.5 4.8 %collective-permute-done.10.refs_7_ = bf16[528,256]{1,0:T(8,128)(2,1)S(1)} collective-permute-done((bf16[528,256]{1,0:T(8,128)(2,1)S(1)}, bf16[528,256]{1,0:T(8,128)(2,1)S(1)}, u32[]{:S(2)}, u32[]{:S(2)}) %collective-permute-start.10) | collective-permute-done | bytes 270368 | tf_op jit(solution)/shard_map/ppermute | solution.py:297
  145.2 3.1 %collective-permute-done.11.refs_11_ = bf16[528,256]{1,0:T(8,128)(2,1)S(1)} collective-permute-done((bf16[528,256]{1,0:T(8,128)(2,1)S(1)}, bf16[528,256]{1,0:T(8,128)(2,1)S(1)}, u32[]{:S(2)}, u32[]{:S(2)}) %collective-permute-start.11) | collective-permute-done | bytes 270368 | tf_op jit(solution)/shard_map/ppermute | solution.py:297
  149.9 4.6 %all-to-all-start.2 = ((bf16[8,256,128]{2,1,0:T(8,128)(2,1)}), bf16[8,256,128]{2,1,0:T(8,128)(2,1)S(1)}, u32[]{:S(2)}, u32[]{:S(2)}) async-start(bf16[8,256,128]{2,1,0:T(8,128)(2,1)} %bitcast.25), calls=%async_computation.2 | async-start | bytes 1048576 | tf_op jit(solution)/shard_map/all_to_all | solution.py:388
  156.6 10.3 %pool.9 = bf16[4096,128]{1,0:T(8,128)(2,1)S(1)} custom-call(s32[32768]{0:T(1024)S(1)} %get-tuple-element.72.ids_ref, bf16[2,16384,128]{2,1,0:T(8,128)(2,1)} %table_ref.4, bf16[4096,128]{1,0:T(8,128)(2,1)S(1)} %pool.8.refs_0_), custom_call_target="tpu_custom_call", output_to_operand_aliasing={{}: (2, {})} | custom-call | flops 1048576 | bytes 800000 | tf_op jit(solution)/shard_map/pool/pallas_call | solution.py:56
  168.6 4.1 %collective-permute-done.14.refs_12_ = bf16[528,256]{1,0:T(8,128)(2,1)} collective-permute-done((bf16[528,256]{1,0:T(8,128)(2,1)}, bf16[528,256]{1,0:T(8,128)(2,1)}, u32[]{:S(2)}, u32[]{:S(2)}) %collective-permute-start.14) | collective-permute-done | bytes 270368 | tf_op jit(solution)/shard_map/ppermute | solution.py:297
  173.7 4.5 %all-to-all-start.3 = ((bf16[8,256,128]{2,1,0:T(8,128)(2,1)}), bf16[8,256,128]{2,1,0:T(8,128)(2,1)S(1)}, u32[]{:S(2)}, u32[]{:S(2)}) async-start(bf16[8,256,128]{2,1,0:T(8,128)(2,1)} %bitcast.27), calls=%async_computation.3 | async-start | bytes 1048576 | tf_op jit(solution)/shard_map/all_to_all | solution.py:388
  178.6 12.8 %tower.2 = (bf16[8,256,256]{2,1,0:T(8,128)(2,1)}, f32[256,1]{1,0:T(8,128)S(1)}) custom-call(s32[16]{0:T(128)S(1)} %select_reduce_fusion.table_of_ref, s32[8]{0:T(128)S(1)} %convert_reduce_fusion.1.count_ref, bf16[8,512,128]{2,1,0:T(8,128)(2,1)} %all-to-all-done.1.refs_0_, bf16[8,256,128]{2,1,0:T(8,128)(2,1)} %copy-done.2, ...), custom_call_target="tpu_custom_call" | custom-call | flops 4026531840 | bytes 60000000 | tf_op jit(solution)/shard_map/tower/pallas_call | solution.py:261
  191.4 6.0 %all-to-all-start.4 = ((bf16[8,256,256]{2,1,0:T(8,128)(2,1)}), bf16[8,256,256]{2,1,0:T(8,128)(2,1)}, u32[]{:S(2)}, u32[]{:S(2)}) async-start(bf16[8,256,256]{2,1,0:T(8,128)(2,1)} %get-tuple-element.86), calls=%async_computation.4 | async-start | bytes 2097152 | tf_op jit(solution)/shard_map/all_to_all | solution.py:453
  197.4 12.8 %tower.3 = (bf16[8,256,256]{2,1,0:T(8,128)(2,1)}, f32[256,1]{1,0:T(8,128)S(1)}) custom-call(s32[16]{0:T(128)S(1)} %select_reduce_fusion.table_of_ref, s32[8]{0:T(128)S(1)} %convert_reduce_fusion.1.count_ref, bf16[8,512,128]{2,1,0:T(8,128)(2,1)} %all-to-all-done.1.refs_0_, bf16[8,256,128]{2,1,0:T(8,128)(2,1)} %copy-done.3, ...), custom_call_target="tpu_custom_call" | custom-call | flops 4026531840 | bytes 60000000 | tf_op jit(solution)/shard_map/tower/pallas_call | solution.py:261
  210.3 11.4 %all-to-all-done.4 = bf16[8,256,256]{2,1,0:T(8,128)(2,1)} async-done(((bf16[8,256,256]{2,1,0:T(8,128)(2,1)}), bf16[8,256,256]{2,1,0:T(8,128)(2,1)}, u32[]{:S(2)}, u32[]{:S(2)}) %all-to-all-start.4) | async-done | bytes 1048608 | tf_op jit(solution)/shard_map/all_to_all | solution.py:453
  221.7 3.6 %all-to-all-start.5 = ((bf16[8,256,256]{2,1,0:T(8,128)(2,1)}), bf16[8,256,256]{2,1,0:T(8,128)(2,1)S(1)}, u32[]{:S(2)}, u32[]{:S(2)}) async-start(bf16[8,256,256]{2,1,0:T(8,128)(2,1)} %get-tuple-element.89), calls=%async_computation.5 | async-start | bytes 2097152 | tf_op jit(solution)/shard_map/all_to_all | solution.py:457
  226.1 24.7 %all-to-all-done.5 = bf16[8,256,256]{2,1,0:T(8,128)(2,1)S(1)} async-done(((bf16[8,256,256]{2,1,0:T(8,128)(2,1)}), bf16[8,256,256]{2,1,0:T(8,128)(2,1)S(1)}, u32[]{:S(2)}, u32[]{:S(2)}) %all-to-all-start.5) | async-done | bytes 1048608 | tf_op jit(solution)/shard_map/all_to_all | solution.py:457
  (89 shorter events, 30.3 us)
Async XLA Ops:
  8.5 14.0 %all-to-all-start = ((s32[8,1,512]{2,1,0:T(1,128)}), s32[8,1,512]{2,1,0:T(1,128)S(1)}, u32[]{:S(2)}, u32[]{:S(2)}) async-start(s32[8,1,512]{2,1,0:T(1,128)} %broadcast_in_dim.23), calls=%async_computation | async-start | bytes 32768 | tf_op jit(solution)/shard_map/all_to_all | solution.py:351
  15.9 162.7 %all-gather.2.cloned.1.call-start = ((), (), s32[]{:S(2)}) async-start(), calls=%async_computation.6 | async-start | bytes 5242880 | tf_op jit(solution)/shard_map/all_gather | solution.py:362
  31.6 39.3 %collective-permute-start = (bf16[4,528,256]{2,1,0:T(8,128)(2,1)}, bf16[4,528,256]{2,1,0:T(8,128)(2,1)}, u32[]{:S(2)}, u32[]{:S(2)}) collective-permute-start(bf16[4,528,256]{2,1,0:T(8,128)(2,1)} %get-tuple-element.50), channel_id=1, source_target_pairs={{0,1},{1,0},{2,3},{3,2},{4,5},{5,4},{6,7},{7,6},{8,9},{9,8},{10,11... | collective-permute-start | bytes 3244040 | tf_op jit(solution)/shard_map/ppermute | solution.py:297
  35.9 13.3 %collective-permute-start.2 = (bf16[528,256]{1,0:T(8,128)(2,1)S(1)}, bf16[528,256]{1,0:T(8,128)(2,1)S(1)}, u32[]{:S(2)}, u32[]{:S(2)}) collective-permute-start(bf16[528,256]{1,0:T(8,128)(2,1)S(1)} %pad_maximum_fusion.1), channel_id=1, source_target_pairs={{0,4},{1,5},{2,6},{3,7},{4,0},{5,1},{6,2},{7,3},{8,12},{9,13},{10,... | collective-permute-start | bytes 811016 | tf_op jit(solution)/shard_map/ppermute | solution.py:297
  36.5 34.3 %collective-permute-start.1 = (bf16[528,256]{1,0:T(8,128)(2,1)S(1)}, bf16[528,256]{1,0:T(8,128)(2,1)S(1)}, u32[]{:S(2)}, u32[]{:S(2)}) collective-permute-start(bf16[528,256]{1,0:T(8,128)(2,1)S(1)} %pad_maximum_fusion.1), channel_id=1, source_target_pairs={{0,2},{1,3},{2,0},{3,1},{4,6},{5,7},{6,4},{7,5},{8,10},{9,11},{10,... | collective-permute-start | bytes 811016 | tf_op jit(solution)/shard_map/ppermute | solution.py:297
  49.2 21.7 %collective-permute-start.3 = (bf16[528,256]{1,0:T(8,128)(2,1)S(1)}, bf16[528,256]{1,0:T(8,128)(2,1)S(1)}, u32[]{:S(2)}, u32[]{:S(2)}) collective-permute-start(bf16[528,256]{1,0:T(8,128)(2,1)S(1)} %collective-permute-done.2), channel_id=1, source_target_pairs={{0,2},{1,3},{2,0},{3,1},{4,6},{5,7},{6,4},{7,5},{8,10},{9,11},{10,... | collective-permute-start | bytes 811016 | tf_op jit(solution)/shard_map/ppermute | solution.py:297
  71.0 26.6 %collective-permute-start.7 = (bf16[2112,256]{1,0:T(8,128)(2,1)S(1)}, bf16[2112,256]{1,0:T(8,128)(2,1)S(1)}, u32[]{:S(2)}, u32[]{:S(2)}) collective-permute-start(bf16[2112,256]{1,0:T(8,128)(2,1)S(1)} %constant_dynamic-update-slice_fusion.refs_13_), channel_id=1, source_target_pairs={{0,1},{1,0},{2,3},{3,2},{4,5},{5,4},{6,7},{7,6},{8,9},{9,8},{10,11... | collective-permute-start | bytes 3244040 | tf_op jit(solution)/shard_map/ppermute | solution.py:297
  73.9 19.0 %collective-permute-start.4 = (bf16[528,256]{1,0:T(8,128)(2,1)S(1)}, bf16[528,256]{1,0:T(8,128)(2,1)S(1)}, u32[]{:S(2)}, u32[]{:S(2)}) collective-permute-start(bf16[528,256]{1,0:T(8,128)(2,1)S(1)} %get-tuple-element.93), channel_id=1, source_target_pairs={{0,2},{1,3},{2,0},{3,1},{4,6},{5,7},{6,4},{7,5},{8,10},{9,11},{10,... | collective-permute-start | bytes 811016 | tf_op jit(solution)/shard_map/ppermute | solution.py:297
  76.0 21.5 %collective-permute-start.5 = (bf16[528,256]{1,0:T(8,128)(2,1)S(1)}, bf16[528,256]{1,0:T(8,128)(2,1)S(1)}, u32[]{:S(2)}, u32[]{:S(2)}) collective-permute-start(bf16[528,256]{1,0:T(8,128)(2,1)S(1)} %get-tuple-element.92), channel_id=1, source_target_pairs={{0,4},{1,5},{2,6},{3,7},{4,0},{5,1},{6,2},{7,3},{8,12},{9,13},{10,... | collective-permute-start | bytes 811016 | tf_op jit(solution)/shard_map/ppermute | solution.py:297
  76.0 21.5 %collective-permute-start.6 = (bf16[528,256]{1,0:T(8,128)(2,1)S(1)}, bf16[528,256]{1,0:T(8,128)(2,1)S(1)}, u32[]{:S(2)}, u32[]{:S(2)}) collective-permute-start(bf16[528,256]{1,0:T(8,128)(2,1)S(1)} %get-tuple-element.91), channel_id=1, source_target_pairs={{0,6},{1,7},{2,4},{3,5},{4,2},{5,3},{6,0},{7,1},{8,14},{9,15},{10,... | collective-permute-start | bytes 811016 | tf_op jit(solution)/shard_map/ppermute | solution.py:297
  97.5 16.0 %copy-start.8 = (bf16[2112,256]{1,0:T(8,128)(2,1)}, bf16[2112,256]{1,0:T(8,128)(2,1)S(1)}, u32[]{:S(2)}) copy-start(bf16[2112,256]{1,0:T(8,128)(2,1)S(1)} %collective-permute-done.7.refs_14_) | copy-start | bytes 3244036
  97.7 15.9 %collective-permute-start.8 = (bf16[528,256]{1,0:T(8,128)(2,1)S(1)}, bf16[528,256]{1,0:T(8,128)(2,1)S(1)}, u32[]{:S(2)}, u32[]{:S(2)}) collective-permute-start(bf16[528,256]{1,0:T(8,128)(2,1)S(1)} %add_convert_fusion.refs_5_), channel_id=1, source_target_pairs={{0,4},{1,5},{2,6},{3,7},{4,0},{5,1},{6,2},{7,3},{8,12},{9,13},{10,... | collective-permute-start | bytes 811016 | tf_op jit(solution)/shard_map/ppermute | solution.py:297
  102.3 11.3 %collective-permute-start.9 = (bf16[528,256]{1,0:T(8,128)(2,1)S(1)}, bf16[528,256]{1,0:T(8,128)(2,1)S(1)}, u32[]{:S(2)}, u32[]{:S(2)}) collective-permute-start(bf16[528,256]{1,0:T(8,128)(2,1)S(1)} %add_convert_fusion.refs_5_), channel_id=1, source_target_pairs={{0,1},{1,0},{2,3},{3,2},{4,5},{5,4},{6,7},{7,6},{8,9},{9,8},{10,11... | collective-permute-start | bytes 811016 | tf_op jit(solution)/shard_map/ppermute | solution.py:297
  113.6 35.5 %all-to-all-start.1 = ((bf16[8,512,128]{2,1,0:T(8,128)(2,1)}), bf16[8,512,128]{2,1,0:T(8,128)(2,1)}, u32[]{:S(2)}, u32[]{:S(2)}) async-start(bf16[8,512,128]{2,1,0:T(8,128)(2,1)} %bitcast.24), calls=%async_computation.1 | async-start | bytes 2097152 | tf_op jit(solution)/shard_map/all_to_all | solution.py:388
  118.8 26.5 %collective-permute-start.10 = (bf16[528,256]{1,0:T(8,128)(2,1)S(1)}, bf16[528,256]{1,0:T(8,128)(2,1)S(1)}, u32[]{:S(2)}, u32[]{:S(2)}) collective-permute-start(bf16[528,256]{1,0:T(8,128)(2,1)S(1)} %add_convert_fusion.refs_5_), channel_id=1, source_target_pairs={{0,2},{1,3},{2,0},{3,1},{4,6},{5,7},{6,4},{7,5},{8,10},{9,11},{10,... | collective-permute-start | bytes 811016 | tf_op jit(solution)/shard_map/ppermute | solution.py:297
  120.8 27.5 %collective-permute-start.11 = (bf16[528,256]{1,0:T(8,128)(2,1)S(1)}, bf16[528,256]{1,0:T(8,128)(2,1)S(1)}, u32[]{:S(2)}, u32[]{:S(2)}) collective-permute-start(bf16[528,256]{1,0:T(8,128)(2,1)S(1)} %collective-permute-done.8.refs_9_), channel_id=1, source_target_pairs={{0,2},{1,3},{2,0},{3,1},{4,6},{5,7},{6,4},{7,5},{8,10},{9,11},{10,... | collective-permute-start | bytes 811016 | tf_op jit(solution)/shard_map/ppermute | solution.py:297
  120.8 28.2 %collective-permute-start.12 = (bf16[528,256]{1,0:T(8,128)(2,1)S(1)}, bf16[528,256]{1,0:T(8,128)(2,1)S(1)}, u32[]{:S(2)}, u32[]{:S(2)}) collective-permute-start(bf16[528,256]{1,0:T(8,128)(2,1)S(1)} %collective-permute-done.8.refs_9_), channel_id=1, source_target_pairs={{0,1},{1,0},{2,3},{3,2},{4,5},{5,4},{6,7},{7,6},{8,9},{9,8},{10,11... | collective-permute-start | bytes 811016 | tf_op jit(solution)/shard_map/ppermute | solution.py:297
  149.9 22.9 %all-to-all-start.2 = ((bf16[8,256,128]{2,1,0:T(8,128)(2,1)}), bf16[8,256,128]{2,1,0:T(8,128)(2,1)S(1)}, u32[]{:S(2)}, u32[]{:S(2)}) async-start(bf16[8,256,128]{2,1,0:T(8,128)(2,1)} %bitcast.25), calls=%async_computation.2 | async-start | bytes 1048576 | tf_op jit(solution)/shard_map/all_to_all | solution.py:388
  154.5 14.1 %collective-permute-start.13 = (bf16[528,256]{1,0:T(8,128)(2,1)S(1)}, bf16[528,256]{1,0:T(8,128)(2,1)S(1)}, u32[]{:S(2)}, u32[]{:S(2)}) collective-permute-start(bf16[528,256]{1,0:T(8,128)(2,1)S(1)} %collective-permute-done.10.refs_7_), channel_id=1, source_target_pairs={{0,1},{1,0},{2,3},{3,2},{4,5},{5,4},{6,7},{7,6},{8,9},{9,8},{10,11... | collective-permute-start | bytes 811016 | tf_op jit(solution)/shard_map/ppermute | solution.py:297
  156.6 16.2 %collective-permute-start.14 = (bf16[528,256]{1,0:T(8,128)(2,1)}, bf16[528,256]{1,0:T(8,128)(2,1)}, u32[]{:S(2)}, u32[]{:S(2)}) collective-permute-start(bf16[528,256]{1,0:T(8,128)(2,1)} %copy-done.9), channel_id=1, source_target_pairs={{0,1},{1,0},{2,3},{3,2},{4,5},{5,4},{6,7},{7,6},{8,9},{9,8},{10,11... | collective-permute-start | bytes 811016 | tf_op jit(solution)/shard_map/ppermute | solution.py:297
  166.9 11.7 %copy-start.1 = (f32[1024]{0:T(1024)S(1)}, f32[1024]{0:T(1024)}, u32[]{:S(2)}) copy-start(f32[1024]{0:T(1024)} %param.17) | copy-start | bytes 12292
  173.7 17.7 %all-to-all-start.3 = ((bf16[8,256,128]{2,1,0:T(8,128)(2,1)}), bf16[8,256,128]{2,1,0:T(8,128)(2,1)S(1)}, u32[]{:S(2)}, u32[]{:S(2)}) async-start(bf16[8,256,128]{2,1,0:T(8,128)(2,1)} %bitcast.27), calls=%async_computation.3 | async-start | bytes 1048576 | tf_op jit(solution)/shard_map/all_to_all | solution.py:388
  191.4 30.2 %all-to-all-start.4 = ((bf16[8,256,256]{2,1,0:T(8,128)(2,1)}), bf16[8,256,256]{2,1,0:T(8,128)(2,1)}, u32[]{:S(2)}, u32[]{:S(2)}) async-start(bf16[8,256,256]{2,1,0:T(8,128)(2,1)} %get-tuple-element.86), calls=%async_computation.4 | async-start | bytes 2097152 | tf_op jit(solution)/shard_map/all_to_all | solution.py:453
  221.7 29.1 %all-to-all-start.5 = ((bf16[8,256,256]{2,1,0:T(8,128)(2,1)}), bf16[8,256,256]{2,1,0:T(8,128)(2,1)S(1)}, u32[]{:S(2)}, u32[]{:S(2)}) async-start(bf16[8,256,256]{2,1,0:T(8,128)(2,1)} %get-tuple-element.89), calls=%async_computation.5 | async-start | bytes 2097152 | tf_op jit(solution)/shard_map/all_to_all | solution.py:457
  (10 other events, 65.7 us)
Sparse Core Ops, SparseCore 0:
  18.3 35.9 all-gather.1

commit v3 on v2

--- a/solution.py
+++ b/solution.py
@@ -78,8 +78,8 @@
     )(ids, tables, *more)
 
 
-def items_kernel(users, place_ref, ids_ref, row_ref, bank_ref, lq_ref, *refs):
-    *out_refs, low, high, part_low, part_high = refs
+def items_kernel(users, ids_ref, row_ref, bank_ref, lq_ref, *refs):
+    out_ref, low, high, part_low, part_high = refs
     count = ids_ref.shape[0]
     owned, width = bank_ref.shape
     items, blocks = lq_ref.shape
@@ -97,53 +97,49 @@
     low[pl.ds(owned, 8), :] = jnp.zeros((8, LANES), jnp.float32)
     high[pl.ds(owned, 8), :] = jnp.zeros((8, LANES), jnp.float32)
     per = users // step
-    held = users + LQ_ROWS
-    me = place_ref[0]
-    for p, out_ref in enumerate(out_refs):
-        def part(c, carry):
-            block = c // per
-            start = (me ^ (2 * block + p)) * users + (c % per) * step
-
-            def group(g, inner):
-                base = pl.multiple_of(g * unroll, unroll)
-                for j in range(unroll):
-                    at = ids_ref[start + base + j]
-                    part_low[pl.ds(base + j, 1), :] = low[pl.ds(at, 1), :]
-                    part_high[pl.ds(base + j, 1), :] = high[pl.ds(at, 1), :]
-                return inner
-
-            lax.fori_loop(0, step // unroll, group, 0)
-            at = pl.ds(pl.multiple_of((c % per) * step, 16), step)
-            out_ref[block, at, :] = jnp.concatenate([part_low[...], part_high[...]], axis=1).astype(jnp.bfloat16)
-            return carry
-
-        lax.fori_loop(0, count // step // 2, part, 0)
-        for block in range(out_ref.shape[0]):
-            lines = []
-            for c in range(per):
-                at = pl.multiple_of((me ^ (2 * block + p)) * users + c * step, step)
-                ids = row_ref[:, pl.ds(at, step)]
-                spot = lax.broadcasted_iota(jnp.int32, (blocks, step), 0)
-                shift = jnp.int32(items.bit_length() - 1)
-                one_hot = jnp.where(spot == lax.shift_right_arithmetic(ids, shift), 1.0, 0.0)
-                by_item = jnp.dot(lq_ref[...], one_hot.astype(jnp.bfloat16), preferred_element_type=jnp.float32)
-                spot = lax.broadcasted_iota(jnp.int32, (items, step), 0)
-                kept = jnp.where(spot == (ids & (items - 1)), by_item, 0.0)
-                lines.append(jnp.sum(kept, axis=0, keepdims=True))
-            lines.append(jnp.zeros((LQ_ROWS - per, step), jnp.float32))
-            out_ref[block, pl.ds(users, LQ_ROWS), :] = jnp.concatenate(lines, axis=0).astype(jnp.bfloat16)
-
-
-def held_items(place, ids, users, bank, log_q):
+
+    def part(c, carry):
+        start = c * step
+
+        def group(g, inner):
+            base = pl.multiple_of(g * unroll, unroll)
+            for j in range(unroll):
+                at = ids_ref[start + base + j]
+                part_low[pl.ds(base + j, 1), :] = low[pl.ds(at, 1), :]
+                part_high[pl.ds(base + j, 1), :] = high[pl.ds(at, 1), :]
+            return inner
+
+        lax.fori_loop(0, step // unroll, group, 0)
+        at = pl.ds(pl.multiple_of((c % per) * step, 16), step)
+        out_ref[c // per, at, :] = jnp.concatenate([part_low[...], part_high[...]], axis=1).astype(jnp.bfloat16)
+        return carry
+
+    lax.fori_loop(0, count // step, part, 0)
+    for block in range(count // users):
+        lines = []
+        for c in range(per):
+            ids = row_ref[:, pl.ds(block * users + c * step, step)]
+            spot = lax.broadcasted_iota(jnp.int32, (blocks, step), 0)
+            shift = jnp.int32(items.bit_length() - 1)
+            one_hot = jnp.where(spot == lax.shift_right_arithmetic(ids, shift), 1.0, 0.0)
+            by_item = jnp.dot(lq_ref[...], one_hot.astype(jnp.bfloat16), preferred_element_type=jnp.float32)
+            spot = lax.broadcasted_iota(jnp.int32, (items, step), 0)
+            kept = jnp.where(spot == (ids & (items - 1)), by_item, 0.0)
+            lines.append(jnp.sum(kept, axis=0, keepdims=True))
+        lines.append(jnp.zeros((LQ_ROWS - per, step), jnp.float32))
+        out_ref[block, pl.ds(users, LQ_ROWS), :] = jnp.concatenate(lines, axis=0).astype(jnp.bfloat16)
+
+
+def held_items(ids, users, bank, log_q):
     count = ids.shape[0]
     owned, width = bank.shape
     held = (ids >= 0) & (ids < owned)
-    out = jax.ShapeDtypeStruct((count // users // 2, users + LQ_ROWS, width), jnp.bfloat16)
+    out = jax.ShapeDtypeStruct((count // users, users + LQ_ROWS, width), jnp.bfloat16)
     return pl.pallas_call(
         functools.partial(items_kernel, users),
-        in_specs=[pl.BlockSpec(memory_space=pltpu.SMEM)] * 2 + [pl.BlockSpec(memory_space=pltpu.VMEM)] * 3,
-        out_specs=[pl.BlockSpec(memory_space=pltpu.VMEM)] * 2,
-        out_shape=[out, out],
+        in_specs=[pl.BlockSpec(memory_space=pltpu.SMEM)] + [pl.BlockSpec(memory_space=pltpu.VMEM)] * 3,
+        out_specs=pl.BlockSpec(memory_space=pltpu.VMEM),
+        out_shape=out,
         scratch_shapes=[
             pltpu.VMEM((owned + 8, LANES), jnp.float32),
             pltpu.VMEM((owned + 8, LANES), jnp.float32),
@@ -153,40 +149,42 @@
         compiler_params=pltpu.CompilerParams(vmem_limit_bytes=ITEM_BYTES),
         cost_estimate=pl.CostEstimate(flops=0, bytes_accessed=30_000_000, transcendentals=0),
         name="held_items",
-    )(place, jnp.where(held, ids, owned), ids[None, :], bank, log_q.T)
-
-
-def tower_kernel(scale, lead, n_x, table_of_ref, count_ref, *refs):
+    )(jnp.where(held, ids, owned), ids[None, :], bank, log_q.T)
+
+
+def tower_kernel(scale, lead, n_x, n_w, n_noise, table_of_ref, count_ref, shard_ref, *refs):
     x_refs, refs = refs[:n_x], refs[n_x:]
     owners, users, emb = x_refs[0].shape
-    w_first_ref, b_ref, w2_ref, *refs = refs
+    w_refs, refs = refs[:n_w], refs[n_w:]
+    b_ref, w2_ref, *refs = refs
     pos_refs, refs = refs[:owners], refs[owners:]
-    noise_refs, refs = refs[:2], refs[2:]
+    noise_refs, refs = refs[:n_noise], refs[n_noise:]
     grad_ref, loss_ref, w_ref, pre_ref, score_ref, noise_vec, noise_lq, picked_lq, w_sem = refs
     depth = n_x * emb
     held, width = pos_refs[0].shape
     batch_users = held - LQ_ROWS
-    most = 2 * noise_refs[0].shape[0] // owners - LQ_ROWS
-    items = most // MOST
     nnoise = noise_vec.shape[0]
-
-    def place(slot, table):
+    items = nnoise // picked_lq.shape[0]
+    most = MOST * items
+
+    def place(o, i, table):
         return pltpu.make_async_copy(
-            w_first_ref.at[pl.ds(slot * emb, emb), :],
+            w_refs[o].at[pl.ds(i * emb, emb), :],
             w_ref.at[pl.ds(pl.multiple_of(table * emb, emb), emb), :],
             w_sem.at[table],
         )
 
-    for slot in range(w_first_ref.shape[0] // emb):
-        place(slot, table_of_ref[slot]).start()
+    per = w_refs[0].shape[0] // emb
+    for o in range(n_w):
+        for i in range(per):
+            place(o, i, table_of_ref[(shard_ref[0] ^ o) * per + i]).start()
     filled = jnp.int32(0)
-    for o in range(owners):
-        noise_ref = noise_refs[o // (owners // 2)]
-        begin = o % (owners // 2) * (most + LQ_ROWS)
+    step = most + LQ_ROWS
+    for o, (noise_ref, begin) in enumerate((r, c) for r in noise_refs for c in range(0, r.shape[0], step)):
         noise_lq[...] = noise_ref[pl.ds(begin + most, LQ_ROWS), :LANES].astype(jnp.float32)
         used = count_ref[o]
 
-        def fill(k, carry):
+        def fill(k, carry, noise_ref=noise_ref, begin=begin, filled=filled):
             n = filled + k
             start = pl.multiple_of(begin + k * items, 16)
             noise_vec[pl.ds(pl.multiple_of(n * items, items), items), :] = noise_ref[pl.ds(start, items), :]
@@ -202,7 +200,7 @@
     for s in range(owners):
         x = jnp.concatenate([r[s] for r in x_refs], axis=1)
         for table in range(s * n_x, (s + 1) * n_x):
-            place(0, table).wait()
+            place(0, 0, table).wait()
         pre = pre + jnp.dot(x, weight(s), preferred_element_type=jnp.float32)
     pre_ref[...] = pre
     hidden = (pre * jax.nn.sigmoid(pre)).astype(jnp.bfloat16)
@@ -248,7 +246,7 @@
         ).astype(jnp.bfloat16)
 
 
-def tower(lead, users, table_of, counts, xs, w, b, w2, pos, noise, n_noise):
+def tower(lead, users, table_of, counts, shard, xs, ws, b, w2, pos, noise, n_noise, n_picked):
     owners, _, emb = xs[0][0].shape
     per_owner = len(xs)
     hid, width = w2.shape
@@ -259,13 +257,13 @@
     flops = 2 * users * (2 * depth * hid + 2 * hid * width + 2 * candidates * width)
     wide = per_owner * emb
     return pl.pallas_call(
-        functools.partial(tower_kernel, width ** (-0.5), lead, per_owner),
+        functools.partial(tower_kernel, width ** (-0.5), lead, per_owner, len(ws), len(noise)),
         grid=(1,),
-        in_specs=[smem] * 2
+        in_specs=[smem] * 3
         + [
             pl.BlockSpec((owners, users, emb), lambda i, at=at: (0, at, 0), pipeline_mode=once) for _, at in xs
         ]
-        + [pl.BlockSpec(memory_space=pl.ANY)]
+        + [pl.BlockSpec(memory_space=pl.ANY)] * len(ws)
         + [pl.BlockSpec(a.shape, lambda i: (0, 0), pipeline_mode=once) for a in (b, w2, *pos, *noise)],
         out_specs=[
             pl.BlockSpec((owners, users, wide), lambda i: (0, 0, 0)),
@@ -281,7 +279,7 @@
             pltpu.VMEM((users, candidates), jnp.float32),
             pltpu.VMEM((n_noise, width), jnp.bfloat16),
             pltpu.VMEM((LQ_ROWS, LANES), jnp.float32),
-            pltpu.VMEM((n_noise * MOST // (2 * noise[0].shape[0] // owners - LQ_ROWS), LANES), jnp.float32),
+            pltpu.VMEM((n_picked, LANES), jnp.float32),
             pltpu.SemaphoreType.DMA((depth // emb,)),
         ],
         compiler_params=pltpu.CompilerParams(vmem_limit_bytes=VMEM_BYTES),
@@ -289,7 +287,7 @@
             flops=flops, bytes_accessed=60_000_000, transcendentals=users * candidates
         ),
         name="tower",
-    )(table_of, counts, *(x for x, _ in xs), w, b, w2, *pos, *noise)
+    )(table_of, counts, shard, *(x for x, _ in xs), *ws, b, w2, *pos, *noise)
 
 
 def swap(x, axis, offset):
@@ -345,7 +343,7 @@
     blocks_dev, block_items, width = bank.shape
     users = row_users // owners
 
-    place = me.astype(jnp.int32)[None]
+    shard = lax.axis_index("batch").astype(jnp.int32)[None]
 
     copies = jnp.broadcast_to(pos_items[None, :], (owners, users))
     item_ids = lax.all_to_all(copies, "table", split_axis=0, concat_axis=0, tiled=True).reshape(-1)
@@ -359,11 +357,13 @@
     local_block = jnp.sum(pick * (sample - me * blocks_dev)[None, :], axis=1)
     noise_lq = jnp.pad(log_q[local_block], ((0, LQ_ROWS - MOST), (0, width - block_items)))
     my_noise = jnp.concatenate([bank[local_block].reshape(MOST * block_items, width), noise_lq], axis=0)
-    w_whole = lax.all_gather(w_first, "batch", axis=0, tiled=True)
+    item_ids, my_noise, w_part = tie(item_ids, my_noise, w_first)
+    w_rounds = Spread(w_part, "batch")
+    w_got = w_rounds.send()
     near_noise, noise_from, offset = [my_noise], [0], owners // 2
     noise_got = [swap(my_noise, "table", offset)]
     owned = blocks_dev * block_items
-    same, other = held_items(place, item_ids - me * owned, users, bank.reshape(owned, width), log_q)
+    mine = held_items(item_ids - me * owned, users, bank.reshape(owned, width), log_q)
 
     by_table = jnp.transpose(feature_ids, (1, 2, 0))
     used = jnp.arange(bag, dtype=jnp.int32)[None, :, None] < jnp.transpose(bag_lengths, (1, 0))[:, None, :]
@@ -387,40 +387,31 @@
         pooled = pooled.reshape(owners, -1, emb)
         return lax.all_to_all(pooled, "table", split_axis=0, concat_axis=0, tiled=True)
 
-    def both(a, b):
-        return (a.astype(jnp.float32) + b.astype(jnp.float32)).astype(jnp.bfloat16)
-
-    same, other, tables, *ids = tie(same, other, tables, *ids)
+    mine, tables, noise_got, *ids = tie(mine, tables, noise_got, *ids)
 
     def more_noise():
         near_noise.extend(noise_got)
         noise_from.extend([o ^ offset for o in noise_from])
 
-    near = swap(other, "table", 1)
+    mine = lax.all_to_all(mine, "table", split_axis=0, concat_axis=0, tiled=True)
     while offset > 2:
         more_noise()
         offset //= 2
         noise_got = [swap(v, "table", offset) for v in near_noise]
-    cut = blocks * 5 // 8
-    pooled = pool(ids[0], tables, 0, bag, straight, 0, cut, blocks, None)
-    pooled, near, noise_got, *ids = tie(pooled, near, noise_got, *ids)
-    more_noise()
-    near_noise = jnp.concatenate(near_noise, axis=0)
-    far_noise = swap(near_noise, "table", 1)
-    sums = [both(same[q], near[q]) for q in range(owners // 2)]
-    far = [swap(sums[q], "table", 2 * q) for q in range(1, owners // 2)]
-    pooled = pool(ids[0], tables, 0, bag, straight, cut, blocks, blocks, pooled)
+    first_noise = swap(jnp.concatenate(near_noise, axis=0), "table", 1)
+    pooled = pool(ids[0], tables, 0, bag, straight, 0, blocks, blocks, None)
     whole = [pooled]
     for j in range(1, per_owner - 1):
         tables, pooled = tie(tables, pooled)
         pooled = pool(ids[j], tables, j, bag, straight, 0, blocks, blocks, None)
         whole.append(pooled)
 
-    tables, whole, far, sums, far_noise = tie(tables, whole, far, sums, far_noise)
-    own_pos = sums[0].astype(jnp.float32)
-    for block in far:
-        own_pos = own_pos + block.astype(jnp.float32)
-    own_pos = own_pos.astype(jnp.bfloat16)
+    tables, whole, mine, noise_got, first_noise, w_got = tie(tables, whole, mine, noise_got, first_noise, w_got)
+    w_got = w_rounds.send(w_got)
+    more_noise()
+    far_noise = swap(jnp.concatenate(noise_got, axis=0), "table", 1)
+    near_noise = jnp.concatenate(near_noise, axis=0)
+    own_pos = jnp.sum(mine.astype(jnp.float32), axis=0).astype(jnp.bfloat16)
     own_pos, tables = tie(own_pos, tables)
     pos_rounds = Spread(own_pos, "table")
     got = pos_rounds.send()
@@ -429,7 +420,7 @@
     final = functools.partial(pool, tables=tables, table=per_owner - 1, bag=bag, order=halves, blocks=blocks)
     cut = blocks // 4
     pooled = final(ids=last, first=0, last=cut, given=None)
-    pooled, whole, got, last = tie(pooled, whole, got, last)
+    pooled, whole, got, far_noise, last = tie(pooled, whole, got, far_noise, last)
     xs = [exchange(v) for v in whole]
     got = pos_rounds.send(got)
     pooled = final(ids=last, first=cut, last=blocks - cut, given=pooled)
@@ -440,14 +431,15 @@
     pooled, early, got = tie(pooled, early, got)
     late = exchange(pooled[row_users // 2 :])
     pos = pos_rounds.finish(got)
+    ws = w_rounds.finish(w_got)
 
     slots = jnp.arange(feature_slot.shape[0], dtype=jnp.int32)
     table_of = jnp.sum(jnp.where(feature_slot[None, :] == slots[:, None], slots[None, :], 0), axis=1)
     noise_owner = me ^ jnp.asarray(noise_from + [o ^ 1 for o in noise_from], jnp.int32)
     counts = jnp.sum((owner_of[None, :] == noise_owner[:, None]).astype(jnp.int32), axis=1)
     run = functools.partial(
-        tower, users=users // 2, table_of=table_of, counts=counts, w=w_whole, b=b_first[None, :], w2=w_second, pos=pos,
-        noise=[near_noise, far_noise], n_noise=sample.shape[0] * block_items,
+        tower, users=users // 2, table_of=table_of, counts=counts, shard=shard, ws=ws, b=b_first[None, :], w2=w_second, pos=pos,
+        noise=[near_noise, first_noise, far_noise], n_noise=sample.shape[0] * block_items, n_picked=sample.shape[0],
     )
     grad_early, loss_early = run(lead=0, xs=[(v, 0) for v in xs] + [(early, 0)])
     back = [lax.all_to_all(grad_early, "table", split_axis=0, concat_axis=0, tiled=True)]

time: 262 us -> 250 us (0.954)
  between operations: 14.4 us -> 0.98 us
  starting transfers between devices: 50.8 us -> 57.1 us
  waiting for transfers between devices: 71.5 us -> 65.4 us
  Pallas kernels: 109 us -> 106 us
  local copies, waits for them, and re-layouts: 8.88 us -> 11.7 us
    all_to_all x0 -> x1, starting transfers between devices: none -> 5.85 us  [on_device(): lax.all_to_all(mine, 'table', split_axis=0, concat_axis=0, tiled=True)]
    all_to_all x1, waiting for transfers between devices: 4.26 us -> 0.21 us  [on_device(): lax.all_to_all(copies, 'table', split_axis=0, concat_axis=0, tiled=True)]
    pallas_call x5 -> x4, Pallas kernels: 74.3 us -> 70.8 us  [pool(): pl.pallas_call(functools.partial(pool_kernel, bag), grid=(last - first,),...]
    ppermute x15, waiting for transfers between devices: 30.3 us -> 27.3 us  [swap(): return lax.ppermute(x, axis, [(i, i ^ offset) for i in range(size)])]
  transfers between devices with their start and end apart: 22 -> 22, of which waited for: 9 -> 14; matrix products, arithmetic and copies ran while one was open for 4% -> 4% of each run, Pallas kernels for 42% -> 42%
where the time goes in v3:
time: 250 us; the launch traced here: 249 us
  Pallas kernels  106 us (42%)
  waiting for transfers between devices  65.4 us (26%)
  starting transfers between devices  57.1 us (23%)
  local copies, waits for them, and re-layouts  11.7 us (5%)
  other arithmetic  8.09 us (3%)
    pallas_call x4, Pallas kernels, pool(): pl.pallas_call(functools.partial(pool_kernel, bag), grid=(last - first,),...  70.8 us
    ppermute x15, waiting for transfers between devices, swap(): return lax.ppermute(x, axis, [(i, i ^ offset) for i in range(size)])  27.3 us
    pallas_call x2, Pallas kernels, tower(): pl.pallas_call(functools.partial(tower_kernel, width ** (-0.5), lead, per...  25.5 us
    all_to_all x1, waiting for transfers between devices, on_device(): lax.all_to_all(grad_late, 'table', split_axis=0, concat_axis=0, tiled=True)  24.9 us
    ppermute x15, starting transfers between devices, swap(): return lax.ppermute(x, axis, [(i, i ^ offset) for i in range(size)])  20.1 us
    all_to_all x3, starting transfers between devices, exchange(): lax.all_to_all(pooled, 'table', split_axis=0, concat_axis=0, tiled=True)  14.5 us
    all_to_all x1, waiting for transfers between devices, on_device(): lax.all_to_all(grad_early, 'table', split_axis=0, concat_axis=0, tiled=True)  12.6 us
    pallas_call x1, Pallas kernels, held_items(): pl.pallas_call(functools.partial(items_kernel, users), in_specs=[pl.Block...  9.24 us
  transfers between devices with their start and end apart: 22, of which 14 were waited for; matrix products, arithmetic and copies ran while one was open for 4% of the time, Pallas kernels for 42%

profile of v3, /device:TPU:0, one launch (start us, length us, event | category | flops | bytes accessed | tf_op | source)
XLA Modules:
  0.0 248.8 jit_solution(12803112738196912759)
XLA Ops:
  1.9 7.3 %all-to-all-start = ((s32[8,1,512]{2,1,0:T(1,128)}), s32[8,1,512]{2,1,0:T(1,128)S(1)}, u32[]{:S(2)}, u32[]{:S(2)}) async-start(s32[8,1,512]{2,1,0:T(1,128)} %broadcast_in_dim.25), calls=%async_computation | async-start | bytes 32768 | tf_op jit(solution)/shard_map/all_to_all | solution.py:349
  15.8 2.8 %collective-permute-start = (bf16[528,256]{1,0:T(8,128)(2,1)S(1)}, bf16[528,256]{1,0:T(8,128)(2,1)S(1)}, u32[]{:S(2)}, u32[]{:S(2)}) collective-permute-start(bf16[528,256]{1,0:T(8,128)(2,1)S(1)} %fusion.1), channel_id=1, source_target_pairs={{0,4},{1,5},{2,6},{3,7},{4,0},{5,1},{6,2},{7,3},{8,12},{9,13},{10,... | collective-permute-start | bytes 811016 | tf_op jit(solution)/shard_map/ppermute | solution.py:295
  18.7 9.2 %held_items.1 = bf16[8,528,256]{2,1,0:T(8,128)(2,1)} custom-call(s32[4096]{0:T(1024)S(1)} %get-tuple-element.84.ids_ref, s32[1,4096]{1,0:T(1,128)S(1)} %bitcast.48, bf16[4096,256]{1,0:T(8,128)(2,1)S(1)} %bitcast.47, bf16[64,64]{1,0:T(8,128)(2,1)S(1)} %bitcast.49), custom_call_target="tpu_custom_call" | custom-call | bytes 30000000 | tf_op jit(solution)/shard_map/held_items/pallas_call | solution.py:138
  27.9 2.3 collective-permute-done
  30.3 5.8 %all-to-all-start.1 = ((bf16[8,528,256]{2,1,0:T(8,128)(2,1)}), bf16[8,528,256]{2,1,0:T(8,128)(2,1)}, u32[]{:S(2)}, u32[]{:S(2)}) async-start(bf16[8,528,256]{2,1,0:T(8,128)(2,1)} %held_items.1), calls=%async_computation.1 | async-start | bytes 4325376 | tf_op jit(solution)/shard_map/all_to_all | solution.py:396
  41.8 32.5 %pool.4 = bf16[4096,128]{1,0:T(8,128)(2,1)} custom-call(s32[32768]{0:T(1024)S(1)} %get-tuple-element.47.ids_ref, bf16[2,16384,128]{2,1,0:T(8,128)(2,1)} %table_ref.3), custom_call_target="tpu_custom_call" | custom-call | flops 4194304 | bytes 3200000 | tf_op jit(solution)/shard_map/pool/pallas_call | solution.py:56
  74.3 4.9 %collective-permute-done.1 = bf16[528,256]{1,0:T(8,128)(2,1)S(1)} collective-permute-done((bf16[528,256]{1,0:T(8,128)(2,1)S(1)}, bf16[528,256]{1,0:T(8,128)(2,1)S(1)}, u32[]{:S(2)}, u32[]{:S(2)}) %collective-permute-start.1) | collective-permute-done | bytes 270368 | tf_op jit(solution)/shard_map/ppermute | solution.py:295
  79.1 4.9 %collective-permute-done.2 = bf16[528,256]{1,0:T(8,128)(2,1)S(1)} collective-permute-done((bf16[528,256]{1,0:T(8,128)(2,1)S(1)}, bf16[528,256]{1,0:T(8,128)(2,1)S(1)}, u32[]{:S(2)}, u32[]{:S(2)}) %collective-permute-start.2) | collective-permute-done | bytes 270368 | tf_op jit(solution)/shard_map/ppermute | solution.py:295
  90.4 3.4 %collective-permute-start.6 = (bf16[528,256]{1,0:T(8,128)(2,1)S(1)}, bf16[528,256]{1,0:T(8,128)(2,1)S(1)}, u32[]{:S(2)}, u32[]{:S(2)}) collective-permute-start(bf16[528,256]{1,0:T(8,128)(2,1)S(1)} %reduce_sum.58.refs_8_), channel_id=1, source_target_pairs={{0,4},{1,5},{2,6},{3,7},{4,0},{5,1},{6,2},{7,3},{8,12},{9,13},{10,... | collective-permute-start | bytes 811016 | tf_op jit(solution)/shard_map/ppermute | solution.py:295
  94.4 10.3 %pool.5.refs_0_ = bf16[4096,128]{1,0:T(8,128)(2,1)S(1)} custom-call(s32[32768]{0:T(1024)S(1)} %get-tuple-element.63.ids_ref, bf16[2,16384,128]{2,1,0:T(8,128)(2,1)} %table_ref.3), custom_call_target="tpu_custom_call" | custom-call | flops 1048576 | bytes 800000 | tf_op jit(solution)/shard_map/pool/pallas_call | solution.py:56
  106.1 5.4 %all-to-all-start.2 = ((bf16[8,512,128]{2,1,0:T(8,128)(2,1)}), bf16[8,512,128]{2,1,0:T(8,128)(2,1)}, u32[]{:S(2)}, u32[]{:S(2)}) async-start(bf16[8,512,128]{2,1,0:T(8,128)(2,1)} %bitcast.20), calls=%async_computation.2 | async-start | bytes 2097152 | tf_op jit(solution)/shard_map/all_to_all | solution.py:388
  115.6 17.6 %pool.6.refs_0_ = bf16[4096,128]{1,0:T(8,128)(2,1)S(1)} custom-call(s32[32768]{0:T(1024)S(1)} %get-tuple-element.63.ids_ref, bf16[2,16384,128]{2,1,0:T(8,128)(2,1)} %table_ref.3, bf16[4096,128]{1,0:T(8,128)(2,1)S(1)} %pool.5.refs_0_), custom_call_target="tpu_custom_call", output_to_operand_aliasing={{}: (2, {})} | custom-call | flops 2097152 | bytes 1600000 | tf_op jit(solution)/shard_map/pool/pallas_call | solution.py:56
  133.2 4.6 %collective-permute-done.9.refs_10_ = bf16[528,256]{1,0:T(8,128)(2,1)S(1)} collective-permute-done((bf16[528,256]{1,0:T(8,128)(2,1)S(1)}, bf16[528,256]{1,0:T(8,128)(2,1)S(1)}, u32[]{:S(2)}, u32[]{:S(2)}) %collective-permute-start.9) | collective-permute-done | bytes 270368 | tf_op jit(solution)/shard_map/ppermute | solution.py:295
  137.8 2.9 %collective-permute-done.10.refs_14_ = bf16[528,256]{1,0:T(8,128)(2,1)S(1)} collective-permute-done((bf16[528,256]{1,0:T(8,128)(2,1)S(1)}, bf16[528,256]{1,0:T(8,128)(2,1)S(1)}, u32[]{:S(2)}, u32[]{:S(2)}) %collective-permute-start.10) | collective-permute-done | bytes 270368 | tf_op jit(solution)/shard_map/ppermute | solution.py:295
  141.6 4.6 %all-to-all-start.3 = ((bf16[8,256,128]{2,1,0:T(8,128)(2,1)}), bf16[8,256,128]{2,1,0:T(8,128)(2,1)}, u32[]{:S(2)}, u32[]{:S(2)}) async-start(bf16[8,256,128]{2,1,0:T(8,128)(2,1)} %bitcast.52), calls=%async_computation.3 | async-start | bytes 1048576 | tf_op jit(solution)/shard_map/all_to_all | solution.py:388
  148.6 10.3 %pool.7 = bf16[4096,128]{1,0:T(8,128)(2,1)S(1)} custom-call(s32[32768]{0:T(1024)S(1)} %get-tuple-element.63.ids_ref, bf16[2,16384,128]{2,1,0:T(8,128)(2,1)} %table_ref.3, bf16[4096,128]{1,0:T(8,128)(2,1)S(1)} %pool.6.refs_0_), custom_call_target="tpu_custom_call", output_to_operand_aliasing={{}: (2, {})} | custom-call | flops 1048576 | bytes 800000 | tf_op jit(solution)/shard_map/pool/pallas_call | solution.py:56
  160.2 5.2 %collective-permute-done.13.refs_15_ = bf16[528,256]{1,0:T(8,128)(2,1)} collective-permute-done((bf16[528,256]{1,0:T(8,128)(2,1)}, bf16[528,256]{1,0:T(8,128)(2,1)}, u32[]{:S(2)}, u32[]{:S(2)}) %collective-permute-start.13) | collective-permute-done | bytes 270368 | tf_op jit(solution)/shard_map/ppermute | solution.py:295
  166.2 4.5 %all-to-all-start.4 = ((bf16[8,256,128]{2,1,0:T(8,128)(2,1)}), bf16[8,256,128]{2,1,0:T(8,128)(2,1)}, u32[]{:S(2)}, u32[]{:S(2)}) async-start(bf16[8,256,128]{2,1,0:T(8,128)(2,1)} %bitcast.53), calls=%async_computation.4 | async-start | bytes 1048576 | tf_op jit(solution)/shard_map/all_to_all | solution.py:388
  171.9 12.8 %tower.2 = (bf16[8,256,256]{2,1,0:T(8,128)(2,1)}, f32[256,1]{1,0:T(8,128)S(1)}) custom-call(s32[16]{0:T(128)S(1)} %select_reduce_fusion.table_of_ref, s32[8]{0:T(128)S(1)} %convert_reduce_fusion.1.count_ref, s32[1]{0:T(128)} %bitcast.1.shard_ref, bf16[8,512,128]{2,1,0:T(8,128)(2,1)} %all-to-all-done.2.refs_0_, bf16[8,256,128]{2,1,0:T(8,128)(2,1)} %all-to-all-done.3.refs_1_, ...), custom_call_target="tpu_custom_call" | custom-call | flops 4026531840 | bytes 60000000 | tf_op jit(solution)/shard_map/tower/pallas_call | solution.py:259
  184.9 5.8 %all-to-all-start.5 = ((bf16[8,256,256]{2,1,0:T(8,128)(2,1)}), bf16[8,256,256]{2,1,0:T(8,128)(2,1)}, u32[]{:S(2)}, u32[]{:S(2)}) async-start(bf16[8,256,256]{2,1,0:T(8,128)(2,1)} %get-tuple-element.80), calls=%async_computation.5 | async-start | bytes 2097152 | tf_op jit(solution)/shard_map/all_to_all | solution.py:445
  190.7 12.8 %tower.3 = (bf16[8,256,256]{2,1,0:T(8,128)(2,1)}, f32[256,1]{1,0:T(8,128)S(1)}) custom-call(s32[16]{0:T(128)S(1)} %select_reduce_fusion.table_of_ref, s32[8]{0:T(128)S(1)} %convert_reduce_fusion.1.count_ref, s32[1]{0:T(128)} %bitcast.1.shard_ref, bf16[8,512,128]{2,1,0:T(8,128)(2,1)} %all-to-all-done.2.refs_0_, bf16[8,256,128]{2,1,0:T(8,128)(2,1)} %all-to-all-done.4.refs_1_, ...), custom_call_target="tpu_custom_call" | custom-call | flops 4026531840 | bytes 60000000 | tf_op jit(solution)/shard_map/tower/pallas_call | solution.py:259
  203.5 12.6 %all-to-all-done.5 = bf16[8,256,256]{2,1,0:T(8,128)(2,1)} async-done(((bf16[8,256,256]{2,1,0:T(8,128)(2,1)}), bf16[8,256,256]{2,1,0:T(8,128)(2,1)}, u32[]{:S(2)}, u32[]{:S(2)}) %all-to-all-start.5) | async-done | bytes 1048608 | tf_op jit(solution)/shard_map/all_to_all | solution.py:445
  216.1 3.6 %all-to-all-start.6 = ((bf16[8,256,256]{2,1,0:T(8,128)(2,1)}), bf16[8,256,256]{2,1,0:T(8,128)(2,1)S(1)}, u32[]{:S(2)}, u32[]{:S(2)}) async-start(bf16[8,256,256]{2,1,0:T(8,128)(2,1)} %get-tuple-element.83), calls=%async_computation.6 | async-start | bytes 2097152 | tf_op jit(solution)/shard_map/all_to_all | solution.py:449
  220.5 24.9 %all-to-all-done.6 = bf16[8,256,256]{2,1,0:T(8,128)(2,1)S(1)} async-done(((bf16[8,256,256]{2,1,0:T(8,128)(2,1)}), bf16[8,256,256]{2,1,0:T(8,128)(2,1)S(1)}, u32[]{:S(2)}, u32[]{:S(2)}) %all-to-all-start.6) | async-done | bytes 1048608 | tf_op jit(solution)/shard_map/all_to_all | solution.py:449
  (94 shorter events, 36.8 us)
Async XLA Ops:
  1.9 13.8 %all-to-all-start = ((s32[8,1,512]{2,1,0:T(1,128)}), s32[8,1,512]{2,1,0:T(1,128)S(1)}, u32[]{:S(2)}, u32[]{:S(2)}) async-start(s32[8,1,512]{2,1,0:T(1,128)} %broadcast_in_dim.25), calls=%async_computation | async-start | bytes 32768 | tf_op jit(solution)/shard_map/all_to_all | solution.py:349
  15.8 14.5 %collective-permute-start = (bf16[528,256]{1,0:T(8,128)(2,1)S(1)}, bf16[528,256]{1,0:T(8,128)(2,1)S(1)}, u32[]{:S(2)}, u32[]{:S(2)}) collective-permute-start(bf16[528,256]{1,0:T(8,128)(2,1)S(1)} %fusion.1), channel_id=1, source_target_pairs={{0,4},{1,5},{2,6},{3,7},{4,0},{5,1},{6,2},{7,3},{8,12},{9,13},{10,... | collective-permute-start | bytes 811016 | tf_op jit(solution)/shard_map/ppermute | solution.py:295
  30.3 55.8 %all-to-all-start.1 = ((bf16[8,528,256]{2,1,0:T(8,128)(2,1)}), bf16[8,528,256]{2,1,0:T(8,128)(2,1)}, u32[]{:S(2)}, u32[]{:S(2)}) async-start(bf16[8,528,256]{2,1,0:T(8,128)(2,1)} %held_items.1), calls=%async_computation.1 | async-start | bytes 4325376 | tf_op jit(solution)/shard_map/all_to_all | solution.py:396
  36.1 47.9 %collective-permute-start.4 = (bf16[512,1024]{1,0:T(8,128)(2,1)S(1)}, bf16[512,1024]{1,0:T(8,128)(2,1)S(1)}, u32[]{:S(2)}, u32[]{:S(2)}) collective-permute-start(bf16[512,1024]{1,0:T(8,128)(2,1)S(1)} %copy-done.10), channel_id=1, source_target_pairs={{0,16},{8,24},{16,0},{24,8},{1,17},{9,25},{17,1},{25,9},{2,18},{10... | collective-permute-start | bytes 3145736 | tf_op jit(solution)/shard_map/ppermute | solution.py:295
  37.7 48.2 %collective-permute-start.5 = (bf16[512,1024]{1,0:T(8,128)(2,1)S(1)}, bf16[512,1024]{1,0:T(8,128)(2,1)}, u32[]{:S(2)}, u32[]{:S(2)}) collective-permute-start(bf16[512,1024]{1,0:T(8,128)(2,1)S(1)} %copy-done.10), channel_id=1, source_target_pairs={{0,8},{8,0},{16,24},{24,16},{1,9},{9,1},{17,25},{25,17},{2,10},{10... | collective-permute-start | bytes 3145736 | tf_op jit(solution)/shard_map/ppermute | solution.py:295
  37.7 46.3 %collective-permute-start.3 = (bf16[1056,256]{1,0:T(8,128)(2,1)S(1)}, bf16[1056,256]{1,0:T(8,128)(2,1)S(1)}, u32[]{:S(2)}, u32[]{:S(2)}) collective-permute-start(bf16[1056,256]{1,0:T(8,128)(2,1)S(1)} %pad_maximum_fusion.1), channel_id=1, source_target_pairs={{0,1},{1,0},{2,3},{3,2},{4,5},{5,4},{6,7},{7,6},{8,9},{9,8},{10,11... | collective-permute-start | bytes 1622024 | tf_op jit(solution)/shard_map/ppermute | solution.py:295
  39.8 39.4 %collective-permute-start.1 = (bf16[528,256]{1,0:T(8,128)(2,1)S(1)}, bf16[528,256]{1,0:T(8,128)(2,1)S(1)}, u32[]{:S(2)}, u32[]{:S(2)}) collective-permute-start(bf16[528,256]{1,0:T(8,128)(2,1)S(1)} %fusion.1), channel_id=1, source_target_pairs={{0,2},{1,3},{2,0},{3,1},{4,6},{5,7},{6,4},{7,5},{8,10},{9,11},{10,... | collective-permute-start | bytes 811016 | tf_op jit(solution)/shard_map/ppermute | solution.py:295
  41.2 42.8 %collective-permute-start.2 = (bf16[528,256]{1,0:T(8,128)(2,1)S(1)}, bf16[528,256]{1,0:T(8,128)(2,1)S(1)}, u32[]{:S(2)}, u32[]{:S(2)}) collective-permute-start(bf16[528,256]{1,0:T(8,128)(2,1)S(1)} %collective-permute-done), channel_id=1, source_target_pairs={{0,2},{1,3},{2,0},{3,1},{4,6},{5,7},{6,4},{7,5},{8,10},{9,11},{10,... | collective-permute-start | bytes 811016 | tf_op jit(solution)/shard_map/ppermute | solution.py:295
  86.9 19.2 %collective-permute-start.8 = (bf16[1056,256]{1,0:T(8,128)(2,1)}, bf16[1056,256]{1,0:T(8,128)(2,1)}, u32[]{:S(2)}, u32[]{:S(2)}) collective-permute-start(bf16[1056,256]{1,0:T(8,128)(2,1)} %pad_maximum_fusion.2), channel_id=1, source_target_pairs={{0,1},{1,0},{2,3},{3,2},{4,5},{5,4},{6,7},{7,6},{8,9},{9,8},{10,11... | collective-permute-start | bytes 1622024 | tf_op jit(solution)/shard_map/ppermute | solution.py:295
  90.4 14.5 %collective-permute-start.6 = (bf16[528,256]{1,0:T(8,128)(2,1)S(1)}, bf16[528,256]{1,0:T(8,128)(2,1)S(1)}, u32[]{:S(2)}, u32[]{:S(2)}) collective-permute-start(bf16[528,256]{1,0:T(8,128)(2,1)S(1)} %reduce_sum.58.refs_8_), channel_id=1, source_target_pairs={{0,4},{1,5},{2,6},{3,7},{4,0},{5,1},{6,2},{7,3},{8,12},{9,13},{10,... | collective-permute-start | bytes 811016 | tf_op jit(solution)/shard_map/ppermute | solution.py:295
  93.8 12.3 %collective-permute-start.7 = (bf16[528,256]{1,0:T(8,128)(2,1)S(1)}, bf16[528,256]{1,0:T(8,128)(2,1)S(1)}, u32[]{:S(2)}, u32[]{:S(2)}) collective-permute-start(bf16[528,256]{1,0:T(8,128)(2,1)S(1)} %reduce_sum.58.refs_8_), channel_id=1, source_target_pairs={{0,1},{1,0},{2,3},{3,2},{4,5},{5,4},{6,7},{7,6},{8,9},{9,8},{10,11... | collective-permute-start | bytes 811016 | tf_op jit(solution)/shard_map/ppermute | solution.py:295
  106.1 34.6 %all-to-all-start.2 = ((bf16[8,512,128]{2,1,0:T(8,128)(2,1)}), bf16[8,512,128]{2,1,0:T(8,128)(2,1)}, u32[]{:S(2)}, u32[]{:S(2)}) async-start(bf16[8,512,128]{2,1,0:T(8,128)(2,1)} %bitcast.20), calls=%async_computation.2 | async-start | bytes 2097152 | tf_op jit(solution)/shard_map/all_to_all | solution.py:388
  111.5 26.3 %collective-permute-start.9 = (bf16[528,256]{1,0:T(8,128)(2,1)S(1)}, bf16[528,256]{1,0:T(8,128)(2,1)S(1)}, u32[]{:S(2)}, u32[]{:S(2)}) collective-permute-start(bf16[528,256]{1,0:T(8,128)(2,1)S(1)} %reduce_sum.58.refs_8_), channel_id=1, source_target_pairs={{0,2},{1,3},{2,0},{3,1},{4,6},{5,7},{6,4},{7,5},{8,10},{9,11},{10,... | collective-permute-start | bytes 811016 | tf_op jit(solution)/shard_map/ppermute | solution.py:295
  113.5 27.2 %collective-permute-start.10 = (bf16[528,256]{1,0:T(8,128)(2,1)S(1)}, bf16[528,256]{1,0:T(8,128)(2,1)S(1)}, u32[]{:S(2)}, u32[]{:S(2)}) collective-permute-start(bf16[528,256]{1,0:T(8,128)(2,1)S(1)} %collective-permute-done.6.refs_12_), channel_id=1, source_target_pairs={{0,2},{1,3},{2,0},{3,1},{4,6},{5,7},{6,4},{7,5},{8,10},{9,11},{10,... | collective-permute-start | bytes 811016 | tf_op jit(solution)/shard_map/ppermute | solution.py:295
  113.6 27.1 %collective-permute-start.11 = (bf16[528,256]{1,0:T(8,128)(2,1)S(1)}, bf16[528,256]{1,0:T(8,128)(2,1)S(1)}, u32[]{:S(2)}, u32[]{:S(2)}) collective-permute-start(bf16[528,256]{1,0:T(8,128)(2,1)S(1)} %collective-permute-done.6.refs_12_), channel_id=1, source_target_pairs={{0,1},{1,0},{2,3},{3,2},{4,5},{5,4},{6,7},{7,6},{8,9},{9,8},{10,11... | collective-permute-start | bytes 811016 | tf_op jit(solution)/shard_map/ppermute | solution.py:295
  133.2 15.2 %copy-start.15 = (s32[8]{0:T(128)S(1)}, s32[8]{0:T(128)}, u32[]{:S(2)}) copy-start(s32[8]{0:T(128)} %constant.44.clone) | copy-start | bytes 100
  141.6 23.8 %all-to-all-start.3 = ((bf16[8,256,128]{2,1,0:T(8,128)(2,1)}), bf16[8,256,128]{2,1,0:T(8,128)(2,1)}, u32[]{:S(2)}, u32[]{:S(2)}) async-start(bf16[8,256,128]{2,1,0:T(8,128)(2,1)} %bitcast.52), calls=%async_computation.3 | async-start | bytes 1048576 | tf_op jit(solution)/shard_map/all_to_all | solution.py:388
  146.2 24.7 %collective-permute-start.14 = (bf16[512,1024]{1,0:T(8,128)(2,1)}, bf16[512,1024]{1,0:T(8,128)(2,1)}, u32[]{:S(2)}, u32[]{:S(2)}) collective-permute-start(bf16[512,1024]{1,0:T(8,128)(2,1)} %copy-done.11), channel_id=1, source_target_pairs={{0,8},{8,0},{16,24},{24,16},{1,9},{9,1},{17,25},{25,17},{2,10},{10... | collective-permute-start | bytes 3145736 | tf_op jit(solution)/shard_map/ppermute | solution.py:295
  146.2 13.9 %collective-permute-start.12 = (bf16[528,256]{1,0:T(8,128)(2,1)S(1)}, bf16[528,256]{1,0:T(8,128)(2,1)S(1)}, u32[]{:S(2)}, u32[]{:S(2)}) collective-permute-start(bf16[528,256]{1,0:T(8,128)(2,1)S(1)} %collective-permute-done.9.refs_10_), channel_id=1, source_target_pairs={{0,1},{1,0},{2,3},{3,2},{4,5},{5,4},{6,7},{7,6},{8,9},{9,8},{10,11... | collective-permute-start | bytes 811016 | tf_op jit(solution)/shard_map/ppermute | solution.py:295
  148.3 17.0 %collective-permute-start.13 = (bf16[528,256]{1,0:T(8,128)(2,1)}, bf16[528,256]{1,0:T(8,128)(2,1)}, u32[]{:S(2)}, u32[]{:S(2)}) collective-permute-start(bf16[528,256]{1,0:T(8,128)(2,1)} %copy-done.13), channel_id=1, source_target_pairs={{0,1},{1,0},{2,3},{3,2},{4,5},{5,4},{6,7},{7,6},{8,9},{9,8},{10,11... | collective-permute-start | bytes 811016 | tf_op jit(solution)/shard_map/ppermute | solution.py:295
  159.0 11.8 %copy-start.3 = (bf16[528,256]{1,0:T(8,128)(2,1)S(1)}, bf16[528,256]{1,0:T(8,128)(2,1)}, u32[]{:S(2)}) copy-start(bf16[528,256]{1,0:T(8,128)(2,1)} %copy-done.2) | copy-start | bytes 811012
  166.2 18.7 %all-to-all-start.4 = ((bf16[8,256,128]{2,1,0:T(8,128)(2,1)}), bf16[8,256,128]{2,1,0:T(8,128)(2,1)}, u32[]{:S(2)}, u32[]{:S(2)}) async-start(bf16[8,256,128]{2,1,0:T(8,128)(2,1)} %bitcast.53), calls=%async_computation.4 | async-start | bytes 1048576 | tf_op jit(solution)/shard_map/all_to_all | solution.py:388
  184.9 31.2 %all-to-all-start.5 = ((bf16[8,256,256]{2,1,0:T(8,128)(2,1)}), bf16[8,256,256]{2,1,0:T(8,128)(2,1)}, u32[]{:S(2)}, u32[]{:S(2)}) async-start(bf16[8,256,256]{2,1,0:T(8,128)(2,1)} %get-tuple-element.80), calls=%async_computation.5 | async-start | bytes 2097152 | tf_op jit(solution)/shard_map/all_to_all | solution.py:445
  216.1 29.3 %all-to-all-start.6 = ((bf16[8,256,256]{2,1,0:T(8,128)(2,1)}), bf16[8,256,256]{2,1,0:T(8,128)(2,1)S(1)}, u32[]{:S(2)}, u32[]{:S(2)}) async-start(bf16[8,256,256]{2,1,0:T(8,128)(2,1)} %get-tuple-element.83), calls=%async_computation.6 | async-start | bytes 2097152 | tf_op jit(solution)/shard_map/all_to_all | solution.py:449
  (14 other events, 80.4 us)

commit v4 on v3

--- a/solution.py
+++ b/solution.py
@@ -25,7 +25,7 @@
 def pool_kernel(bag, ids_ref, table_ref, *refs):
     out_ref, wide, rows = refs[-3:]
     table_rows = table_ref.shape[1]
-    unroll = 16
+    unroll = 32
 
     @pl.when(pl.program_id(0) == 0)
     def _():
@@ -152,14 +152,16 @@
     )(jnp.where(held, ids, owned), ids[None, :], bank, log_q.T)
 
 
-def tower_kernel(scale, lead, n_x, n_w, n_noise, table_of_ref, count_ref, shard_ref, *refs):
+def tower_kernel(scale, lead, n_x, n_w, n_noise, apart, table_of_ref, count_ref, place_ref, *refs):
     x_refs, refs = refs[:n_x], refs[n_x:]
     owners, users, emb = x_refs[0].shape
     w_refs, refs = refs[:n_w], refs[n_w:]
     b_ref, w2_ref, *refs = refs
     pos_refs, refs = refs[:owners], refs[owners:]
     noise_refs, refs = refs[:n_noise], refs[n_noise:]
-    grad_ref, loss_ref, w_ref, pre_ref, score_ref, noise_vec, noise_lq, picked_lq, w_sem = refs
+    n_grad = owners if apart else 1
+    grad_refs, refs = refs[:n_grad], refs[n_grad:]
+    loss_ref, w_ref, pre_ref, score_ref, noise_vec, noise_lq, picked_lq, w_sem = refs
     depth = n_x * emb
     held, width = pos_refs[0].shape
     batch_users = held - LQ_ROWS
@@ -177,7 +179,7 @@
     per = w_refs[0].shape[0] // emb
     for o in range(n_w):
         for i in range(per):
-            place(o, i, table_of_ref[(shard_ref[0] ^ o) * per + i]).start()
+            place(o, i, table_of_ref[(place_ref[1] ^ o) * per + i]).start()
     filled = jnp.int32(0)
     step = most + LQ_ROWS
     for o, (noise_ref, begin) in enumerate((r, c) for r in noise_refs for c in range(0, r.shape[0], step)):
@@ -241,12 +243,15 @@
     sig = jax.nn.sigmoid(pre)
     pre_grad = (hidden_grad * sig * (1.0 + pre * (1.0 - sig))).astype(jnp.bfloat16)
     for s in range(owners):
-        grad_ref[s] = lax.dot_general(
-            pre_grad, weight(s), CONTRACT, preferred_element_type=jnp.float32
-        ).astype(jnp.bfloat16)
-
-
-def tower(lead, users, table_of, counts, shard, xs, ws, b, w2, pos, noise, n_noise, n_picked):
+        part = weight(place_ref[0] ^ s if apart else s)
+        grad = lax.dot_general(pre_grad, part, CONTRACT, preferred_element_type=jnp.float32).astype(jnp.bfloat16)
+        if apart:
+            grad_refs[s][...] = grad
+        else:
+            grad_refs[0][s] = grad
+
+
+def tower(lead, users, apart, table_of, counts, place, xs, ws, b, w2, pos, noise, n_noise, n_picked):
     owners, _, emb = xs[0][0].shape
     per_owner = len(xs)
     hid, width = w2.shape
@@ -256,8 +261,9 @@
     smem = pl.BlockSpec(memory_space=pltpu.SMEM)
     flops = 2 * users * (2 * depth * hid + 2 * hid * width + 2 * candidates * width)
     wide = per_owner * emb
+    shapes = [(users, wide)] * owners if apart else [(owners, users, wide)]
     return pl.pallas_call(
-        functools.partial(tower_kernel, width ** (-0.5), lead, per_owner, len(ws), len(noise)),
+        functools.partial(tower_kernel, width ** (-0.5), lead, per_owner, len(ws), len(noise), apart),
         grid=(1,),
         in_specs=[smem] * 3
         + [
@@ -265,14 +271,10 @@
         ]
         + [pl.BlockSpec(memory_space=pl.ANY)] * len(ws)
         + [pl.BlockSpec(a.shape, lambda i: (0, 0), pipeline_mode=once) for a in (b, w2, *pos, *noise)],
-        out_specs=[
-            pl.BlockSpec((owners, users, wide), lambda i: (0, 0, 0)),
-            pl.BlockSpec((users, 1), lambda i: (0, 0)),
-        ],
-        out_shape=[
-            jax.ShapeDtypeStruct((owners, users, wide), jnp.bfloat16),
-            jax.ShapeDtypeStruct((users, 1), jnp.float32),
-        ],
+        out_specs=[pl.BlockSpec(shape, lambda i, n=len(shape): (0,) * n) for shape in shapes]
+        + [pl.BlockSpec((users, 1), lambda i: (0, 0))],
+        out_shape=[jax.ShapeDtypeStruct(shape, jnp.bfloat16) for shape in shapes]
+        + [jax.ShapeDtypeStruct((users, 1), jnp.float32)],
         scratch_shapes=[
             pltpu.VMEM((depth, hid), jnp.bfloat16),
             pltpu.VMEM((users, hid), jnp.float32),
@@ -287,7 +289,7 @@
             flops=flops, bytes_accessed=60_000_000, transcendentals=users * candidates
         ),
         name="tower",
-    )(table_of, counts, shard, *(x for x, _ in xs), *ws, b, w2, *pos, *noise)
+    )(table_of, counts, place, *(x for x, _ in xs), *ws, b, w2, *pos, *noise)
 
 
 def swap(x, axis, offset):
@@ -343,7 +345,7 @@
     blocks_dev, block_items, width = bank.shape
     users = row_users // owners
 
-    shard = lax.axis_index("batch").astype(jnp.int32)[None]
+    place = jnp.stack([me, lax.axis_index("batch")]).astype(jnp.int32)
 
     copies = jnp.broadcast_to(pos_items[None, :], (owners, users))
     item_ids = lax.all_to_all(copies, "table", split_axis=0, concat_axis=0, tiled=True).reshape(-1)
@@ -438,18 +440,20 @@
     noise_owner = me ^ jnp.asarray(noise_from + [o ^ 1 for o in noise_from], jnp.int32)
     counts = jnp.sum((owner_of[None, :] == noise_owner[:, None]).astype(jnp.int32), axis=1)
     run = functools.partial(
-        tower, users=users // 2, table_of=table_of, counts=counts, shard=shard, ws=ws, b=b_first[None, :], w2=w_second, pos=pos,
+        tower, users=users // 2, table_of=table_of, counts=counts, place=place, ws=ws, b=b_first[None, :], w2=w_second, pos=pos,
         noise=[near_noise, first_noise, far_noise], n_noise=sample.shape[0] * block_items, n_picked=sample.shape[0],
     )
-    grad_early, loss_early = run(lead=0, xs=[(v, 0) for v in xs] + [(early, 0)])
+    grad_early, loss_early = run(lead=0, apart=False, xs=[(v, 0) for v in xs] + [(early, 0)])
     back = [lax.all_to_all(grad_early, "table", split_axis=0, concat_axis=0, tiled=True)]
     _, late = tie(loss_early, late)
-    grad_late, loss_late = run(lead=users // 2, xs=[(v, 1) for v in xs] + [(late, 0)])
-    back[0], grad_late = tie(back[0], grad_late)
-    back.append(lax.all_to_all(grad_late, "table", split_axis=0, concat_axis=0, tiled=True))
+    *grad_late, loss_late = run(lead=users // 2, apart=True, xs=[(v, 1) for v in xs] + [(late, 0)])
+    came = {o: grad_late[o] if o == 0 else swap(grad_late[o], "table", o) for o in reversed(range(owners))}
+    both = jnp.concatenate([back[0], jnp.zeros_like(back[0])], axis=1)
+    for o in range(owners):
+        both = lax.dynamic_update_slice(both, came[o][None], (me ^ o, users // 2, 0))
     losses = [loss_early[:, 0], loss_late[:, 0]]
     own_lq = own_pos[users : users + users // width].astype(jnp.float32).reshape(users)
-    grad = jnp.concatenate(back, axis=1).reshape(row_users, per_owner, emb)
+    grad = both.reshape(row_users, per_owner, emb)
     return (jnp.concatenate(losses) + own_lq, grad)
 
 

time: 250 us -> 244 us (0.976)
  waiting for transfers between devices: 65.4 us -> 49 us
  local copies, waits for them, and re-layouts: 11.7 us -> 22.8 us
  starting transfers between devices: 57.1 us -> 60.2 us
    all_to_all x1 -> x0, waiting for transfers between devices: 24.9 us -> none  [on_device(): lax.all_to_all(grad_late, 'table', split_axis=0, concat_axis=0, tiled=True)]
    ppermute x15 -> x22, waiting for transfers between devices: 27.3 us -> 34.6 us  [swap(): return lax.ppermute(x, axis, [(i, i ^ offset) for i in range(size)])]
    ppermute x15 -> x22, starting transfers between devices: 20.1 us -> 27.2 us  [swap(): return lax.ppermute(x, axis, [(i, i ^ offset) for i in range(size)])]
    dynamic_update_slice x0 -> x8, local copies, waits for them, and re-layouts: none -> 5.25 us  [on_device(): lax.dynamic_update_slice(both, came[o][None], (me ^ o, users // 2, 0))]
    all_to_all x1 -> x0, starting transfers between devices: 3.56 us -> none  [on_device(): lax.all_to_all(grad_late, 'table', split_axis=0, concat_axis=0, tiled=True)]
    concatenate x0 -> x1, local copies, waits for them, and re-layouts: none -> 2.71 us  [on_device(): both = jnp.concatenate([back[0], jnp.zeros_like(back[0])], axis=1)]
  transfers between devices with their start and end apart: 22 -> 28, of which waited for: 14 -> 14; matrix products, arithmetic and copies ran while one was open for 4% -> 8% of each run, Pallas kernels for 42% -> 43%
where the time goes in v4:
time: 244 us; the launch traced here: 243 us
  Pallas kernels  104 us (43%)
  starting transfers between devices  60.2 us (25%)
  waiting for transfers between devices  49 us (20%)
  local copies, waits for them, and re-layouts  22.8 us (9%)
  other arithmetic  5.97 us (2%)
    pallas_call x4, Pallas kernels, pool(): pl.pallas_call(functools.partial(pool_kernel, bag), grid=(last - first,),...  69.1 us
    ppermute x22, waiting for transfers between devices, swap(): return lax.ppermute(x, axis, [(i, i ^ offset) for i in range(size)])  34.6 us
    ppermute x22, starting transfers between devices, swap(): return lax.ppermute(x, axis, [(i, i ^ offset) for i in range(size)])  27.2 us
    pallas_call x2, Pallas kernels, tower(): pl.pallas_call(functools.partial(tower_kernel, width ** (-0.5), lead, per...  25.5 us
    all_to_all x3, starting transfers between devices, exchange(): lax.all_to_all(pooled, 'table', split_axis=0, concat_axis=0, tiled=True)  13.9 us
    all_to_all x1, waiting for transfers between devices, on_device(): lax.all_to_all(grad_early, 'table', split_axis=0, concat_axis=0, tiled=True)  13.2 us
    pallas_call x1, Pallas kernels, held_items(): pl.pallas_call(functools.partial(items_kernel, users), in_specs=[pl.Block...  9.3 us
    all_to_all x1, starting transfers between devices, on_device(): lax.all_to_all(copies, 'table', split_axis=0, concat_axis=0, tiled=True)  7.25 us
  transfers between devices with their start and end apart: 28, of which 14 were waited for; matrix products, arithmetic and copies ran while one was open for 8% of the time, Pallas kernels for 43%

profile of v4, /device:TPU:0, one launch (start us, length us, event | category | flops | bytes accessed | tf_op | source)
XLA Modules:
  0.0 242.8 jit_solution(685358163250591711)
XLA Ops:
  2.1 7.3 %all-to-all-start = ((s32[8,1,512]{2,1,0:T(1,128)}), s32[8,1,512]{2,1,0:T(1,128)S(1)}, u32[]{:S(2)}, u32[]{:S(2)}) async-start(s32[8,1,512]{2,1,0:T(1,128)} %broadcast_in_dim.42), calls=%async_computation | async-start | bytes 32768 | tf_op jit(solution)/shard_map/all_to_all | solution.py:351
  15.9 2.6 %collective-permute-start = (bf16[528,256]{1,0:T(8,128)(2,1)S(1)}, bf16[528,256]{1,0:T(8,128)(2,1)S(1)}, u32[]{:S(2)}, u32[]{:S(2)}) collective-permute-start(bf16[528,256]{1,0:T(8,128)(2,1)S(1)} %fusion.1), channel_id=1, source_target_pairs={{0,4},{1,5},{2,6},{3,7},{4,0},{5,1},{6,2},{7,3},{8,12},{9,13},{10,... | collective-permute-start | bytes 811016 | tf_op jit(solution)/shard_map/ppermute | solution.py:297
  18.7 9.3 %held_items.1 = bf16[8,528,256]{2,1,0:T(8,128)(2,1)} custom-call(s32[4096]{0:T(1024)S(1)} %get-tuple-element.94.ids_ref, s32[1,4096]{1,0:T(1,128)S(1)} %bitcast.65, bf16[4096,256]{1,0:T(8,128)(2,1)S(1)} %bitcast.64, bf16[64,64]{1,0:T(8,128)(2,1)S(1)} %bitcast.66), custom_call_target="tpu_custom_call" | custom-call | bytes 30000000 | tf_op jit(solution)/shard_map/held_items/pallas_call | solution.py:138
  30.3 5.8 %all-to-all-start.1 = ((bf16[8,528,256]{2,1,0:T(8,128)(2,1)}), bf16[8,528,256]{2,1,0:T(8,128)(2,1)}, u32[]{:S(2)}, u32[]{:S(2)}) async-start(bf16[8,528,256]{2,1,0:T(8,128)(2,1)} %held_items.1), calls=%async_computation.1 | async-start | bytes 4325376 | tf_op jit(solution)/shard_map/all_to_all | solution.py:398
  41.9 31.6 %pool.4 = bf16[4096,128]{1,0:T(8,128)(2,1)} custom-call(s32[32768]{0:T(1024)S(1)} %get-tuple-element.52.ids_ref, bf16[2,16384,128]{2,1,0:T(8,128)(2,1)} %table_ref.3), custom_call_target="tpu_custom_call" | custom-call | flops 4194304 | bytes 3200000 | tf_op jit(solution)/shard_map/pool/pallas_call | solution.py:56
  73.5 5.7 %collective-permute-done.1 = bf16[528,256]{1,0:T(8,128)(2,1)S(1)} collective-permute-done((bf16[528,256]{1,0:T(8,128)(2,1)S(1)}, bf16[528,256]{1,0:T(8,128)(2,1)S(1)}, u32[]{:S(2)}, u32[]{:S(2)}) %collective-permute-start.1) | collective-permute-done | bytes 270368 | tf_op jit(solution)/shard_map/ppermute | solution.py:297
  79.1 4.9 %collective-permute-done.2 = bf16[528,256]{1,0:T(8,128)(2,1)S(1)} collective-permute-done((bf16[528,256]{1,0:T(8,128)(2,1)S(1)}, bf16[528,256]{1,0:T(8,128)(2,1)S(1)}, u32[]{:S(2)}, u32[]{:S(2)}) %collective-permute-start.2) | collective-permute-done | bytes 270368 | tf_op jit(solution)/shard_map/ppermute | solution.py:297
  90.2 2.7 %collective-permute-start.6 = (bf16[528,256]{1,0:T(8,128)(2,1)S(1)}, bf16[528,256]{1,0:T(8,128)(2,1)S(1)}, u32[]{:S(2)}, u32[]{:S(2)}) collective-permute-start(bf16[528,256]{1,0:T(8,128)(2,1)S(1)} %reduce_sum.58.refs_8_), channel_id=1, source_target_pairs={{0,4},{1,5},{2,6},{3,7},{4,0},{5,1},{6,2},{7,3},{8,12},{9,13},{10,... | collective-permute-start | bytes 811016 | tf_op jit(solution)/shard_map/ppermute | solution.py:297
  93.0 10.1 %pool.5.refs_0_ = bf16[4096,128]{1,0:T(8,128)(2,1)S(1)} custom-call(s32[32768]{0:T(1024)S(1)} %get-tuple-element.68.ids_ref, bf16[2,16384,128]{2,1,0:T(8,128)(2,1)} %table_ref.3), custom_call_target="tpu_custom_call" | custom-call | flops 1048576 | bytes 800000 | tf_op jit(solution)/shard_map/pool/pallas_call | solution.py:56
  105.0 4.9 %all-to-all-start.2 = ((bf16[8,512,128]{2,1,0:T(8,128)(2,1)}), bf16[8,512,128]{2,1,0:T(8,128)(2,1)}, u32[]{:S(2)}, u32[]{:S(2)}) async-start(bf16[8,512,128]{2,1,0:T(8,128)(2,1)} %bitcast.21), calls=%async_computation.2 | async-start | bytes 2097152 | tf_op jit(solution)/shard_map/all_to_all | solution.py:390
  113.9 17.2 %pool.6.refs_0_ = bf16[4096,128]{1,0:T(8,128)(2,1)S(1)} custom-call(s32[32768]{0:T(1024)S(1)} %get-tuple-element.68.ids_ref, bf16[2,16384,128]{2,1,0:T(8,128)(2,1)} %table_ref.3, bf16[4096,128]{1,0:T(8,128)(2,1)S(1)} %pool.5.refs_0_), custom_call_target="tpu_custom_call", output_to_operand_aliasing={{}: (2, {})} | custom-call | flops 2097152 | bytes 1600000 | tf_op jit(solution)/shard_map/pool/pallas_call | solution.py:56
  131.2 5.2 %collective-permute-done.9.refs_10_ = bf16[528,256]{1,0:T(8,128)(2,1)S(1)} collective-permute-done((bf16[528,256]{1,0:T(8,128)(2,1)S(1)}, bf16[528,256]{1,0:T(8,128)(2,1)S(1)}, u32[]{:S(2)}, u32[]{:S(2)}) %collective-permute-start.9) | collective-permute-done | bytes 270368 | tf_op jit(solution)/shard_map/ppermute | solution.py:297
  136.4 3.6 %collective-permute-done.10.refs_14_ = bf16[528,256]{1,0:T(8,128)(2,1)} collective-permute-done((bf16[528,256]{1,0:T(8,128)(2,1)S(1)}, bf16[528,256]{1,0:T(8,128)(2,1)}, u32[]{:S(2)}, u32[]{:S(2)}) %collective-permute-start.10) | collective-permute-done | bytes 270368 | tf_op jit(solution)/shard_map/ppermute | solution.py:297
  140.8 4.6 %all-to-all-start.3 = ((bf16[8,256,128]{2,1,0:T(8,128)(2,1)}), bf16[8,256,128]{2,1,0:T(8,128)(2,1)}, u32[]{:S(2)}, u32[]{:S(2)}) async-start(bf16[8,256,128]{2,1,0:T(8,128)(2,1)} %bitcast.22), calls=%async_computation.3 | async-start | bytes 1048576 | tf_op jit(solution)/shard_map/all_to_all | solution.py:390
  147.9 10.1 %pool.7 = bf16[4096,128]{1,0:T(8,128)(2,1)S(1)} custom-call(s32[32768]{0:T(1024)S(1)} %get-tuple-element.68.ids_ref, bf16[2,16384,128]{2,1,0:T(8,128)(2,1)} %table_ref.3, bf16[4096,128]{1,0:T(8,128)(2,1)S(1)} %pool.6.refs_0_), custom_call_target="tpu_custom_call", output_to_operand_aliasing={{}: (2, {})} | custom-call | flops 1048576 | bytes 800000 | tf_op jit(solution)/shard_map/pool/pallas_call | solution.py:56
  159.4 5.2 %collective-permute-done.13.refs_15_ = bf16[528,256]{1,0:T(8,128)(2,1)} collective-permute-done((bf16[528,256]{1,0:T(8,128)(2,1)}, bf16[528,256]{1,0:T(8,128)(2,1)}, u32[]{:S(2)}, u32[]{:S(2)}) %collective-permute-start.13) | collective-permute-done | bytes 270368 | tf_op jit(solution)/shard_map/ppermute | solution.py:297
  165.5 4.3 %all-to-all-start.4 = ((bf16[8,256,128]{2,1,0:T(8,128)(2,1)}), bf16[8,256,128]{2,1,0:T(8,128)(2,1)S(1)}, u32[]{:S(2)}, u32[]{:S(2)}) async-start(bf16[8,256,128]{2,1,0:T(8,128)(2,1)} %bitcast.69), calls=%async_computation.4 | async-start | bytes 1048576 | tf_op jit(solution)/shard_map/all_to_all | solution.py:390
  172.9 13.1 %tower.2 = (bf16[8,256,256]{2,1,0:T(8,128)(2,1)}, f32[256,1]{1,0:T(8,128)S(1)}) custom-call(s32[16]{0:T(128)S(1)} %select_reduce_fusion.table_of_ref, s32[8]{0:T(128)S(1)} %convert_reduce_fusion.1.count_ref, s32[2]{0:T(128)S(1)} %pad_add_fusion.place_ref, bf16[8,512,128]{2,1,0:T(8,128)(2,1)} %all-to-all-done.2.refs_0_, ...), custom_call_target="tpu_custom_call" | custom-call | flops 4026531840 | bytes 60000000 | tf_op jit(solution)/shard_map/tower/pallas_call | solution.py:265
  186.0 6.0 %all-to-all-start.5 = ((bf16[8,256,256]{2,1,0:T(8,128)(2,1)}), bf16[8,256,256]{2,1,0:T(8,128)(2,1)}, u32[]{:S(2)}, u32[]{:S(2)}) async-start(bf16[8,256,256]{2,1,0:T(8,128)(2,1)} %get-tuple-element.85), calls=%async_computation.5 | async-start | bytes 2097152 | tf_op jit(solution)/shard_map/all_to_all | solution.py:447
  192.1 12.4 %tower.3 = (bf16[256,256]{1,0:T(8,128)(2,1)S(1)}, bf16[256,256]{1,0:T(8,128)(2,1)S(1)}, bf16[256,256]{1,0:T(8,128)(2,1)S(1)}, bf16[256,256]{1,0:T(8,128)(2,1)S(1...) custom-call(s32[16]{0:T(128)S(1)} %select_reduce_fusion.table_of_ref, ...), custom_call_target="tpu_custom_call" | custom-call | flops 4026531840 | bytes 60000000 | tf_op jit(solution)/shard_map/tower/pallas_call | solution.py:265
  208.2 2.8 %collective-permute-start.18 = (bf16[256,256]{1,0:T(8,128)(2,1)S(1)}, bf16[256,256]{1,0:T(8,128)(2,1)S(1)}, u32[]{:S(2)}, u32[]{:S(2)}) collective-permute-start(bf16[256,256]{1,0:T(8,128)(2,1)S(1)} %get-tuple-element.90), channel_id=1, source_target_pairs={{0,4},{1,5},{2,6},{3,7},{4,0},{5,1},{6,2},{7,3},{8,12},{9,13},{10,... | collective-permute-start | bytes 393224 | tf_op jit(solution)/shard_map/ppermute | solution.py:297
  213.1 13.2 %all-to-all-done.5 = bf16[8,256,256]{2,1,0:T(8,128)(2,1)} async-done(((bf16[8,256,256]{2,1,0:T(8,128)(2,1)}), bf16[8,256,256]{2,1,0:T(8,128)(2,1)}, u32[]{:S(2)}, u32[]{:S(2)}) %all-to-all-start.5) | async-done | bytes 1048608 | tf_op jit(solution)/shard_map/all_to_all | solution.py:447
  226.4 2.7 %concatenate.23 = bf16[8,512,256]{2,1,0:T(8,128)(2,1)} pad(bf16[8,256,256]{2,1,0:T(8,128)(2,1)} %all-to-all-done.5, bf16[]{:T(256)} %constant.17.clone.1), padding=0_0x0_256x0_0 | pad | bytes 3145730 | tf_op jit(solution)/shard_map/concatenate | solution.py:451
  238.8 4.0 %reshape.104 = bf16[4096,2,128]{2,1,0:T(2,128)(2,1)} reshape(bf16[8,512,256]{2,1,0:T(8,128)(2,1)} %bitcast_dynamic-update-slice_fusion) | data formatting | bytes 4194304 | tf_op jit(solution)/shard_map/reshape | solution.py:456
  (117 shorter events, 52.5 us)
Async XLA Ops:
  15.9 14.3 %collective-permute-start = (bf16[528,256]{1,0:T(8,128)(2,1)S(1)}, bf16[528,256]{1,0:T(8,128)(2,1)S(1)}, u32[]{:S(2)}, u32[]{:S(2)}) collective-permute-start(bf16[528,256]{1,0:T(8,128)(2,1)S(1)} %fusion.1), channel_id=1, source_target_pairs={{0,4},{1,5},{2,6},{3,7},{4,0},{5,1},{6,2},{7,3},{8,12},{9,13},{10,... | collective-permute-start | bytes 811016 | tf_op jit(solution)/shard_map/ppermute | solution.py:297
  30.3 55.8 %all-to-all-start.1 = ((bf16[8,528,256]{2,1,0:T(8,128)(2,1)}), bf16[8,528,256]{2,1,0:T(8,128)(2,1)}, u32[]{:S(2)}, u32[]{:S(2)}) async-start(bf16[8,528,256]{2,1,0:T(8,128)(2,1)} %held_items.1), calls=%async_computation.1 | async-start | bytes 4325376 | tf_op jit(solution)/shard_map/all_to_all | solution.py:398
  36.1 47.9 %collective-permute-start.5 = (bf16[512,1024]{1,0:T(8,128)(2,1)S(1)}, bf16[512,1024]{1,0:T(8,128)(2,1)S(1)}, u32[]{:S(2)}, u32[]{:S(2)}) collective-permute-start(bf16[512,1024]{1,0:T(8,128)(2,1)S(1)} %copy-done.12), channel_id=1, source_target_pairs={{0,8},{8,0},{16,24},{24,16},{1,9},{9,1},{17,25},{25,17},{2,10},{10... | collective-permute-start | bytes 3145736 | tf_op jit(solution)/shard_map/ppermute | solution.py:297
  36.2 48.8 %collective-permute-start.4 = (bf16[512,1024]{1,0:T(8,128)(2,1)S(1)}, bf16[512,1024]{1,0:T(8,128)(2,1)}, u32[]{:S(2)}, u32[]{:S(2)}) collective-permute-start(bf16[512,1024]{1,0:T(8,128)(2,1)S(1)} %copy-done.12), channel_id=1, source_target_pairs={{0,16},{8,24},{16,0},{24,8},{1,17},{9,25},{17,1},{25,9},{2,18},{10... | collective-permute-start | bytes 3145736 | tf_op jit(solution)/shard_map/ppermute | solution.py:297
  37.8 46.2 %collective-permute-start.3 = (bf16[1056,256]{1,0:T(8,128)(2,1)S(1)}, bf16[1056,256]{1,0:T(8,128)(2,1)S(1)}, u32[]{:S(2)}, u32[]{:S(2)}) collective-permute-start(bf16[1056,256]{1,0:T(8,128)(2,1)S(1)} %pad_maximum_fusion), channel_id=1, source_target_pairs={{0,1},{1,0},{2,3},{3,2},{4,5},{5,4},{6,7},{7,6},{8,9},{9,8},{10,11... | collective-permute-start | bytes 1622024 | tf_op jit(solution)/shard_map/ppermute | solution.py:297
  39.8 39.3 %collective-permute-start.1 = (bf16[528,256]{1,0:T(8,128)(2,1)S(1)}, bf16[528,256]{1,0:T(8,128)(2,1)S(1)}, u32[]{:S(2)}, u32[]{:S(2)}) collective-permute-start(bf16[528,256]{1,0:T(8,128)(2,1)S(1)} %fusion.1), channel_id=1, source_target_pairs={{0,2},{1,3},{2,0},{3,1},{4,6},{5,7},{6,4},{7,5},{8,10},{9,11},{10,... | collective-permute-start | bytes 811016 | tf_op jit(solution)/shard_map/ppermute | solution.py:297
  41.3 42.7 %collective-permute-start.2 = (bf16[528,256]{1,0:T(8,128)(2,1)S(1)}, bf16[528,256]{1,0:T(8,128)(2,1)S(1)}, u32[]{:S(2)}, u32[]{:S(2)}) collective-permute-start(bf16[528,256]{1,0:T(8,128)(2,1)S(1)} %collective-permute-done), channel_id=1, source_target_pairs={{0,2},{1,3},{2,0},{3,1},{4,6},{5,7},{6,4},{7,5},{8,10},{9,11},{10,... | collective-permute-start | bytes 811016 | tf_op jit(solution)/shard_map/ppermute | solution.py:297
  86.1 18.9 %collective-permute-start.8 = (bf16[1056,256]{1,0:T(8,128)(2,1)S(1)}, bf16[1056,256]{1,0:T(8,128)(2,1)}, u32[]{:S(2)}, u32[]{:S(2)}) collective-permute-start(bf16[1056,256]{1,0:T(8,128)(2,1)S(1)} %pad_maximum_fusion.1), channel_id=1, source_target_pairs={{0,1},{1,0},{2,3},{3,2},{4,5},{5,4},{6,7},{7,6},{8,9},{9,8},{10,11... | collective-permute-start | bytes 1622024 | tf_op jit(solution)/shard_map/ppermute | solution.py:297
  89.6 15.4 %collective-permute-start.7 = (bf16[528,256]{1,0:T(8,128)(2,1)S(1)}, bf16[528,256]{1,0:T(8,128)(2,1)S(1)}, u32[]{:S(2)}, u32[]{:S(2)}) collective-permute-start(bf16[528,256]{1,0:T(8,128)(2,1)S(1)} %reduce_sum.58.refs_8_), channel_id=1, source_target_pairs={{0,1},{1,0},{2,3},{3,2},{4,5},{5,4},{6,7},{7,6},{8,9},{9,8},{10,11... | collective-permute-start | bytes 811016 | tf_op jit(solution)/shard_map/ppermute | solution.py:297
  90.2 14.8 %collective-permute-start.6 = (bf16[528,256]{1,0:T(8,128)(2,1)S(1)}, bf16[528,256]{1,0:T(8,128)(2,1)S(1)}, u32[]{:S(2)}, u32[]{:S(2)}) collective-permute-start(bf16[528,256]{1,0:T(8,128)(2,1)S(1)} %reduce_sum.58.refs_8_), channel_id=1, source_target_pairs={{0,4},{1,5},{2,6},{3,7},{4,0},{5,1},{6,2},{7,3},{8,12},{9,13},{10,... | collective-permute-start | bytes 811016 | tf_op jit(solution)/shard_map/ppermute | solution.py:297
  105.0 35.0 %all-to-all-start.2 = ((bf16[8,512,128]{2,1,0:T(8,128)(2,1)}), bf16[8,512,128]{2,1,0:T(8,128)(2,1)}, u32[]{:S(2)}, u32[]{:S(2)}) async-start(bf16[8,512,128]{2,1,0:T(8,128)(2,1)} %bitcast.21), calls=%async_computation.2 | async-start | bytes 2097152 | tf_op jit(solution)/shard_map/all_to_all | solution.py:390
  109.9 26.5 %collective-permute-start.9 = (bf16[528,256]{1,0:T(8,128)(2,1)S(1)}, bf16[528,256]{1,0:T(8,128)(2,1)S(1)}, u32[]{:S(2)}, u32[]{:S(2)}) collective-permute-start(bf16[528,256]{1,0:T(8,128)(2,1)S(1)} %reduce_sum.58.refs_8_), channel_id=1, source_target_pairs={{0,2},{1,3},{2,0},{3,1},{4,6},{5,7},{6,4},{7,5},{8,10},{9,11},{10,... | collective-permute-start | bytes 811016 | tf_op jit(solution)/shard_map/ppermute | solution.py:297
  111.9 24.5 %collective-permute-start.11 = (bf16[528,256]{1,0:T(8,128)(2,1)S(1)}, bf16[528,256]{1,0:T(8,128)(2,1)S(1)}, u32[]{:S(2)}, u32[]{:S(2)}) collective-permute-start(bf16[528,256]{1,0:T(8,128)(2,1)S(1)} %collective-permute-done.6.refs_12_), channel_id=1, source_target_pairs={{0,1},{1,0},{2,3},{3,2},{4,5},{5,4},{6,7},{7,6},{8,9},{9,8},{10,11... | collective-permute-start | bytes 811016 | tf_op jit(solution)/shard_map/ppermute | solution.py:297
  113.4 26.6 %collective-permute-start.10 = (bf16[528,256]{1,0:T(8,128)(2,1)S(1)}, bf16[528,256]{1,0:T(8,128)(2,1)}, u32[]{:S(2)}, u32[]{:S(2)}) collective-permute-start(bf16[528,256]{1,0:T(8,128)(2,1)S(1)} %collective-permute-done.6.refs_12_), channel_id=1, source_target_pairs={{0,2},{1,3},{2,0},{3,1},{4,6},{5,7},{6,4},{7,5},{8,10},{9,11},{10,... | collective-permute-start | bytes 811016 | tf_op jit(solution)/shard_map/ppermute | solution.py:297
  140.8 23.8 %all-to-all-start.3 = ((bf16[8,256,128]{2,1,0:T(8,128)(2,1)}), bf16[8,256,128]{2,1,0:T(8,128)(2,1)}, u32[]{:S(2)}, u32[]{:S(2)}) async-start(bf16[8,256,128]{2,1,0:T(8,128)(2,1)} %bitcast.22), calls=%async_computation.3 | async-start | bytes 1048576 | tf_op jit(solution)/shard_map/all_to_all | solution.py:390
  145.4 26.5 %collective-permute-start.14 = (bf16[512,1024]{1,0:T(8,128)(2,1)}, bf16[512,1024]{1,0:T(8,128)(2,1)}, u32[]{:S(2)}, u32[]{:S(2)}) collective-permute-start(bf16[512,1024]{1,0:T(8,128)(2,1)} %collective-permute-done.4.refs_4_), channel_id=1, source_target_pairs={{0,8},{8,0},{16,24},{24,16},{1,9},{9,1},{17,25},{25,17},{2,10},{10... | collective-permute-start | bytes 3145736 | tf_op jit(solution)/shard_map/ppermute | solution.py:297
  147.5 17.1 %collective-permute-start.13 = (bf16[528,256]{1,0:T(8,128)(2,1)}, bf16[528,256]{1,0:T(8,128)(2,1)}, u32[]{:S(2)}, u32[]{:S(2)}) collective-permute-start(bf16[528,256]{1,0:T(8,128)(2,1)} %collective-permute-done.10.refs_14_), channel_id=1, source_target_pairs={{0,1},{1,0},{2,3},{3,2},{4,5},{5,4},{6,7},{7,6},{8,9},{9,8},{10,11... | collective-permute-start | bytes 811016 | tf_op jit(solution)/shard_map/ppermute | solution.py:297
  165.5 20.5 %all-to-all-start.4 = ((bf16[8,256,128]{2,1,0:T(8,128)(2,1)}), bf16[8,256,128]{2,1,0:T(8,128)(2,1)S(1)}, u32[]{:S(2)}, u32[]{:S(2)}) async-start(bf16[8,256,128]{2,1,0:T(8,128)(2,1)} %bitcast.69), calls=%async_computation.4 | async-start | bytes 1048576 | tf_op jit(solution)/shard_map/all_to_all | solution.py:390
  186.0 40.4 %all-to-all-start.5 = ((bf16[8,256,256]{2,1,0:T(8,128)(2,1)}), bf16[8,256,256]{2,1,0:T(8,128)(2,1)}, u32[]{:S(2)}, u32[]{:S(2)}) async-start(bf16[8,256,256]{2,1,0:T(8,128)(2,1)} %get-tuple-element.85), calls=%async_computation.5 | async-start | bytes 2097152 | tf_op jit(solution)/shard_map/all_to_all | solution.py:447
  204.6 25.1 %collective-permute-start.15 = (bf16[256,256]{1,0:T(8,128)(2,1)S(1)}, bf16[256,256]{1,0:T(8,128)(2,1)S(1)}, u32[]{:S(2)}, u32[]{:S(2)}) collective-permute-start(bf16[256,256]{1,0:T(8,128)(2,1)S(1)} %get-tuple-element.87), channel_id=1, source_target_pairs={{0,1},{1,0},{2,3},{3,2},{4,5},{5,4},{6,7},{7,6},{8,9},{9,8},{10,11... | collective-permute-start | bytes 393224 | tf_op jit(solution)/shard_map/ppermute | solution.py:297
  206.7 23.7 %collective-permute-start.16 = (bf16[256,256]{1,0:T(8,128)(2,1)S(1)}, bf16[256,256]{1,0:T(8,128)(2,1)S(1)}, u32[]{:S(2)}, u32[]{:S(2)}) collective-permute-start(bf16[256,256]{1,0:T(8,128)(2,1)S(1)} %get-tuple-element.88), channel_id=1, source_target_pairs={{0,2},{1,3},{2,0},{3,1},{4,6},{5,7},{6,4},{7,5},{8,10},{9,11},{10,... | collective-permute-start | bytes 393224 | tf_op jit(solution)/shard_map/ppermute | solution.py:297
  208.2 22.9 %collective-permute-start.17 = (bf16[256,256]{1,0:T(8,128)(2,1)S(1)}, bf16[256,256]{1,0:T(8,128)(2,1)S(1)}, u32[]{:S(2)}, u32[]{:S(2)}) collective-permute-start(bf16[256,256]{1,0:T(8,128)(2,1)S(1)} %get-tuple-element.89), channel_id=1, source_target_pairs={{0,3},{1,2},{2,1},{3,0},{4,7},{5,6},{6,5},{7,4},{8,11},{9,10},{10,... | collective-permute-start | bytes 393224 | tf_op jit(solution)/shard_map/ppermute | solution.py:297
  208.2 23.5 %collective-permute-start.18 = (bf16[256,256]{1,0:T(8,128)(2,1)S(1)}, bf16[256,256]{1,0:T(8,128)(2,1)S(1)}, u32[]{:S(2)}, u32[]{:S(2)}) collective-permute-start(bf16[256,256]{1,0:T(8,128)(2,1)S(1)} %get-tuple-element.90), channel_id=1, source_target_pairs={{0,4},{1,5},{2,6},{3,7},{4,0},{5,1},{6,2},{7,3},{8,12},{9,13},{10,... | collective-permute-start | bytes 393224 | tf_op jit(solution)/shard_map/ppermute | solution.py:297
  211.1 23.4 %collective-permute-start.19 = (bf16[256,256]{1,0:T(8,128)(2,1)S(1)}, bf16[256,256]{1,0:T(8,128)(2,1)S(1)}, u32[]{:S(2)}, u32[]{:S(2)}) collective-permute-start(bf16[256,256]{1,0:T(8,128)(2,1)S(1)} %get-tuple-element.91), channel_id=1, source_target_pairs={{0,5},{1,4},{2,7},{3,6},{4,1},{5,0},{6,3},{7,2},{8,13},{9,12},{10,... | collective-permute-start | bytes 393224 | tf_op jit(solution)/shard_map/ppermute | solution.py:297
  (21 other events, 293.2 us)

commit v5 on v4

--- a/solution.py
+++ b/solution.py
@@ -447,10 +447,15 @@
     back = [lax.all_to_all(grad_early, "table", split_axis=0, concat_axis=0, tiled=True)]
     _, late = tie(loss_early, late)
     *grad_late, loss_late = run(lead=users // 2, apart=True, xs=[(v, 1) for v in xs] + [(late, 0)])
-    came = {o: grad_late[o] if o == 0 else swap(grad_late[o], "table", o) for o in reversed(range(owners))}
-    both = jnp.concatenate([back[0], jnp.zeros_like(back[0])], axis=1)
-    for o in range(owners):
-        both = lax.dynamic_update_slice(both, came[o][None], (me ^ o, users // 2, 0))
+    first = back[0].reshape(owners, users // 2, per_owner, emb)
+    both = jnp.concatenate([first, jnp.zeros_like(first)], axis=1)
+    far = range(owners // 2, owners)
+    came = {o: swap(grad_late[o], "table", o) for o in reversed(far)}
+    both, grad_late = tie(both, grad_late[: owners // 2])
+    came.update({o: grad_late[o] if o == 0 else swap(grad_late[o], "table", o) for o in range(owners // 2)})
+    for o in [*far, *range(owners // 2)]:
+        late_rows = came[o].reshape(1, users // 2, per_owner, emb)
+        both = lax.dynamic_update_slice(both, late_rows, (me ^ o, users // 2, 0, 0))
     losses = [loss_early[:, 0], loss_late[:, 0]]
     own_lq = own_pos[users : users + users // width].astype(jnp.float32).reshape(users)
     grad = both.reshape(row_users, per_owner, emb)

time: 244 us -> 253 us (1.037)
  starting transfers between devices: 60.2 us -> 66.5 us
  waiting for transfers between devices: 49 us -> 54.3 us
    ppermute x22, waiting for transfers between devices: 34.6 us -> 53.1 us  [swap(): return lax.ppermute(x, axis, [(i, i ^ offset) for i in range(size)])]
    all_to_all x1, waiting for transfers between devices: 13.2 us -> 0.01 us  [on_device(): lax.all_to_all(grad_early, 'table', split_axis=0, concat_axis=0, tiled=True)]
    ppermute x22, starting transfers between devices: 27.2 us -> 33.6 us  [swap(): return lax.ppermute(x, axis, [(i, i ^ offset) for i in range(size)])]
  transfers between devices with their start and end apart: 28 -> 28, of which waited for: 14 -> 12; matrix products, arithmetic and copies ran while one was open for 8% -> 7% of each run, Pallas kernels for 43% -> 41%
where the time goes in v5:
time: 253 us; the launch traced here: 252 us
  Pallas kernels  103 us (41%)
  starting transfers between devices  66.5 us (26%)
  waiting for transfers between devices  54.3 us (21%)
  local copies, waits for them, and re-layouts  21.4 us (8%)
  other arithmetic  5.97 us (2%)
    pallas_call x4, Pallas kernels, pool(): pl.pallas_call(functools.partial(pool_kernel, bag), grid=(last - first,),...  69.1 us
    ppermute x22, waiting for transfers between devices, swap(): return lax.ppermute(x, axis, [(i, i ^ offset) for i in range(size)])  53.1 us
    ppermute x22, starting transfers between devices, swap(): return lax.ppermute(x, axis, [(i, i ^ offset) for i in range(size)])  33.6 us
    pallas_call x2, Pallas kernels, tower(): pl.pallas_call(functools.partial(tower_kernel, width ** (-0.5), lead, per...  24.8 us
    all_to_all x3, starting transfers between devices, exchange(): lax.all_to_all(pooled, 'table', split_axis=0, concat_axis=0, tiled=True)  13.9 us
    pallas_call x1, Pallas kernels, held_items(): pl.pallas_call(functools.partial(items_kernel, users), in_specs=[pl.Block...  9.3 us
    all_to_all x1, starting transfers between devices, on_device(): lax.all_to_all(copies, 'table', split_axis=0, concat_axis=0, tiled=True)  7.25 us
    all_to_all x1, starting transfers between devices, on_device(): lax.all_to_all(grad_early, 'table', split_axis=0, concat_axis=0, tiled=True)  6.01 us
  transfers between devices with their start and end apart: 28, of which 12 were waited for; matrix products, arithmetic and copies ran while one was open for 7% of the time, Pallas kernels for 41%

profile of v5, /device:TPU:0, one launch (start us, length us, event | category | flops | bytes accessed | tf_op | source)
XLA Modules:
  0.0 252.4 jit_solution(4395449647782686413)
XLA Ops:
  2.1 7.3 %all-to-all-start = ((s32[8,1,512]{2,1,0:T(1,128)}), s32[8,1,512]{2,1,0:T(1,128)S(1)}, u32[]{:S(2)}, u32[]{:S(2)}) async-start(s32[8,1,512]{2,1,0:T(1,128)} %broadcast_in_dim.22), calls=%async_computation | async-start | bytes 32768 | tf_op jit(solution)/shard_map/all_to_all | solution.py:351
  18.7 9.3 %held_items.1 = bf16[8,528,256]{2,1,0:T(8,128)(2,1)} custom-call(s32[4096]{0:T(1024)S(1)} %get-tuple-element.104.ids_ref, s32[1,4096]{1,0:T(1,128)S(1)} %bitcast.50, bf16[4096,256]{1,0:T(8,128)(2,1)S(1)} %bitcast.49, bf16[64,64]{1,0:T(8,128)(2,1)S(1)} %bitcast.51), custom_call_target="tpu_custom_call" | custom-call | bytes 30000000 | tf_op jit(solution)/shard_map/held_items/pallas_call | solution.py:138
  30.3 5.8 %all-to-all-start.1 = ((bf16[8,528,256]{2,1,0:T(8,128)(2,1)}), bf16[8,528,256]{2,1,0:T(8,128)(2,1)}, u32[]{:S(2)}, u32[]{:S(2)}) async-start(bf16[8,528,256]{2,1,0:T(8,128)(2,1)} %held_items.1), calls=%async_computation.1 | async-start | bytes 4325376 | tf_op jit(solution)/shard_map/all_to_all | solution.py:398
  41.9 31.6 %pool.4 = bf16[4096,128]{1,0:T(8,128)(2,1)} custom-call(s32[32768]{0:T(1024)S(1)} %get-tuple-element.57.ids_ref, bf16[2,16384,128]{2,1,0:T(8,128)(2,1)} %table_ref.3), custom_call_target="tpu_custom_call" | custom-call | flops 4194304 | bytes 3200000 | tf_op jit(solution)/shard_map/pool/pallas_call | solution.py:56
  73.5 5.7 %collective-permute-done.1 = bf16[528,256]{1,0:T(8,128)(2,1)S(1)} collective-permute-done((bf16[528,256]{1,0:T(8,128)(2,1)S(1)}, bf16[528,256]{1,0:T(8,128)(2,1)S(1)}, u32[]{:S(2)}, u32[]{:S(2)}) %collective-permute-start.1) | collective-permute-done | bytes 270368 | tf_op jit(solution)/shard_map/ppermute | solution.py:297
  79.1 4.9 %collective-permute-done.2 = bf16[528,256]{1,0:T(8,128)(2,1)S(1)} collective-permute-done((bf16[528,256]{1,0:T(8,128)(2,1)S(1)}, bf16[528,256]{1,0:T(8,128)(2,1)S(1)}, u32[]{:S(2)}, u32[]{:S(2)}) %collective-permute-start.2) | collective-permute-done | bytes 270368 | tf_op jit(solution)/shard_map/ppermute | solution.py:297
  90.2 2.7 %collective-permute-start.6 = (bf16[528,256]{1,0:T(8,128)(2,1)S(1)}, bf16[528,256]{1,0:T(8,128)(2,1)S(1)}, u32[]{:S(2)}, u32[]{:S(2)}) collective-permute-start(bf16[528,256]{1,0:T(8,128)(2,1)S(1)} %reduce_sum.58.refs_8_), channel_id=1, source_target_pairs={{0,4},{1,5},{2,6},{3,7},{4,0},{5,1},{6,2},{7,3},{8,12},{9,13},{10,... | collective-permute-start | bytes 811016 | tf_op jit(solution)/shard_map/ppermute | solution.py:297
  93.0 10.1 %pool.5.refs_0_ = bf16[4096,128]{1,0:T(8,128)(2,1)S(1)} custom-call(s32[32768]{0:T(1024)S(1)} %get-tuple-element.73.ids_ref, bf16[2,16384,128]{2,1,0:T(8,128)(2,1)} %table_ref.3), custom_call_target="tpu_custom_call" | custom-call | flops 1048576 | bytes 800000 | tf_op jit(solution)/shard_map/pool/pallas_call | solution.py:56
  105.0 4.9 %all-to-all-start.2 = ((bf16[8,512,128]{2,1,0:T(8,128)(2,1)}), bf16[8,512,128]{2,1,0:T(8,128)(2,1)}, u32[]{:S(2)}, u32[]{:S(2)}) async-start(bf16[8,512,128]{2,1,0:T(8,128)(2,1)} %bitcast.21), calls=%async_computation.2 | async-start | bytes 2097152 | tf_op jit(solution)/shard_map/all_to_all | solution.py:390
  113.9 17.2 %pool.6.refs_0_ = bf16[4096,128]{1,0:T(8,128)(2,1)S(1)} custom-call(s32[32768]{0:T(1024)S(1)} %get-tuple-element.73.ids_ref, bf16[2,16384,128]{2,1,0:T(8,128)(2,1)} %table_ref.3, bf16[4096,128]{1,0:T(8,128)(2,1)S(1)} %pool.5.refs_0_), custom_call_target="tpu_custom_call", output_to_operand_aliasing={{}: (2, {})} | custom-call | flops 2097152 | bytes 1600000 | tf_op jit(solution)/shard_map/pool/pallas_call | solution.py:56
  131.2 5.2 %collective-permute-done.9.refs_10_ = bf16[528,256]{1,0:T(8,128)(2,1)S(1)} collective-permute-done((bf16[528,256]{1,0:T(8,128)(2,1)S(1)}, bf16[528,256]{1,0:T(8,128)(2,1)S(1)}, u32[]{:S(2)}, u32[]{:S(2)}) %collective-permute-start.9) | collective-permute-done | bytes 270368 | tf_op jit(solution)/shard_map/ppermute | solution.py:297
  136.4 3.6 %collective-permute-done.10.refs_14_ = bf16[528,256]{1,0:T(8,128)(2,1)} collective-permute-done((bf16[528,256]{1,0:T(8,128)(2,1)S(1)}, bf16[528,256]{1,0:T(8,128)(2,1)}, u32[]{:S(2)}, u32[]{:S(2)}) %collective-permute-start.10) | collective-permute-done | bytes 270368 | tf_op jit(solution)/shard_map/ppermute | solution.py:297
  140.8 4.6 %all-to-all-start.3 = ((bf16[8,256,128]{2,1,0:T(8,128)(2,1)}), bf16[8,256,128]{2,1,0:T(8,128)(2,1)}, u32[]{:S(2)}, u32[]{:S(2)}) async-start(bf16[8,256,128]{2,1,0:T(8,128)(2,1)} %bitcast.22), calls=%async_computation.3 | async-start | bytes 1048576 | tf_op jit(solution)/shard_map/all_to_all | solution.py:390
  147.9 10.1 %pool.7 = bf16[4096,128]{1,0:T(8,128)(2,1)S(1)} custom-call(s32[32768]{0:T(1024)S(1)} %get-tuple-element.73.ids_ref, bf16[2,16384,128]{2,1,0:T(8,128)(2,1)} %table_ref.3, bf16[4096,128]{1,0:T(8,128)(2,1)S(1)} %pool.6.refs_0_), custom_call_target="tpu_custom_call", output_to_operand_aliasing={{}: (2, {})} | custom-call | flops 1048576 | bytes 800000 | tf_op jit(solution)/shard_map/pool/pallas_call | solution.py:56
  159.4 5.2 %collective-permute-done.13.refs_15_ = bf16[528,256]{1,0:T(8,128)(2,1)} collective-permute-done((bf16[528,256]{1,0:T(8,128)(2,1)}, bf16[528,256]{1,0:T(8,128)(2,1)}, u32[]{:S(2)}, u32[]{:S(2)}) %collective-permute-start.13) | collective-permute-done | bytes 270368 | tf_op jit(solution)/shard_map/ppermute | solution.py:297
  165.5 4.3 %all-to-all-start.4 = ((bf16[8,256,128]{2,1,0:T(8,128)(2,1)}), bf16[8,256,128]{2,1,0:T(8,128)(2,1)S(1)}, u32[]{:S(2)}, u32[]{:S(2)}) async-start(bf16[8,256,128]{2,1,0:T(8,128)(2,1)} %bitcast.54), calls=%async_computation.4 | async-start | bytes 1048576 | tf_op jit(solution)/shard_map/all_to_all | solution.py:390
  172.9 12.8 %tower.2 = (bf16[8,256,256]{2,1,0:T(8,128)(2,1)}, f32[256,1]{1,0:T(8,128)S(1)}) custom-call(s32[16]{0:T(128)S(1)} %select_reduce_fusion.table_of_ref, s32[8]{0:T(128)S(1)} %convert_reduce_fusion.1.count_ref, s32[2]{0:T(128)S(1)} %pad_add_fusion.place_ref, bf16[8,512,128]{2,1,0:T(8,128)(2,1)} %all-to-all-done.2.refs_0_, ...), custom_call_target="tpu_custom_call" | custom-call | flops 4026531840 | bytes 60000000 | tf_op jit(solution)/shard_map/tower/pallas_call | solution.py:265
  185.7 6.0 %all-to-all-start.5 = ((bf16[8,256,256]{2,1,0:T(8,128)(2,1)}), bf16[8,256,256]{2,1,0:T(8,128)(2,1)}, u32[]{:S(2)}, u32[]{:S(2)}) async-start(bf16[8,256,256]{2,1,0:T(8,128)(2,1)} %get-tuple-element.90), calls=%async_computation.5 | async-start | bytes 2097152 | tf_op jit(solution)/shard_map/all_to_all | solution.py:447
  191.8 12.0 %tower.3 = (bf16[256,256]{1,0:T(8,128)(2,1)S(1)}, bf16[256,256]{1,0:T(8,128)(2,1)S(1)}, bf16[256,256]{1,0:T(8,128)(2,1)S(1)}, bf16[256,256]{1,0:T(8,128)(2,1)S(1...) custom-call(s32[16]{0:T(128)S(1)} %select_reduce_fusion.table_of_ref, ...), custom_call_target="tpu_custom_call" | custom-call | flops 4026531840 | bytes 60000000 | tf_op jit(solution)/shard_map/tower/pallas_call | solution.py:265
  204.0 3.0 %collective-permute-start.15 = (bf16[256,256]{1,0:T(8,128)(2,1)S(1)}, bf16[256,256]{1,0:T(8,128)(2,1)S(1)}, u32[]{:S(2)}, u32[]{:S(2)}) collective-permute-start(bf16[256,256]{1,0:T(8,128)(2,1)S(1)} %get-tuple-element.96), channel_id=1, source_target_pairs={{0,4},{1,5},{2,6},{3,7},{4,0},{5,1},{6,2},{7,3},{8,12},{9,13},{10,... | collective-permute-start | bytes 393224 | tf_op jit(solution)/shard_map/ppermute | solution.py:297
  208.4 3.3 %collective-permute-start.17 = (bf16[256,256]{1,0:T(8,128)(2,1)S(1)}, bf16[256,256]{1,0:T(8,128)(2,1)S(1)}, u32[]{:S(2)}, u32[]{:S(2)}) collective-permute-start(bf16[256,256]{1,0:T(8,128)(2,1)S(1)} %get-tuple-element.98), channel_id=1, source_target_pairs={{0,6},{1,7},{2,4},{3,5},{4,2},{5,3},{6,0},{7,1},{8,14},{9,15},{10,... | collective-permute-start | bytes 393224 | tf_op jit(solution)/shard_map/ppermute | solution.py:297
  212.4 20.6 %collective-permute-done.15 = bf16[256,256]{1,0:T(8,128)(2,1)S(1)} collective-permute-done((bf16[256,256]{1,0:T(8,128)(2,1)S(1)}, bf16[256,256]{1,0:T(8,128)(2,1)S(1)}, u32[]{:S(2)}, u32[]{:S(2)}) %collective-permute-start.15) | collective-permute-done | bytes 131104 | tf_op jit(solution)/shard_map/ppermute | solution.py:297
  236.9 2.9 %concatenate.23 = bf16[8,512,2,128]{3,2,1,0:T(2,128)(2,1)} pad(bf16[8,256,2,128]{3,2,1,0:T(2,128)(2,1)S(1)} %reshape.131, bf16[]{:T(256)} %constant.17.clone.1), padding=0_0x0_256x0_0x0_0 | pad | bytes 3145730 | tf_op jit(solution)/shard_map/concatenate | solution.py:451
  241.6 4.0 %collective-permute-start.20 = (bf16[256,256]{1,0:T(8,128)(2,1)S(1)}, bf16[256,256]{1,0:T(8,128)(2,1)S(1)}, u32[]{:S(2)}, u32[]{:S(2)}) collective-permute-start(bf16[256,256]{1,0:T(8,128)(2,1)S(1)} %get-tuple-element.102), channel_id=1, source_target_pairs={{0,2},{1,3},{2,0},{3,1},{4,6},{5,7},{6,4},{7,5},{8,10},{9,11},{10,... | collective-permute-start | bytes 393224 | tf_op jit(solution)/shard_map/ppermute | solution.py:297
  (125 shorter events, 54.3 us)
Async XLA Ops:
  15.9 14.3 %collective-permute-start = (bf16[528,256]{1,0:T(8,128)(2,1)S(1)}, bf16[528,256]{1,0:T(8,128)(2,1)S(1)}, u32[]{:S(2)}, u32[]{:S(2)}) collective-permute-start(bf16[528,256]{1,0:T(8,128)(2,1)S(1)} %fusion.1), channel_id=1, source_target_pairs={{0,4},{1,5},{2,6},{3,7},{4,0},{5,1},{6,2},{7,3},{8,12},{9,13},{10,... | collective-permute-start | bytes 811016 | tf_op jit(solution)/shard_map/ppermute | solution.py:297
  30.3 55.8 %all-to-all-start.1 = ((bf16[8,528,256]{2,1,0:T(8,128)(2,1)}), bf16[8,528,256]{2,1,0:T(8,128)(2,1)}, u32[]{:S(2)}, u32[]{:S(2)}) async-start(bf16[8,528,256]{2,1,0:T(8,128)(2,1)} %held_items.1), calls=%async_computation.1 | async-start | bytes 4325376 | tf_op jit(solution)/shard_map/all_to_all | solution.py:398
  36.1 47.9 %collective-permute-start.5 = (bf16[512,1024]{1,0:T(8,128)(2,1)S(1)}, bf16[512,1024]{1,0:T(8,128)(2,1)S(1)}, u32[]{:S(2)}, u32[]{:S(2)}) collective-permute-start(bf16[512,1024]{1,0:T(8,128)(2,1)S(1)} %copy-done.12), channel_id=1, source_target_pairs={{0,8},{8,0},{16,24},{24,16},{1,9},{9,1},{17,25},{25,17},{2,10},{10... | collective-permute-start | bytes 3145736 | tf_op jit(solution)/shard_map/ppermute | solution.py:297
  36.2 48.8 %collective-permute-start.4 = (bf16[512,1024]{1,0:T(8,128)(2,1)S(1)}, bf16[512,1024]{1,0:T(8,128)(2,1)}, u32[]{:S(2)}, u32[]{:S(2)}) collective-permute-start(bf16[512,1024]{1,0:T(8,128)(2,1)S(1)} %copy-done.12), channel_id=1, source_target_pairs={{0,16},{8,24},{16,0},{24,8},{1,17},{9,25},{17,1},{25,9},{2,18},{10... | collective-permute-start | bytes 3145736 | tf_op jit(solution)/shard_map/ppermute | solution.py:297
  37.8 46.2 %collective-permute-start.3 = (bf16[1056,256]{1,0:T(8,128)(2,1)S(1)}, bf16[1056,256]{1,0:T(8,128)(2,1)S(1)}, u32[]{:S(2)}, u32[]{:S(2)}) collective-permute-start(bf16[1056,256]{1,0:T(8,128)(2,1)S(1)} %pad_maximum_fusion), channel_id=1, source_target_pairs={{0,1},{1,0},{2,3},{3,2},{4,5},{5,4},{6,7},{7,6},{8,9},{9,8},{10,11... | collective-permute-start | bytes 1622024 | tf_op jit(solution)/shard_map/ppermute | solution.py:297
  39.8 39.3 %collective-permute-start.1 = (bf16[528,256]{1,0:T(8,128)(2,1)S(1)}, bf16[528,256]{1,0:T(8,128)(2,1)S(1)}, u32[]{:S(2)}, u32[]{:S(2)}) collective-permute-start(bf16[528,256]{1,0:T(8,128)(2,1)S(1)} %fusion.1), channel_id=1, source_target_pairs={{0,2},{1,3},{2,0},{3,1},{4,6},{5,7},{6,4},{7,5},{8,10},{9,11},{10,... | collective-permute-start | bytes 811016 | tf_op jit(solution)/shard_map/ppermute | solution.py:297
  41.3 42.7 %collective-permute-start.2 = (bf16[528,256]{1,0:T(8,128)(2,1)S(1)}, bf16[528,256]{1,0:T(8,128)(2,1)S(1)}, u32[]{:S(2)}, u32[]{:S(2)}) collective-permute-start(bf16[528,256]{1,0:T(8,128)(2,1)S(1)} %collective-permute-done), channel_id=1, source_target_pairs={{0,2},{1,3},{2,0},{3,1},{4,6},{5,7},{6,4},{7,5},{8,10},{9,11},{10,... | collective-permute-start | bytes 811016 | tf_op jit(solution)/shard_map/ppermute | solution.py:297
  86.1 18.9 %collective-permute-start.8 = (bf16[1056,256]{1,0:T(8,128)(2,1)S(1)}, bf16[1056,256]{1,0:T(8,128)(2,1)}, u32[]{:S(2)}, u32[]{:S(2)}) collective-permute-start(bf16[1056,256]{1,0:T(8,128)(2,1)S(1)} %pad_maximum_fusion.1), channel_id=1, source_target_pairs={{0,1},{1,0},{2,3},{3,2},{4,5},{5,4},{6,7},{7,6},{8,9},{9,8},{10,11... | collective-permute-start | bytes 1622024 | tf_op jit(solution)/shard_map/ppermute | solution.py:297
  89.6 15.4 %collective-permute-start.7 = (bf16[528,256]{1,0:T(8,128)(2,1)S(1)}, bf16[528,256]{1,0:T(8,128)(2,1)S(1)}, u32[]{:S(2)}, u32[]{:S(2)}) collective-permute-start(bf16[528,256]{1,0:T(8,128)(2,1)S(1)} %reduce_sum.58.refs_8_), channel_id=1, source_target_pairs={{0,1},{1,0},{2,3},{3,2},{4,5},{5,4},{6,7},{7,6},{8,9},{9,8},{10,11... | collective-permute-start | bytes 811016 | tf_op jit(solution)/shard_map/ppermute | solution.py:297
  90.2 14.8 %collective-permute-start.6 = (bf16[528,256]{1,0:T(8,128)(2,1)S(1)}, bf16[528,256]{1,0:T(8,128)(2,1)S(1)}, u32[]{:S(2)}, u32[]{:S(2)}) collective-permute-start(bf16[528,256]{1,0:T(8,128)(2,1)S(1)} %reduce_sum.58.refs_8_), channel_id=1, source_target_pairs={{0,4},{1,5},{2,6},{3,7},{4,0},{5,1},{6,2},{7,3},{8,12},{9,13},{10,... | collective-permute-start | bytes 811016 | tf_op jit(solution)/shard_map/ppermute | solution.py:297
  105.0 35.0 %all-to-all-start.2 = ((bf16[8,512,128]{2,1,0:T(8,128)(2,1)}), bf16[8,512,128]{2,1,0:T(8,128)(2,1)}, u32[]{:S(2)}, u32[]{:S(2)}) async-start(bf16[8,512,128]{2,1,0:T(8,128)(2,1)} %bitcast.21), calls=%async_computation.2 | async-start | bytes 2097152 | tf_op jit(solution)/shard_map/all_to_all | solution.py:390
  109.9 26.5 %collective-permute-start.9 = (bf16[528,256]{1,0:T(8,128)(2,1)S(1)}, bf16[528,256]{1,0:T(8,128)(2,1)S(1)}, u32[]{:S(2)}, u32[]{:S(2)}) collective-permute-start(bf16[528,256]{1,0:T(8,128)(2,1)S(1)} %reduce_sum.58.refs_8_), channel_id=1, source_target_pairs={{0,2},{1,3},{2,0},{3,1},{4,6},{5,7},{6,4},{7,5},{8,10},{9,11},{10,... | collective-permute-start | bytes 811016 | tf_op jit(solution)/shard_map/ppermute | solution.py:297
  111.9 24.5 %collective-permute-start.11 = (bf16[528,256]{1,0:T(8,128)(2,1)S(1)}, bf16[528,256]{1,0:T(8,128)(2,1)S(1)}, u32[]{:S(2)}, u32[]{:S(2)}) collective-permute-start(bf16[528,256]{1,0:T(8,128)(2,1)S(1)} %collective-permute-done.6.refs_12_), channel_id=1, source_target_pairs={{0,1},{1,0},{2,3},{3,2},{4,5},{5,4},{6,7},{7,6},{8,9},{9,8},{10,11... | collective-permute-start | bytes 811016 | tf_op jit(solution)/shard_map/ppermute | solution.py:297
  113.4 26.6 %collective-permute-start.10 = (bf16[528,256]{1,0:T(8,128)(2,1)S(1)}, bf16[528,256]{1,0:T(8,128)(2,1)}, u32[]{:S(2)}, u32[]{:S(2)}) collective-permute-start(bf16[528,256]{1,0:T(8,128)(2,1)S(1)} %collective-permute-done.6.refs_12_), channel_id=1, source_target_pairs={{0,2},{1,3},{2,0},{3,1},{4,6},{5,7},{6,4},{7,5},{8,10},{9,11},{10,... | collective-permute-start | bytes 811016 | tf_op jit(solution)/shard_map/ppermute | solution.py:297
  140.8 23.8 %all-to-all-start.3 = ((bf16[8,256,128]{2,1,0:T(8,128)(2,1)}), bf16[8,256,128]{2,1,0:T(8,128)(2,1)}, u32[]{:S(2)}, u32[]{:S(2)}) async-start(bf16[8,256,128]{2,1,0:T(8,128)(2,1)} %bitcast.22), calls=%async_computation.3 | async-start | bytes 1048576 | tf_op jit(solution)/shard_map/all_to_all | solution.py:390
  145.4 26.5 %collective-permute-start.14 = (bf16[512,1024]{1,0:T(8,128)(2,1)}, bf16[512,1024]{1,0:T(8,128)(2,1)}, u32[]{:S(2)}, u32[]{:S(2)}) collective-permute-start(bf16[512,1024]{1,0:T(8,128)(2,1)} %collective-permute-done.4.refs_4_), channel_id=1, source_target_pairs={{0,8},{8,0},{16,24},{24,16},{1,9},{9,1},{17,25},{25,17},{2,10},{10... | collective-permute-start | bytes 3145736 | tf_op jit(solution)/shard_map/ppermute | solution.py:297
  145.5 14.0 %collective-permute-start.12 = (bf16[528,256]{1,0:T(8,128)(2,1)S(1)}, bf16[528,256]{1,0:T(8,128)(2,1)S(1)}, u32[]{:S(2)}, u32[]{:S(2)}) collective-permute-start(bf16[528,256]{1,0:T(8,128)(2,1)S(1)} %collective-permute-done.9.refs_10_), channel_id=1, source_target_pairs={{0,1},{1,0},{2,3},{3,2},{4,5},{5,4},{6,7},{7,6},{8,9},{9,8},{10,11... | collective-permute-start | bytes 811016 | tf_op jit(solution)/shard_map/ppermute | solution.py:297
  147.5 17.1 %collective-permute-start.13 = (bf16[528,256]{1,0:T(8,128)(2,1)}, bf16[528,256]{1,0:T(8,128)(2,1)}, u32[]{:S(2)}, u32[]{:S(2)}) collective-permute-start(bf16[528,256]{1,0:T(8,128)(2,1)} %collective-permute-done.10.refs_14_), channel_id=1, source_target_pairs={{0,1},{1,0},{2,3},{3,2},{4,5},{5,4},{6,7},{7,6},{8,9},{9,8},{10,11... | collective-permute-start | bytes 811016 | tf_op jit(solution)/shard_map/ppermute | solution.py:297
  165.5 20.2 %all-to-all-start.4 = ((bf16[8,256,128]{2,1,0:T(8,128)(2,1)}), bf16[8,256,128]{2,1,0:T(8,128)(2,1)S(1)}, u32[]{:S(2)}, u32[]{:S(2)}) async-start(bf16[8,256,128]{2,1,0:T(8,128)(2,1)} %bitcast.54), calls=%async_computation.4 | async-start | bytes 1048576 | tf_op jit(solution)/shard_map/all_to_all | solution.py:390
  185.7 49.8 %all-to-all-start.5 = ((bf16[8,256,256]{2,1,0:T(8,128)(2,1)}), bf16[8,256,256]{2,1,0:T(8,128)(2,1)}, u32[]{:S(2)}, u32[]{:S(2)}) async-start(bf16[8,256,256]{2,1,0:T(8,128)(2,1)} %get-tuple-element.90), calls=%async_computation.5 | async-start | bytes 2097152 | tf_op jit(solution)/shard_map/all_to_all | solution.py:447
  204.0 28.9 %collective-permute-start.15 = (bf16[256,256]{1,0:T(8,128)(2,1)S(1)}, bf16[256,256]{1,0:T(8,128)(2,1)S(1)}, u32[]{:S(2)}, u32[]{:S(2)}) collective-permute-start(bf16[256,256]{1,0:T(8,128)(2,1)S(1)} %get-tuple-element.96), channel_id=1, source_target_pairs={{0,4},{1,5},{2,6},{3,7},{4,0},{5,1},{6,2},{7,3},{8,12},{9,13},{10,... | collective-permute-start | bytes 393224 | tf_op jit(solution)/shard_map/ppermute | solution.py:297
  207.0 28.4 %collective-permute-start.16 = (bf16[256,256]{1,0:T(8,128)(2,1)S(1)}, bf16[256,256]{1,0:T(8,128)(2,1)S(1)}, u32[]{:S(2)}, u32[]{:S(2)}) collective-permute-start(bf16[256,256]{1,0:T(8,128)(2,1)S(1)} %get-tuple-element.97), channel_id=1, source_target_pairs={{0,5},{1,4},{2,7},{3,6},{4,1},{5,0},{6,3},{7,2},{8,13},{9,12},{10,... | collective-permute-start | bytes 393224 | tf_op jit(solution)/shard_map/ppermute | solution.py:297
  208.4 27.0 %collective-permute-start.17 = (bf16[256,256]{1,0:T(8,128)(2,1)S(1)}, bf16[256,256]{1,0:T(8,128)(2,1)S(1)}, u32[]{:S(2)}, u32[]{:S(2)}) collective-permute-start(bf16[256,256]{1,0:T(8,128)(2,1)S(1)} %get-tuple-element.98), channel_id=1, source_target_pairs={{0,6},{1,7},{2,4},{3,5},{4,2},{5,3},{6,0},{7,1},{8,14},{9,15},{10,... | collective-permute-start | bytes 393224 | tf_op jit(solution)/shard_map/ppermute | solution.py:297
  211.7 23.7 %collective-permute-start.18 = (bf16[256,256]{1,0:T(8,128)(2,1)S(1)}, bf16[256,256]{1,0:T(8,128)(2,1)S(1)}, u32[]{:S(2)}, u32[]{:S(2)}) collective-permute-start(bf16[256,256]{1,0:T(8,128)(2,1)S(1)} %get-tuple-element.99), channel_id=1, source_target_pairs={{0,7},{1,6},{2,5},{3,4},{4,3},{5,2},{6,1},{7,0},{8,15},{9,14},{10,... | collective-permute-start | bytes 393224 | tf_op jit(solution)/shard_map/ppermute | solution.py:297
  (21 other events, 290.1 us)
